TPU v7x, 256 devices: a whole 4x4x8 slice. The times are simulated.
256 devices in a mesh: grp: 32 (over z_lo, x, core), dp: 8 (over z_hi, y).
Axes of the slice: x: 4, y: 4, z: 8 (z_hi: 2, z_lo: 4; z = z_hi * 4 + z_lo), core: 2. Of those that a mesh axis runs over, the one named last changes fastest.
Arguments:
- projection_rows: bfloat16 [8, 4096, 6144], P('dp', 'grp'), may hold values from -7 to 7
- normed_input_rows: bfloat16 [8, 4096, 4096], P('dp', 'grp'), may hold values from -6 to 6
- adapter_down: bfloat16 [4096, 16], replicated, may hold values from -0.09375 to 0.09375
- adapter_up: bfloat16 [16, 4096], replicated, may hold values from -1.5 to 1.5
- lengths: int32 [8, 5], P('dp'), may hold values from 128 to 2048, as said below
- groups: int32 [8, 5], P('dp'), may hold values from 2 to 16, as said below
- output_gradient: bfloat16 [8, 4096, 4096], P('dp', 'grp'), may hold values from -6 to 6
Outputs:
- attn_out: bfloat16 [8, 4096, 4096], P('dp', 'grp')
- grad_qkv: bfloat16 [8, 4096, 6144], P('dp', 'grp')
- grad_lora_a: float32 [4096, 16], replicated
- grad_lora_b: float32 [16, 4096], replicated
Inputs may be any that keep to these rules, and one draw needn't show every extreme that they name: `groups`: each replica's 5 group widths are powers of two that add up to 32; each group starts at a multiple of its own width, and exactly one group of each replica has 16 devices. `lengths`: sequence j has at most 128 * groups[j] rows and at least half as many; the sequence in a replica's widest group has exactly 2048 rows.
All inputs are finite; a program needn't handle non-finite values.
Results may differ from a plain program's by a relative error of at most 0.012.
The roundings to bfloat16 on the way count: a program that leaves them out, or rounds other values in their place, can miss the bound.
Values may be sent and summed in bfloat16 or wider, within the bound.
No kernel may reach another device: no remote copies, remote signals or barrier semaphores. Data moves between devices by JAX's collectives and lax.ppermute only.
A program may use at most 192 MiB of HBM per device.

v0:
```python
import math

import jax
import jax.numpy as jnp
from jax import lax
from jax.sharding import PartitionSpec as P

HEAD_DIM = 128


rope_base = 500000.0


def from_partner(value, axis, apart):
    return lax.ppermute(value, axis, [(i, i ^ 1 << apart) for i in range(lax.axis_size(axis))])


def rope_tables(offsets, half_dim):
    index_float = jnp.arange(half_dim, dtype=jnp.float32)
    inverse = jnp.power(jnp.float32(rope_base), -index_float / half_dim)
    angles = offsets.astype(jnp.float32)[:, None] * inverse[None, :]
    return (jnp.cos(angles), jnp.sin(angles))


def rotate(table, cosine, sine, direction):
    count, width = table.shape
    half_dim = cosine.shape[1]
    split_view = table.reshape(count, width // (2 * half_dim), 2, half_dim)
    first_half = split_view[:, :, 0]
    second_half = split_view[:, :, 1]
    cos_view = cosine[:, None, :]
    sin_view = direction * sine[:, None, :]
    rotated = jnp.stack(
        [
            first_half * cos_view - second_half * sin_view,
            second_half * cos_view + first_half * sin_view,
        ],
        axis=2,
    )
    return rotated.reshape(count, width)


def split_pair(table, section_bit, own_bit):
    row_count, slot_count, width = table.shape
    paired = table.reshape(row_count, slot_count >> section_bit + 1, 2, 1 << section_bit, width)
    lower_half = paired[:, :, 0]
    upper_half = paired[:, :, 1]
    held_half = jnp.where(own_bit == 1, upper_half, lower_half)
    sent_half = jnp.where(own_bit == 1, lower_half, upper_half)
    return (held_half, sent_half)


def join_pair(held_half, came_half, own_bit):
    row_count, high_count, low_count, width = held_half.shape
    lower_half = jnp.where(own_bit == 0, held_half, came_half)
    upper_half = jnp.where(own_bit == 1, held_half, came_half)
    return jnp.stack([lower_half, upper_half], axis=2).reshape(
        row_count, high_count * 2 * low_count, width
    )


def local(
    projection_rows, normed_input_rows, adapter_down, adapter_up, lengths, groups, output_gradient
):
    qkv_local = projection_rows[0]
    x_local = normed_input_rows[0]
    grad_raw = output_gradient[0]
    length_row = lengths[0]
    width_row = groups[0]
    token_count = qkv_local.shape[0]
    group_count = lax.axis_size("grp")
    group_index = lax.axis_index("grp")
    most_blocks = group_count // 2
    section_count = most_blocks.bit_length() - 1
    query_column_count = adapter_up.shape[1]
    kv_width = (qkv_local.shape[1] - query_column_count) // 2
    head_total = query_column_count // HEAD_DIM
    kv_total = kv_width // HEAD_DIM
    share = head_total // kv_total
    factor = 1.0 / math.sqrt(HEAD_DIM)
    packed_qkv, packed_inputs = (
        lax.all_to_all(qkv_local, "dp", split_axis=0, concat_axis=0, tiled=True),
        lax.all_to_all(x_local, "dp", split_axis=0, concat_axis=0, tiled=True),
    )
    reduced_input = jnp.dot(packed_inputs, adapter_down, preferred_element_type=jnp.float32).astype(
        jnp.bfloat16
    )
    seq_index = jnp.arange(width_row.shape[0], dtype=jnp.int32)
    ends_dev = jnp.cumsum(width_row)
    my_sequence = jnp.sum((group_index >= ends_dev).astype(jnp.int32))
    picked = seq_index == my_sequence
    width_me = jnp.sum(jnp.where(picked, width_row, 0))
    start_me = jnp.sum(jnp.where(picked, ends_dev - width_row, 0))
    length_me = jnp.sum(jnp.where(picked, length_row, 0))
    depth = jnp.sum((2 ** jnp.arange(6, dtype=jnp.int32) < width_me).astype(jnp.int32))
    row_at = jnp.arange(token_count, dtype=jnp.int32)
    local_offsets = (group_index - start_me) * token_count + row_at
    row_valid = local_offsets < length_me
    grad_local = jnp.where(row_valid[:, None], grad_raw, jnp.zeros_like(grad_raw))
    cosine, sine = rope_tables(local_offsets, HEAD_DIM // 2)
    frozen_query = packed_qkv[:, :query_column_count].astype(jnp.float32) + jnp.dot(
        reduced_input, adapter_up, preferred_element_type=jnp.float32
    )
    queries = rotate(frozen_query, cosine, sine, 1.0).astype(jnp.bfloat16)
    key_rows = rotate(
        packed_qkv[:, query_column_count : query_column_count + kv_width].astype(jnp.float32),
        cosine,
        sine,
        1.0,
    ).astype(jnp.bfloat16)
    value_rows = packed_qkv[:, query_column_count + kv_width :]
    key_wide = jnp.repeat(key_rows.reshape(token_count, kv_total, HEAD_DIM), share, axis=1)
    value_wide = jnp.repeat(value_rows.reshape(token_count, kv_total, HEAD_DIM), share, axis=1)
    buffers = [
        queries.reshape(token_count, head_total, HEAD_DIM),
        key_wide,
        value_wide,
        grad_local.reshape(token_count, head_total, HEAD_DIM),
    ]
    forward_bits = list(range(section_count))
    for section_bit in forward_bits:
        own_bit = group_index >> section_bit & 1
        pieces = [split_pair(table, section_bit, own_bit) for table in buffers]
        arrived = from_partner(
            (pieces[0][1], pieces[1][1], pieces[2][1], pieces[3][1]), "grp", section_bit
        )
        active = section_bit < depth
        buffers = [
            jnp.where(active, join_pair(pieces[slot][0], arrived[slot], own_bit), buffers[slot])
            for slot in range(4)
        ]
    query_slots, key_slots, value_slots, grad_slots = buffers
    slot_at = jnp.arange(head_total, dtype=jnp.int32)
    run_pos = slot_at % width_me
    causal_rows = row_at[None, :] <= row_at[:, None]
    same_rows = row_at[None, :] == row_at[:, None]

    def score_block(shift_by, key_shift):
        raw_scores = (
            jnp.einsum("ish,jsh->sij", query_slots, key_shift, preferred_element_type=jnp.float32)
            * factor
        )
        key_run = (slot_at - shift_by) % width_me
        key_valid = key_run[:, None] * token_count + row_at[None, :] < length_me
        first_block = shift_by == 0
        causal = jnp.logical_or(jnp.logical_not(first_block), causal_rows)
        diagonal = jnp.logical_and(first_block, same_rows)
        allowed = (
            (run_pos >= shift_by)[:, None, None]
            & causal[None]
            & (key_valid[:, None, :] | diagonal[None])
        )
        return jnp.where(allowed, raw_scores, -jnp.inf)

    top_init = jnp.full((head_total, token_count), -jnp.inf, jnp.float32)
    total_init = jnp.zeros((head_total, token_count), jnp.float32)
    store_init = jnp.full(
        (most_blocks, head_total, token_count, token_count), -jnp.inf, jnp.float32
    )

    def first_pass(shift_by, carry):
        running_top, running_total, score_store = carry
        scores = score_block(shift_by, jnp.roll(key_slots, shift_by, axis=1))
        score_store = lax.dynamic_update_index_in_dim(score_store, scores, shift_by, 0)
        next_top = jnp.maximum(running_top, jnp.max(scores, axis=2))
        next_total = running_total * jnp.exp(running_top - next_top) + jnp.sum(
            jnp.exp(scores - next_top[:, :, None]), axis=2
        )
        return (next_top, next_total, score_store)

    row_top, row_total, score_store = lax.fori_loop(
        0, width_me, first_pass, (top_init, total_init, store_init)
    )

    def second_pass(shift_by, carry):
        out_sum, prob_store = carry
        scores = lax.dynamic_index_in_dim(prob_store, shift_by, 0, keepdims=False)
        probs = jnp.exp(scores - row_top[:, :, None]) / row_total[:, :, None]
        prob_store = lax.dynamic_update_index_in_dim(prob_store, probs, shift_by, 0)
        probs_half = probs.astype(jnp.bfloat16)
        value_shift = jnp.roll(value_slots, shift_by, axis=1)
        return (
            out_sum
            + jnp.einsum(
                "sij,jsh->ish", probs_half, value_shift, preferred_element_type=jnp.float32
            ),
            prob_store,
        )

    out_float, prob_store = lax.fori_loop(
        0, width_me, second_pass, (jnp.zeros(query_slots.shape, jnp.float32), score_store)
    )
    out_slots = out_float.astype(jnp.bfloat16)
    delta_rows = jnp.sum(grad_slots.astype(jnp.float32) * out_slots.astype(jnp.float32), axis=2).T

    def third_pass(shift_by, carry):
        query_sum, key_sum, value_sum = carry
        key_shift = jnp.roll(key_slots, shift_by, axis=1)
        value_shift = jnp.roll(value_slots, shift_by, axis=1)
        probs = lax.dynamic_index_in_dim(prob_store, shift_by, 0, keepdims=False)
        probs_half = probs.astype(jnp.bfloat16)
        grad_probs = jnp.einsum(
            "ish,jsh->sij", grad_slots, value_shift, preferred_element_type=jnp.float32
        )
        grad_scores = (probs * (grad_probs - delta_rows[:, :, None])).astype(jnp.bfloat16)
        query_sum = query_sum + jnp.einsum(
            "sij,jsh->ish", grad_scores, key_shift, preferred_element_type=jnp.float32
        )
        key_part = jnp.einsum(
            "sij,ish->jsh", grad_scores, query_slots, preferred_element_type=jnp.float32
        )
        value_part = jnp.einsum(
            "sij,ish->jsh", probs_half, grad_slots, preferred_element_type=jnp.float32
        )
        key_sum = key_sum + jnp.roll(key_part, -shift_by, axis=1)
        value_sum = value_sum + jnp.roll(value_part, -shift_by, axis=1)
        return (query_sum, key_sum, value_sum)

    empty = jnp.zeros(query_slots.shape, jnp.float32)
    query_sum, key_sum, value_sum = lax.fori_loop(0, width_me, third_pass, (empty, empty, empty))
    results = [
        out_slots,
        (query_sum * factor).astype(jnp.bfloat16),
        (key_sum * factor).astype(jnp.bfloat16),
        value_sum.astype(jnp.bfloat16),
    ]
    for section_bit in forward_bits[::-1]:
        own_bit = group_index >> section_bit & 1
        pieces = [split_pair(table, section_bit, own_bit) for table in results]
        arrived = from_partner(
            (pieces[0][1], pieces[1][1], pieces[2][1], pieces[3][1]), "grp", section_bit
        )
        active = section_bit < depth
        results = [
            jnp.where(active, join_pair(pieces[slot][0], arrived[slot], own_bit), results[slot])
            for slot in range(4)
        ]
    attn_rows = results[0].reshape(token_count, query_column_count)

    def group_sum(table):
        return (
            table.astype(jnp.float32)
            .reshape(token_count, kv_total, share, HEAD_DIM)
            .sum(axis=2)
            .reshape(token_count, kv_width)
        )

    query_gradient = rotate(
        results[1].reshape(token_count, query_column_count).astype(jnp.float32), cosine, sine, -1.0
    ).astype(jnp.bfloat16)
    grad_key = rotate(group_sum(results[2]), cosine, sine, -1.0).astype(jnp.bfloat16)
    grad_value = group_sum(results[3]).astype(jnp.bfloat16)
    grad_rows = jnp.concatenate([query_gradient, grad_key, grad_value], axis=1)
    term_b = jnp.dot(reduced_input.T, query_gradient, preferred_element_type=jnp.float32)
    reduced_gradient = jnp.dot(
        query_gradient, adapter_up.T, preferred_element_type=jnp.float32
    ).astype(jnp.bfloat16)
    term_a = jnp.dot(packed_inputs.T, reduced_gradient, preferred_element_type=jnp.float32)
    grad_a, grad_b = lax.psum((term_a, term_b), ("grp", "dp"))
    return (attn_rows[None], grad_rows[None], grad_a, grad_b)


def solution(mesh):
    placed = (
        P("dp", "grp", None),
        P("dp", "grp", None),
        P(),
        P(),
        P("dp", None),
        P("dp", None),
        P("dp", "grp", None),
    )
    return jax.shard_map(
        local,
        mesh=mesh,
        in_specs=placed,
        out_specs=(P("dp", "grp", None), P("dp", "grp", None), P(), P()),
        check_vma=False,
    )
```

profile of v0, /device:TPU:1, one launch (start us, length us, event | category | flops | bytes accessed | tf_op | source)
XLA Modules:
  0.0 1288.0 jit_solution(6643555819673887801)
XLA Ops:
  14.5 3.3 collective-permute-start.16
  17.9 9.1 all-to-all-start.1
  36.7 10.0 collective-permute-done.17
  47.9 8.7 all-to-all-start
  64.9 6.9 collective-permute-done.18
  74.8 5.9 collective-permute-start.19
  86.8 20.4 %collective-permute-done.19 = bf16[128,2,8,128]{3,0,2,1:T(8,128)(2,1)S(1)} collective-permute-done((bf16[128,2,8,128]{3,0,2,1:T(8,128)(2,1)S(1)}, bf16[128,2,8,128]{3,0,2,1:T(8,128)(2,1)S(1)}, u32[]{:S(2)}, u32[]{:S(2)}) %collective-permute-start.19) | collective-permute-done | bytes 524320 | tf_op jit(solution)/shard_map/ppermute | solution.py:15
  139.5 7.0 collective-permute-done.1
  150.9 6.8 collective-permute-done.5
  162.4 6.6 collective-permute-done.9
  172.4 10.1 collective-permute-done.2
  186.2 7.5 collective-permute-done.6
  198.6 6.4 collective-permute-done.10
  210.4 3.9 bitcast_select_fusion.7
  225.1 3.7 bitcast_select_fusion.5
  239.1 11.3 broadcast_in_dim.110.clone
  250.4 20.8 %while.46 = (s32[]{:T(128)}, f32[32,128]{1,0:T(8,128)S(1)}, f32[32,128]{1,0:T(8,128)S(1)}, f32[16,32,128,128]{3,2,1,0:T(8,128)}, s32[]{:T(128)}, /*index=5*/s32[...) while((s32[]{:T(128)}, f32[32,128]{1,0:T(8,128)S(1)}, ...), condition=%wide.region_9.11_spmd.clone.clone, body=%wide.region_6.10_spmd.clone.clone.sunk | while | flops 139018800 | bytes 14967484 | solution.py:171
  252.1 3.0 fusion.178
  257.4 3.1 constant_dynamic-update-slice_fusion.2
  262.1 3.0 fusion.178
  267.4 3.1 constant_dynamic-update-slice_fusion.2
  271.4 17.4 %while.44 = (s32[]{:T(128)}, f32[128,32,128]{0,2,1:T(8,128)S(1)}, f32[16,32,128,128]{3,2,1,0:T(8,128)}, s32[]{:T(128)}, bf16[128,32,128]{0,2,1:T(8,128)(2,1)}, /...) while((s32[]{:T(128)}, f32[128,32,128]{0,2,1:T(8,128)S(1)}, ...), condition=%wide.region_11.13_spmd, body=%wide.region_10.12_spmd.sunk | while | flops 137887760 | bytes 11600197 | solution.py:190
  272.1 3.2 bitcast_add_fusion.4
  275.3 4.3 divide_dynamic-update-slice_fusion.2
  280.2 3.2 bitcast_add_fusion.4
  283.5 4.3 divide_dynamic-update-slice_fusion.2
  294.5 110.8 %collective-permute-start.12 = (bf16[128,2,8,128]{3,0,2,1:T(8,128)(2,1)}, bf16[128,2,8,128]{3,0,2,1:T(8,128)(2,1)}, u32[]{:S(2)}, u32[]{:S(2)}) collective-permute-start(bf16[128,2,8,128]{3,0,2,1:T(8,128)(2,1)} %select_bitcast_fusion.19), channel_id=1, source_target_pairs={{0,64},{8,72},{16,80},{24,88},{32,96},{40,104},{48,112},{56,120},{... | collective-permute-start | bytes 1572872 | tf_op jit(solution)/shard_map/ppermute | solution.py:15
  405.3 8.5 multiply_reduce_fusion
  420.0 41.2 %while.45 = (s32[]{:T(128)}, f32[128,32,128]{0,2,1:T(8,128)}, f32[128,32,128]{2,0,1:T(8,128)}, f32[128,32,128]{2,0,1:T(8,128)}, s32[]{:T(128)}, /*index=5*/bf16[...) while((s32[]{:T(128)}, f32[128,32,128]{0,2,1:T(8,128)}, ...), condition=%wide.region_14.17_spmd, body=%wide.region_13.16_spmd.sunk | while | flops 542113792 | bytes 88097464 | solution.py:220
  420.7 3.6 constant_dynamic-slice_fusion.2
  428.7 3.6 bitcast_add_fusion.5
  440.9 3.6 constant_dynamic-slice_fusion.2
  449.0 3.6 bitcast_add_fusion.5
  466.1 122.1 %collective-permute-start.28 = (bf16[128,2,8,128]{3,0,2,1:T(8,128)(2,1)}, bf16[128,2,8,128]{3,0,2,1:T(8,128)(2,1)}, u32[]{:S(2)}, u32[]{:S(2)}) collective-permute-start(bf16[128,2,8,128]{3,0,2,1:T(8,128)(2,1)} %select_bitcast_fusion.3), channel_id=1, source_target_pairs={{0,64},{8,72},{16,80},{24,88},{32,96},{40,104},{48,112},{56,120},{... | collective-permute-start | bytes 1572872 | tf_op jit(solution)/shard_map/ppermute | solution.py:15
  590.9 3.1 copy.766
  615.4 6.4 collective-permute-done.20
  629.9 6.4 collective-permute-done.25
  638.3 9.2 collective-permute-done.21
  649.2 7.4 collective-permute-done.14
  658.0 6.0 collective-permute-start.15
  664.0 3.8 collective-permute-done.30
  669.3 6.0 collective-permute-start.31
  675.3 3.8 collective-permute-done.26
  681.4 5.9 collective-permute-start.27
  687.3 3.0 collective-permute-done.22
  692.7 3.3 collective-permute-start.23
  699.1 3.2 reduce
  727.7 549.9 %all-reduce.3.cloned.1.call-done = (f32[4096,16]{0,1:T(8,128)}, f32[16,4096]{1,0:T(8,128)}) async-done(((f32[4096,16]{0,1:T(8,128)}, f32[16,4096]{1,0:T(8,128)}), (f32[4096,16]{0,1:T(8,128)}, f32[16,4096]{1,0:T(8,128)})) %all-reduce.3.cloned.1.call-update) | async-done | bytes 524304 | tf_op jit(solution)/shard_map/psum | solution.py:259
  (467 shorter events, 232.2 us)
Async XLA Ops:
  7.2 105.0 %copy-start = (bf16[16,4096]{1,0:T(8,128)(2,1)S(1)}, bf16[16,4096]{1,0:T(8,128)(2,1)}, u32[]{:S(2)}) copy-start(bf16[16,4096]{1,0:T(8,128)(2,1)} %param.20) | copy-start | bytes 393220
  14.5 15.6 %collective-permute-start.16 = (bf16[128,16,1,128]{3,0,1,2:T(8,128)(2,1)S(1)}, bf16[128,16,1,128]{3,0,1,2:T(8,128)(2,1)S(1)}, u32[]{:S(2)}, u32[]{:S(2)}) collective-permute-start(bf16[128,16,1,128]{3,0,1,2:T(8,128)(2,1)S(1)} %select_bitcast_fusion.15), channel_id=1, source_target_pairs={{0,8},{8,0},{16,24},{24,16},{32,40},{40,32},{48,56},{56,48},{64,72... | collective-permute-start | bytes 1572872 | tf_op jit(solution)/shard_map/ppermute | solution.py:15
  17.9 30.1 %all-to-all-start.1 = ((bf16[8,16,4096]{2,1,0:T(8,128)(2,1)}), bf16[8,16,4096]{2,1,0:T(8,128)(2,1)}, u32[]{:S(2)}, u32[]{:S(2)}) async-start(bf16[8,16,4096]{2,1,0:T(8,128)(2,1)} %bitcast.951), calls=%async_computation.1 | async-start | bytes 2097152 | tf_op jit(solution)/shard_map/all_to_all | solution.py:83
  33.2 13.5 %collective-permute-start.17 = (bf16[128,8,2,128]{3,0,1,2:T(8,128)(2,1)}, bf16[128,8,2,128]{3,0,1,2:T(8,128)(2,1)}, u32[]{:S(2)}, u32[]{:S(2)}) collective-permute-start(bf16[128,8,2,128]{3,0,1,2:T(8,128)(2,1)} %select_bitcast_fusion.14), channel_id=1, source_target_pairs={{0,16},{8,24},{16,0},{24,8},{32,48},{40,56},{48,32},{56,40},{64,80... | collective-permute-start | bytes 1572872 | tf_op jit(solution)/shard_map/ppermute | solution.py:15
  36.7 36.4 %copy-start.11 = (bf16[128,16,2,1,128]{4,0,2,1,3:T(8,128)(2,1)}, bf16[128,16,2,1,128]{4,0,2,1,3:T(8,128)(2,1)S(1)}, u32[]{:S(2)}) copy-start(bf16[128,16,2,1,128]{4,0,2,1,3:T(8,128)(2,1)S(1)} %copy.736) | copy-start | bytes 3145732
  47.9 60.3 %all-to-all-start = ((bf16[8,16,6144]{2,1,0:T(8,128)(2,1)}), bf16[8,16,6144]{2,1,0:T(8,128)(2,1)}, u32[]{:S(2)}, u32[]{:S(2)}) async-start(bf16[8,16,6144]{2,1,0:T(8,128)(2,1)} %bitcast.947), calls=%async_computation | async-start | bytes 3145728 | tf_op jit(solution)/shard_map/all_to_all | solution.py:82
  56.7 1220.9 %all-reduce.3.cloned.1.call-start = ((), (), s32[]{:S(2)}) async-start(), calls=%async_computation.2 | async-start | bytes 1048576 | tf_op jit(solution)/shard_map/psum | solution.py:259
  60.0 11.7 collective-permute-start.18
  74.7 10.4 copy-start.63
  74.8 32.4 %collective-permute-start.19 = (bf16[128,2,8,128]{3,0,2,1:T(8,128)(2,1)S(1)}, bf16[128,2,8,128]{3,0,2,1:T(8,128)(2,1)S(1)}, u32[]{:S(2)}, u32[]{:S(2)}) collective-permute-start(bf16[128,2,8,128]{3,0,2,1:T(8,128)(2,1)S(1)} %select_bitcast_fusion.12), channel_id=1, source_target_pairs={{0,64},{8,72},{16,80},{24,88},{32,96},{40,104},{48,112},{56,120},{... | collective-permute-start | bytes 1572872 | tf_op jit(solution)/shard_map/ppermute | solution.py:15
  85.1 30.6 %copy-start.60 = (f32[128,64]{0,1:T(8,128)}, f32[128,64]{0,1:T(8,128)S(1)}, u32[]{:S(2)}) copy-start(f32[128,64]{0,1:T(8,128)S(1)} %get-tuple-element.651) | copy-start | bytes 98308
  86.8 25.5 %copy-start.64 = (bf16[128,16]{0,1:T(8,128)(2,1)}, bf16[128,16]{0,1:T(8,128)(2,1)S(1)}, u32[]{:S(2)}) copy-start(bf16[128,16]{0,1:T(8,128)(2,1)S(1)} %convolution_convert_fusion.1) | copy-start | bytes 12292
  111.7 19.9 %collective-permute-start = (bf16[128,16,1,128]{3,0,1,2:T(8,128)(2,1)}, bf16[128,16,1,128]{3,0,1,2:T(8,128)(2,1)}, u32[]{:S(2)}, u32[]{:S(2)}) collective-permute-start(bf16[128,16,1,128]{3,0,1,2:T(8,128)(2,1)} %bitcast.15), channel_id=1, source_target_pairs={{0,8},{8,0},{16,24},{24,16},{32,40},{40,32},{48,56},{56,48},{64,72... | collective-permute-start | bytes 1572872 | tf_op jit(solution)/shard_map/ppermute | solution.py:15
  119.2 15.0 %collective-permute-start.4 = (bf16[128,16,1,128]{3,0,1,2:T(8,128)(2,1)}, bf16[128,16,1,128]{3,0,1,2:T(8,128)(2,1)}, u32[]{:S(2)}, u32[]{:S(2)}) collective-permute-start(bf16[128,16,1,128]{3,0,1,2:T(8,128)(2,1)} %select_bitcast_fusion.26), channel_id=1, source_target_pairs={{0,8},{8,0},{16,24},{24,16},{32,40},{40,32},{48,56},{56,48},{64,72... | collective-permute-start | bytes 1572872 | tf_op jit(solution)/shard_map/ppermute | solution.py:15
  130.1 6.4 collective-permute-start.8
  132.9 13.6 %collective-permute-start.1 = (bf16[128,8,2,128]{3,0,1,2:T(8,128)(2,1)S(1)}, bf16[128,8,2,128]{3,0,1,2:T(8,128)(2,1)S(1)}, u32[]{:S(2)}, u32[]{:S(2)}) collective-permute-start(bf16[128,8,2,128]{3,0,1,2:T(8,128)(2,1)S(1)} %fusion.45), channel_id=1, source_target_pairs={{0,16},{8,24},{16,0},{24,8},{32,48},{40,56},{48,32},{56,40},{64,80... | collective-permute-start | bytes 1572872 | tf_op jit(solution)/shard_map/ppermute | solution.py:15
  136.0 21.8 %collective-permute-start.5 = (bf16[128,8,2,128]{3,0,1,2:T(8,128)(2,1)S(1)}, bf16[128,8,2,128]{3,0,1,2:T(8,128)(2,1)S(1)}, u32[]{:S(2)}, u32[]{:S(2)}) collective-permute-start(bf16[128,8,2,128]{3,0,1,2:T(8,128)(2,1)S(1)} %select_bitcast_fusion.25), channel_id=1, source_target_pairs={{0,16},{8,24},{16,0},{24,8},{32,48},{40,56},{48,32},{56,40},{64,80... | collective-permute-start | bytes 1572872 | tf_op jit(solution)/shard_map/ppermute | solution.py:15
  138.0 31.0 %collective-permute-start.9 = (bf16[128,8,2,128]{3,0,1,2:T(8,128)(2,1)S(1)}, bf16[128,8,2,128]{3,0,1,2:T(8,128)(2,1)S(1)}, u32[]{:S(2)}, u32[]{:S(2)}) collective-permute-start(bf16[128,8,2,128]{3,0,1,2:T(8,128)(2,1)S(1)} %select_bitcast_fusion.22), channel_id=1, source_target_pairs={{0,16},{8,24},{16,0},{24,8},{32,48},{40,56},{48,32},{56,40},{64,80... | collective-permute-start | bytes 1572872 | tf_op jit(solution)/shard_map/ppermute | solution.py:15
  148.1 34.3 %collective-permute-start.2 = (bf16[128,4,4,128]{3,0,2,1:T(8,128)(2,1)S(1)}, bf16[128,4,4,128]{3,0,2,1:T(8,128)(2,1)S(1)}, u32[]{:S(2)}, u32[]{:S(2)}) collective-permute-start(bf16[128,4,4,128]{3,0,2,1:T(8,128)(2,1)S(1)} %fusion.46), channel_id=1, source_target_pairs={{0,32},{8,40},{16,48},{24,56},{32,0},{40,8},{48,16},{56,24},{64,96... | collective-permute-start | bytes 1572872 | tf_op jit(solution)/shard_map/ppermute | solution.py:15
  158.1 35.9 %copy-start.26 = (bf16[128,8,2,2,128]{4,0,3,2,1:T(8,128)(2,1)}, bf16[128,8,2,2,128]{4,0,3,2,1:T(8,128)(2,1)S(1)}, u32[]{:S(2)}) copy-start(bf16[128,8,2,2,128]{4,0,3,2,1:T(8,128)(2,1)S(1)} %copy.667) | copy-start | bytes 3145732
  159.5 34.1 %collective-permute-start.6 = (bf16[128,4,4,128]{3,0,2,1:T(8,128)(2,1)S(1)}, bf16[128,4,4,128]{3,0,2,1:T(8,128)(2,1)S(1)}, u32[]{:S(2)}, u32[]{:S(2)}) collective-permute-start(bf16[128,4,4,128]{3,0,2,1:T(8,128)(2,1)S(1)} %select_bitcast_fusion.24), channel_id=1, source_target_pairs={{0,32},{8,40},{16,48},{24,56},{32,0},{40,8},{48,16},{56,24},{64,96... | collective-permute-start | bytes 1572872 | tf_op jit(solution)/shard_map/ppermute | solution.py:15
  169.3 36.2 %copy-start.28 = (bf16[128,8,2,2,128]{4,0,3,2,1:T(8,128)(2,1)}, bf16[128,8,2,2,128]{4,0,3,2,1:T(8,128)(2,1)S(1)}, u32[]{:S(2)}) copy-start(bf16[128,8,2,2,128]{4,0,3,2,1:T(8,128)(2,1)S(1)} %copy.693) | copy-start | bytes 3145732
  169.5 35.4 %collective-permute-start.10 = (bf16[128,4,4,128]{3,0,2,1:T(8,128)(2,1)S(1)}, bf16[128,4,4,128]{3,0,2,1:T(8,128)(2,1)S(1)}, u32[]{:S(2)}, u32[]{:S(2)}) collective-permute-start(bf16[128,4,4,128]{3,0,2,1:T(8,128)(2,1)S(1)} %select_bitcast_fusion.21), channel_id=1, source_target_pairs={{0,32},{8,40},{16,48},{24,56},{32,0},{40,8},{48,16},{56,24},{64,96... | collective-permute-start | bytes 1572872 | tf_op jit(solution)/shard_map/ppermute | solution.py:15
  183.7 25.7 %collective-permute-start.3 = (bf16[128,2,8,128]{3,0,2,1:T(8,128)(2,1)S(1)}, bf16[128,2,8,128]{3,0,2,1:T(8,128)(2,1)S(1)}, u32[]{:S(2)}, u32[]{:S(2)}) collective-permute-start(bf16[128,2,8,128]{3,0,2,1:T(8,128)(2,1)S(1)} %fusion.47), channel_id=1, source_target_pairs={{0,64},{8,72},{16,80},{24,88},{32,96},{40,104},{48,112},{56,120},{... | collective-permute-start | bytes 1572872 | tf_op jit(solution)/shard_map/ppermute | solution.py:15
  196.4 36.6 %collective-permute-start.7 = (bf16[128,2,8,128]{3,0,2,1:T(8,128)(2,1)}, bf16[128,2,8,128]{3,0,2,1:T(8,128)(2,1)}, u32[]{:S(2)}, u32[]{:S(2)}) collective-permute-start(bf16[128,2,8,128]{3,0,2,1:T(8,128)(2,1)} %select_bitcast_fusion.23), channel_id=1, source_target_pairs={{0,64},{8,72},{16,80},{24,88},{32,96},{40,104},{48,112},{56,120},{... | collective-permute-start | bytes 1572872 | tf_op jit(solution)/shard_map/ppermute | solution.py:15
  207.3 14.6 %collective-permute-start.11 = (bf16[128,2,8,128]{3,0,2,1:T(8,128)(2,1)}, bf16[128,2,8,128]{3,0,2,1:T(8,128)(2,1)}, u32[]{:S(2)}, u32[]{:S(2)}) collective-permute-start(bf16[128,2,8,128]{3,0,2,1:T(8,128)(2,1)} %select_bitcast_fusion.20), channel_id=1, source_target_pairs={{0,64},{8,72},{16,80},{24,88},{32,96},{40,104},{48,112},{56,120},{... | collective-permute-start | bytes 1572872 | tf_op jit(solution)/shard_map/ppermute | solution.py:15
  292.4 121.5 %copy-start.13 = (bf16[128,32,128]{2,1,0:T(8,128)(2,1)}, bf16[128,32,128]{2,1,0:T(8,128)(2,1)S(1)}, u32[]{:S(2)}) copy-start(bf16[128,32,128]{2,1,0:T(8,128)(2,1)S(1)} %copy.710) | copy-start | bytes 3145732
  292.4 112.9 %copy-start.12 = (bf16[128,16,2,1,128]{4,0,2,1,3:T(8,128)(2,1)S(1)}, bf16[128,16,2,1,128]{4,0,2,1,3:T(8,128)(2,1)}, u32[]{:S(2)}) copy-start(bf16[128,16,2,1,128]{4,0,2,1,3:T(8,128)(2,1)} %copy-done.11) | copy-start | bytes 3145732
  292.4 112.9 %copy-start.18 = (bf16[128,8,2,2,128]{4,0,3,2,1:T(8,128)(2,1)S(1)}, bf16[128,8,2,2,128]{4,0,3,2,1:T(8,128)(2,1)}, u32[]{:S(2)}) copy-start(bf16[128,8,2,2,128]{4,0,3,2,1:T(8,128)(2,1)} %copy-done.17) | copy-start | bytes 3145732
  292.4 112.9 %copy-start.20 = (bf16[128,4,2,4,128]{4,0,3,2,1:T(8,128)(2,1)S(1)}, bf16[128,4,2,4,128]{4,0,3,2,1:T(8,128)(2,1)}, u32[]{:S(2)}) copy-start(bf16[128,4,2,4,128]{4,0,3,2,1:T(8,128)(2,1)} %copy-done.19) | copy-start | bytes 3145732
  294.5 303.3 %collective-permute-start.12 = (bf16[128,2,8,128]{3,0,2,1:T(8,128)(2,1)}, bf16[128,2,8,128]{3,0,2,1:T(8,128)(2,1)}, u32[]{:S(2)}, u32[]{:S(2)}) collective-permute-start(bf16[128,2,8,128]{3,0,2,1:T(8,128)(2,1)} %select_bitcast_fusion.19), channel_id=1, source_target_pairs={{0,64},{8,72},{16,80},{24,88},{32,96},{40,104},{48,112},{56,120},{... | collective-permute-start | bytes 1572872 | tf_op jit(solution)/shard_map/ppermute | solution.py:15
  464.1 124.2 %copy-start.3 = (f32[128,32,128]{2,0,1:T(8,128)S(1)}, f32[128,32,128]{2,0,1:T(8,128)}, u32[]{:S(2)}) copy-start(f32[128,32,128]{2,0,1:T(8,128)} %get-tuple-element.275) | copy-start | bytes 6291460
  466.1 135.6 %collective-permute-start.28 = (bf16[128,2,8,128]{3,0,2,1:T(8,128)(2,1)}, bf16[128,2,8,128]{3,0,2,1:T(8,128)(2,1)}, u32[]{:S(2)}, u32[]{:S(2)}) collective-permute-start(bf16[128,2,8,128]{3,0,2,1:T(8,128)(2,1)} %select_bitcast_fusion.3), channel_id=1, source_target_pairs={{0,64},{8,72},{16,80},{24,88},{32,96},{40,104},{48,112},{56,120},{... | collective-permute-start | bytes 1572872 | tf_op jit(solution)/shard_map/ppermute | solution.py:15
  590.9 19.8 %collective-permute-start.24 = (bf16[128,2,8,128]{3,0,2,1:T(8,128)(2,1)}, bf16[128,2,8,128]{3,0,2,1:T(8,128)(2,1)}, u32[]{:S(2)}, u32[]{:S(2)}) collective-permute-start(bf16[128,2,8,128]{3,0,2,1:T(8,128)(2,1)} %select_bitcast_fusion.7), channel_id=1, source_target_pairs={{0,64},{8,72},{16,80},{24,88},{32,96},{40,104},{48,112},{56,120},{... | collective-permute-start | bytes 1572872 | tf_op jit(solution)/shard_map/ppermute | solution.py:15
  596.3 25.5 %collective-permute-start.20 = (bf16[128,2,8,128]{3,0,2,1:T(8,128)(2,1)S(1)}, bf16[128,2,8,128]{3,0,2,1:T(8,128)(2,1)S(1)}, u32[]{:S(2)}, u32[]{:S(2)}) collective-permute-start(bf16[128,2,8,128]{3,0,2,1:T(8,128)(2,1)S(1)} %select_bitcast_fusion.11), channel_id=1, source_target_pairs={{0,64},{8,72},{16,80},{24,88},{32,96},{40,104},{48,112},{56,120},{... | collective-permute-start | bytes 1572872 | tf_op jit(solution)/shard_map/ppermute | solution.py:15
  601.1 24.1 %collective-permute-start.13 = (bf16[128,4,4,128]{3,0,2,1:T(8,128)(2,1)S(1)}, bf16[128,4,4,128]{3,0,2,1:T(8,128)(2,1)S(1)}, u32[]{:S(2)}, u32[]{:S(2)}) collective-permute-start(bf16[128,4,4,128]{3,0,2,1:T(8,128)(2,1)S(1)} %select_bitcast_fusion.18), channel_id=1, source_target_pairs={{0,32},{8,40},{16,48},{24,56},{32,0},{40,8},{48,16},{56,24},{64,96... | collective-permute-start | bytes 1572872 | tf_op jit(solution)/shard_map/ppermute | solution.py:15
  606.4 20.7 %collective-permute-start.29 = (bf16[128,4,4,128]{3,0,2,1:T(8,128)(2,1)S(1)}, bf16[128,4,4,128]{3,0,2,1:T(8,128)(2,1)S(1)}, u32[]{:S(2)}, u32[]{:S(2)}) collective-permute-start(bf16[128,4,4,128]{3,0,2,1:T(8,128)(2,1)S(1)} %select_bitcast_fusion.2), channel_id=1, source_target_pairs={{0,32},{8,40},{16,48},{24,56},{32,0},{40,8},{48,16},{56,24},{64,96... | collective-permute-start | bytes 1572872 | tf_op jit(solution)/shard_map/ppermute | solution.py:15
  614.7 21.6 %collective-permute-start.25 = (bf16[128,4,4,128]{3,0,2,1:T(8,128)(2,1)S(1)}, bf16[128,4,4,128]{3,0,2,1:T(8,128)(2,1)S(1)}, u32[]{:S(2)}, u32[]{:S(2)}) collective-permute-start(bf16[128,4,4,128]{3,0,2,1:T(8,128)(2,1)S(1)} %select_bitcast_fusion.6), channel_id=1, source_target_pairs={{0,32},{8,40},{16,48},{24,56},{32,0},{40,8},{48,16},{56,24},{64,96... | collective-permute-start | bytes 1572872 | tf_op jit(solution)/shard_map/ppermute | solution.py:15
  624.6 23.0 %collective-permute-start.21 = (bf16[128,4,4,128]{3,0,2,1:T(8,128)(2,1)S(1)}, bf16[128,4,4,128]{3,0,2,1:T(8,128)(2,1)S(1)}, u32[]{:S(2)}, u32[]{:S(2)}) collective-permute-start(bf16[128,4,4,128]{3,0,2,1:T(8,128)(2,1)S(1)} %select_bitcast_fusion.10), channel_id=1, source_target_pairs={{0,32},{8,40},{16,48},{24,56},{32,0},{40,8},{48,16},{56,24},{64,96... | collective-permute-start | bytes 1572872 | tf_op jit(solution)/shard_map/ppermute | solution.py:15
  626.7 29.9 %collective-permute-start.14 = (bf16[128,8,2,128]{3,0,1,2:T(8,128)(2,1)S(1)}, bf16[128,8,2,128]{3,0,1,2:T(8,128)(2,1)S(1)}, u32[]{:S(2)}, u32[]{:S(2)}) collective-permute-start(bf16[128,8,2,128]{3,0,1,2:T(8,128)(2,1)S(1)} %select_bitcast_fusion.17), channel_id=1, source_target_pairs={{0,16},{8,24},{16,0},{24,8},{32,48},{40,56},{48,32},{56,40},{64,80... | collective-permute-start | bytes 1572872 | tf_op jit(solution)/shard_map/ppermute | solution.py:15
  628.6 39.2 %collective-permute-start.30 = (bf16[128,8,2,128]{3,0,1,2:T(8,128)(2,1)S(1)}, bf16[128,8,2,128]{3,0,1,2:T(8,128)(2,1)S(1)}, u32[]{:S(2)}, u32[]{:S(2)}) collective-permute-start(bf16[128,8,2,128]{3,0,1,2:T(8,128)(2,1)S(1)} %select_bitcast_fusion.1), channel_id=1, source_target_pairs={{0,16},{8,24},{16,0},{24,8},{32,48},{40,56},{48,32},{56,40},{64,80... | collective-permute-start | bytes 1572872 | tf_op jit(solution)/shard_map/ppermute | solution.py:15
  637.8 41.2 %collective-permute-start.26 = (bf16[128,8,2,128]{3,0,1,2:T(8,128)(2,1)S(1)}, bf16[128,8,2,128]{3,0,1,2:T(8,128)(2,1)S(1)}, u32[]{:S(2)}, u32[]{:S(2)}) collective-permute-start(bf16[128,8,2,128]{3,0,1,2:T(8,128)(2,1)S(1)} %select_bitcast_fusion.5), channel_id=1, source_target_pairs={{0,16},{8,24},{16,0},{24,8},{32,48},{40,56},{48,32},{56,40},{64,80... | collective-permute-start | bytes 1572872 | tf_op jit(solution)/shard_map/ppermute | solution.py:15
  649.1 41.2 %collective-permute-start.22 = (bf16[128,8,2,128]{3,0,1,2:T(8,128)(2,1)S(1)}, bf16[128,8,2,128]{3,0,1,2:T(8,128)(2,1)S(1)}, u32[]{:S(2)}, u32[]{:S(2)}) collective-permute-start(bf16[128,8,2,128]{3,0,1,2:T(8,128)(2,1)S(1)} %select_bitcast_fusion.9), channel_id=1, source_target_pairs={{0,16},{8,24},{16,0},{24,8},{32,48},{40,56},{48,32},{56,40},{64,80... | collective-permute-start | bytes 1572872 | tf_op jit(solution)/shard_map/ppermute | solution.py:15
  658.0 37.9 %collective-permute-start.15 = (bf16[128,16,1,128]{3,0,1,2:T(8,128)(2,1)S(1)}, bf16[128,16,1,128]{3,0,1,2:T(8,128)(2,1)S(1)}, u32[]{:S(2)}, u32[]{:S(2)}) collective-permute-start(bf16[128,16,1,128]{3,0,1,2:T(8,128)(2,1)S(1)} %select_bitcast_fusion.16), channel_id=1, source_target_pairs={{0,8},{8,0},{16,24},{24,16},{32,40},{40,32},{48,56},{56,48},{64,72... | collective-permute-start | bytes 1572872 | tf_op jit(solution)/shard_map/ppermute | solution.py:15
  669.3 26.8 %collective-permute-start.31 = (bf16[128,16,1,128]{3,0,1,2:T(8,128)(2,1)S(1)}, bf16[128,16,1,128]{3,0,1,2:T(8,128)(2,1)S(1)}, u32[]{:S(2)}, u32[]{:S(2)}) collective-permute-start(bf16[128,16,1,128]{3,0,1,2:T(8,128)(2,1)S(1)} %select_bitcast_fusion), channel_id=1, source_target_pairs={{0,8},{8,0},{16,24},{24,16},{32,40},{40,32},{48,56},{56,48},{64,72... | collective-permute-start | bytes 1572872 | tf_op jit(solution)/shard_map/ppermute | solution.py:15
  680.5 9.9 copy-start.21
  681.4 34.2 %collective-permute-start.27 = (bf16[128,16,1,128]{3,0,1,2:T(8,128)(2,1)}, bf16[128,16,1,128]{3,0,1,2:T(8,128)(2,1)}, u32[]{:S(2)}, u32[]{:S(2)}) collective-permute-start(bf16[128,16,1,128]{3,0,1,2:T(8,128)(2,1)} %select_bitcast_fusion.4), channel_id=1, source_target_pairs={{0,8},{8,0},{16,24},{24,16},{32,40},{40,32},{48,56},{56,48},{64,72... | collective-permute-start | bytes 1572872 | tf_op jit(solution)/shard_map/ppermute | solution.py:15
  692.7 10.8 collective-permute-start.23
  (60 other events, 133.5 us)
Sparse Core Ops, SparseCore 0:
  721.9 555.6 all-reduce.2
where the time goes:
time: 1300 us; the launch traced here: 1290 us
  waiting for transfers between devices  676 us (52%)
  starting transfers between devices  313 us (24%)
  local copies, waits for them, and re-layouts  124 us (10%)
  other arithmetic  109 us (8%)
  matrix products  38.3 us (3%)
  between operations  20.7 us (2%)
    psum x1, waiting for transfers between devices, local(): grad_a, grad_b = lax.psum((term_a, term_b), ('grp', 'dp'))  550 us
    ppermute x32, starting transfers between devices, from_partner(): lax.ppermute(value, axis, [(i, i ^ 1 << apart) for i in range(lax.axis_si...  295 us
    ppermute x32, waiting for transfers between devices, from_partner(): lax.ppermute(value, axis, [(i, i ^ 1 << apart) for i in range(lax.axis_si...  126 us
  transfers between devices with their start and end apart: 35, of which 19 were waited for; matrix products, arithmetic and copies ran while one was open for 14% of the time, Pallas kernels for 0%

commit v1 on v0

v1 whole, which is shorter than its diff:
```python
import math

import jax
import jax.numpy as jnp
from jax import lax
from jax.experimental import pallas as pl
from jax.experimental.pallas import tpu as pltpu
from jax.sharding import Mesh
from jax.sharding import PartitionSpec as P

HEAD_DIM = 128
HALF_DIM = HEAD_DIM // 2
BLOCK = 256
PAIR = 2 * HEAD_DIM
PIECE = 2 * PAIR + 2 * HEAD_DIM
rope_base = 500000.0
VMEM_BYTES = 48 * 1024 * 1024
F32 = jnp.float32
BF16 = jnp.bfloat16


def rope_tables(offsets):
    index_float = jnp.arange(HALF_DIM, dtype=F32)
    inverse = jnp.power(F32(rope_base), -index_float / HALF_DIM)
    angles = offsets.astype(F32)[:, None] * inverse[None, :]
    cosine, sine = jnp.cos(angles), jnp.sin(angles)
    return jnp.concatenate([cosine, cosine], axis=1), jnp.concatenate([-sine, sine], axis=1)


def rotated(table, cosine, sine):
    return table * cosine + pltpu.roll(table, HALF_DIM, 1) * sine


def prepare_kernel(qkv_ref, low_ref, up_ref, cos_ref, sin_ref, grad_ref, valid_ref, out_ref):
    cosine = cos_ref[...]
    sine = sin_ref[...]
    low = low_ref[...]
    kept = valid_ref[...] > 0
    queries = up_ref.shape[1]
    kv_width = (qkv_ref.shape[1] - queries) // 2
    pieces = out_ref.shape[0]
    for piece in range(pieces):
        columns = slice(piece * PAIR, (piece + 1) * PAIR)
        full = qkv_ref[:, columns].astype(F32) + jnp.dot(
            low, up_ref[:, columns], preferred_element_type=F32
        )
        for head in range(2):
            at = slice(head * HEAD_DIM, (head + 1) * HEAD_DIM)
            out_ref[piece, :, at] = rotated(full[:, at], cosine, sine).astype(BF16)
        grad = grad_ref[:, columns]
        out_ref[piece, :, PAIR : 2 * PAIR] = jnp.where(kept, grad, jnp.zeros_like(grad))
    for key_head in range(kv_width // HEAD_DIM):
        at = queries + key_head * HEAD_DIM
        keys = rotated(qkv_ref[:, at : at + HEAD_DIM].astype(F32), cosine, sine).astype(BF16)
        values = qkv_ref[:, at + kv_width : at + kv_width + HEAD_DIM]
        for piece in (2 * key_head, 2 * key_head + 1):
            out_ref[piece, :, 2 * PAIR : 2 * PAIR + HEAD_DIM] = keys
            out_ref[piece, :, 2 * PAIR + HEAD_DIM :] = values


def attention_kernel(start_ref, end_ref, x_ref, out_ref, kt, vt, dkt, dvt, numer, probs):
    step = pl.program_id(0)
    blocks = pl.num_programs(0)
    factor = 1.0 / math.sqrt(HEAD_DIM)
    exponent = factor * math.log2(math.e)
    key_at = 2 * PAIR
    value_at = 2 * PAIR + HEAD_DIM

    @pl.when(step == 0)
    def _():
        for block in range(x_ref.shape[0] // BLOCK):
            rows = slice(block * BLOCK, (block + 1) * BLOCK)
            kt[block] = x_ref[rows, key_at:value_at].T
            vt[block] = x_ref[rows, value_at:].T
        dkt[...] = jnp.zeros_like(dkt)
        dvt[...] = jnp.zeros_like(dvt)

    first = start_ref[step]
    last_row = end_ref[step]
    own = pl.ds(pl.multiple_of(step * BLOCK, BLOCK), BLOCK)
    column = lax.broadcasted_iota(jnp.int32, (1, BLOCK), 1)
    row = lax.broadcasted_iota(jnp.int32, (BLOCK, 1), 0)
    queries = [x_ref[own, h * HEAD_DIM : (h + 1) * HEAD_DIM] for h in range(2)]
    grads = [x_ref[own, PAIR + h * HEAD_DIM : PAIR + (h + 1) * HEAD_DIM] for h in range(2)]

    def halves(op, table):
        return op(table[:, :HEAD_DIM], table[:, HEAD_DIM:])

    def key_rows(block):
        return pl.ds(pl.multiple_of(block * BLOCK, BLOCK), BLOCK)

    diagonal = (column == row) | ((column < row) & (step * BLOCK + column < last_row))
    tops = []
    for h in range(2):
        scores = jnp.dot(queries[h], kt[step], preferred_element_type=F32)
        scores = jnp.where(diagonal, scores, -jnp.inf)
        numer[h, step] = scores
        tops.append(halves(jnp.maximum, scores))

    def score_pass(block, carry):
        bias = jnp.where(block * BLOCK + column < last_row, F32(0.0), F32(-jnp.inf))
        result = []
        for h in range(2):
            scores = jnp.dot(queries[h], kt[block], preferred_element_type=F32) + bias
            numer[h, block] = scores
            result.append(jnp.maximum(carry[h], halves(jnp.maximum, scores)))
        return tuple(result)

    tops = lax.fori_loop(first, step, score_pass, tuple(tops))
    tops = [jnp.max(top, axis=1, keepdims=True) for top in tops]

    def exp_pass(block, carry):
        result = []
        for h in range(2):
            powers = jnp.exp2((numer[h, block] - tops[h]) * exponent)
            numer[h, block] = powers
            result.append(carry[h] + halves(jnp.add, powers))
        return tuple(result)

    empty = jnp.zeros((BLOCK, HEAD_DIM), F32)
    totals = lax.fori_loop(first, step + 1, exp_pass, (empty, empty))
    inverse = [1.0 / jnp.sum(total, axis=1, keepdims=True) for total in totals]

    def out_pass(block, carry):
        values = x_ref[key_rows(block), value_at:]
        result = []
        for h in range(2):
            held = numer[h, block] * inverse[h]
            numer[h, block] = held
            rounded = held.astype(BF16)
            probs[h, block] = rounded
            result.append(carry[h] + jnp.dot(rounded, values, preferred_element_type=F32))
        return tuple(result)

    outs = lax.fori_loop(first, step + 1, out_pass, (empty, empty))
    outs = [out.astype(BF16) for out in outs]
    deltas = [
        jnp.sum(grads[h].astype(F32) * outs[h].astype(F32), axis=1, keepdims=True) for h in range(2)
    ]
    queries_t = [table.T for table in queries]
    grads_t = [table.T for table in grads]

    def gradient_pass(block, carry):
        keys = x_ref[key_rows(block), key_at:value_at]
        result = []
        key_part = dkt[block]
        value_part = dvt[block]
        for h in range(2):
            grad_probs = jnp.dot(grads[h], vt[block], preferred_element_type=F32)
            grad_scores = (numer[h, block] * (grad_probs - deltas[h])).astype(BF16)
            result.append(carry[h] + jnp.dot(grad_scores, keys, preferred_element_type=F32))
            key_part += jnp.dot(queries_t[h], grad_scores, preferred_element_type=F32)
            value_part += jnp.dot(grads_t[h], probs[h, block], preferred_element_type=F32)
        dkt[block] = key_part
        dvt[block] = value_part
        return tuple(result)

    query_sums = lax.fori_loop(first, step + 1, gradient_pass, (empty, empty))
    for h in range(2):
        at = h * HEAD_DIM
        out_ref[own, at : at + HEAD_DIM] = outs[h]
        out_ref[own, PAIR + at : PAIR + at + HEAD_DIM] = (query_sums[h] * factor).astype(BF16)

    @pl.when(step == blocks - 1)
    def _():
        for block in range(x_ref.shape[0] // BLOCK):
            rows = slice(block * BLOCK, (block + 1) * BLOCK)
            out_ref[rows, key_at:value_at] = (dkt[block] * factor).T.astype(BF16)
            out_ref[rows, value_at:] = dvt[block].T.astype(BF16)


def attention(table, starts, ends):
    rows, width = table.shape
    blocks = rows // BLOCK
    tiles = blocks * (blocks + 1) // 2
    return pl.pallas_call(
        attention_kernel,
        out_shape=jax.ShapeDtypeStruct((rows, width), BF16),
        grid_spec=pltpu.PrefetchScalarGridSpec(
            num_scalar_prefetch=2,
            grid=(blocks,),
            in_specs=[pl.BlockSpec((rows, width), lambda i, *_: (0, 0))],
            out_specs=pl.BlockSpec((rows, width), lambda i, *_: (0, 0)),
            scratch_shapes=[
                pltpu.VMEM((blocks, HEAD_DIM, BLOCK), BF16),
                pltpu.VMEM((blocks, HEAD_DIM, BLOCK), BF16),
                pltpu.VMEM((blocks, HEAD_DIM, BLOCK), F32),
                pltpu.VMEM((blocks, HEAD_DIM, BLOCK), F32),
                pltpu.VMEM((2, blocks, BLOCK, BLOCK), F32),
                pltpu.VMEM((2, blocks, BLOCK, BLOCK), BF16),
            ],
        ),
        compiler_params=pltpu.CompilerParams(vmem_limit_bytes=VMEM_BYTES),
        cost_estimate=pl.CostEstimate(
            flops=tiles * 2 * 6 * 2 * BLOCK * BLOCK * HEAD_DIM,
            bytes_accessed=4 * rows * width,
            transcendentals=tiles * 2 * BLOCK * BLOCK,
        ),
    )(starts, ends, table)


def finish_kernel(came_ref, low_ref, up_ref, cos_ref, sin_ref, out_ref, grad_ref, dlow_ref, term_ref):
    cosine = cos_ref[...]
    sine = -sin_ref[...]
    low_t = low_ref[...].astype(F32).T.astype(BF16)
    queries = up_ref.shape[1]
    kv_width = (grad_ref.shape[1] - queries) // 2
    dlow = jnp.zeros(dlow_ref.shape, F32)
    for piece in range(came_ref.shape[0]):
        columns = slice(piece * PAIR, (piece + 1) * PAIR)
        out_ref[:, columns] = came_ref[piece, :, :PAIR]
        for head in range(2):
            at = PAIR + head * HEAD_DIM
            to = piece * PAIR + head * HEAD_DIM
            grad_ref[:, to : to + HEAD_DIM] = rotated(
                came_ref[piece, :, at : at + HEAD_DIM].astype(F32), cosine, sine
            ).astype(BF16)
        part = grad_ref[:, columns]
        dlow += lax.dot_general(
            part, up_ref[:, columns], (((1,), (1,)), ((), ())), preferred_element_type=F32
        )
        term_ref[:, columns] = jnp.dot(low_t, part, preferred_element_type=F32)
    dlow_ref[...] = dlow.astype(BF16)
    for key_head in range(kv_width // HEAD_DIM):
        pair = (2 * key_head, 2 * key_head + 1)
        keys, values = (
            sum(came_ref[piece, :, at : at + HEAD_DIM].astype(F32) for piece in pair)
            for at in (2 * PAIR, 2 * PAIR + HEAD_DIM)
        )
        at = queries + key_head * HEAD_DIM
        grad_ref[:, at : at + HEAD_DIM] = rotated(keys, cosine, sine).astype(BF16)
        grad_ref[:, at + kv_width : at + kv_width + HEAD_DIM] = values.astype(BF16)


def exchange(table, axis):
    return lax.all_to_all(table, axis, split_axis=0, concat_axis=0, tiled=True)


def local(
    projection_rows, normed_input_rows, adapter_down, adapter_up, lengths, groups, output_gradient
):
    qkv_local = projection_rows[0]
    x_local = normed_input_rows[0]
    grad_raw = output_gradient[0]
    length_row = lengths[0]
    width_row = groups[0]
    token_count, model_width = x_local.shape
    qkv_width = qkv_local.shape[1]
    rank, query_columns = adapter_up.shape
    members = lax.axis_size("sub")
    half_index = lax.axis_index("half")
    group_index = half_index * members + lax.axis_index("sub")
    low_local = jnp.dot(x_local, adapter_down, preferred_element_type=F32).astype(BF16)
    packed_low = exchange(low_local, "dp")
    packed_qkv = exchange(qkv_local, "dp")

    ends_dev = jnp.cumsum(width_row)
    starts_dev = ends_dev - width_row

    def owner_of(device):
        picked = (device[:, None] >= starts_dev[None, :]) & (device[:, None] < ends_dev[None, :])
        start = jnp.sum(jnp.where(picked, starts_dev[None, :], 0), axis=1)
        length = jnp.sum(jnp.where(picked, length_row[None, :], 0), axis=1)
        return start, length

    start_me, length_me = owner_of(group_index[None])
    row_at = jnp.arange(token_count, dtype=jnp.int32)
    local_offsets = (group_index - start_me) * token_count + row_at
    row_valid = (local_offsets < length_me).astype(jnp.int32)[:, None]
    cosine, sine = rope_tables(local_offsets)
    per_block = BLOCK // token_count
    block_device = half_index * members + per_block * jnp.arange(
        members // per_block, dtype=jnp.int32
    )
    block_start, block_length = owner_of(block_device)
    first_rows = (block_start - half_index * members) * token_count
    starts = first_rows // BLOCK
    ends = first_rows + block_length

    params = pltpu.CompilerParams(vmem_limit_bytes=VMEM_BYTES)
    pieces = pl.pallas_call(
        prepare_kernel,
        out_shape=jax.ShapeDtypeStruct((members, token_count, PIECE), BF16),
        compiler_params=params,
    )(packed_qkv, packed_low, adapter_up, cosine, sine, grad_raw, row_valid)
    table = exchange(pieces, "sub").reshape(members * token_count, PIECE)
    results = attention(table, starts, ends)
    came = exchange(results.reshape(members, token_count, PIECE), "sub")
    attn_rows, grad_rows, reduced_gradient, term_b = pl.pallas_call(
        finish_kernel,
        out_shape=(
            jax.ShapeDtypeStruct((token_count, query_columns), BF16),
            jax.ShapeDtypeStruct((token_count, qkv_width), BF16),
            jax.ShapeDtypeStruct((token_count, rank), BF16),
            jax.ShapeDtypeStruct((rank, query_columns), F32),
        ),
        compiler_params=params,
    )(came, packed_low, adapter_up, cosine, sine)
    gradient_local = exchange(reduced_gradient, "dp")
    term_a = lax.dot_general(
        gradient_local, x_local, (((0,), (0,)), ((), ())), preferred_element_type=F32
    )
    terms = jnp.concatenate([term_a, term_b], axis=0)
    parts = exchange(terms, ("half", "sub"))
    total = jnp.sum(parts, axis=0).reshape(-1, 128)
    replicas = lax.axis_size("dp")
    apart = 1
    while apart < replicas:
        total = total + lax.ppermute(total, "dp", [(i, i ^ apart) for i in range(replicas)])
        apart *= 2
    whole = exchange(jnp.broadcast_to(total.reshape(1, -1), terms.shape), ("half", "sub"))
    return (attn_rows[None], grad_rows[None], whole[:rank].T, whole[rank:])


def solution(mesh):
    members, replicas = mesh.devices.shape
    split = Mesh(mesh.devices.reshape(2, members // 2, replicas), ("half", "sub", "dp"))
    rows = P("dp", ("half", "sub"), None)
    placed = (rows, rows, P(), P(), P("dp", None), P("dp", None), rows)
    return jax.shard_map(
        local,
        mesh=split,
        in_specs=placed,
        out_specs=(rows, rows, P(), P()),
        check_vma=False,
    )
```

time: 1300 us -> 294 us (0.23)
  waiting for transfers between devices: 676 us -> 73.8 us
  starting transfers between devices: 313 us -> 26.1 us
  blocking collectives: 0 us -> 127 us
  local copies, waits for them, and re-layouts: 124 us -> 7.36 us
  other arithmetic: 109 us -> 2.51 us
  Pallas kernels: 0 us -> 53.7 us
  matrix products: 38.3 us -> 1.56 us
  between operations: 20.7 us -> 1.46 us
    psum x1 -> x0, waiting for transfers between devices: 550 us -> none  [local(): grad_a, grad_b = lax.psum((term_a, term_b), ('grp', 'dp'))]
    ppermute x32 -> x3, starting transfers between devices: 295 us -> 1.54 us  [local(): lax.ppermute(total, 'dp', [(i, i ^ apart) for i in range(replicas)])]
    all_to_all x0 -> x5, blocking collectives: none -> 127 us  [exchange(): return lax.all_to_all(table, axis, split_axis=0, concat_axis=0, tiled=True)]
    ppermute x32 -> x3, waiting for transfers between devices: 126 us -> 12 us  [local(): lax.ppermute(total, 'dp', [(i, i ^ apart) for i in range(replicas)])]
    all_to_all x2, waiting for transfers between devices: 0.01 us -> 61.8 us  [exchange(): return lax.all_to_all(table, axis, split_axis=0, concat_axis=0, tiled=True)]
    pallas_call x0 -> x3, Pallas kernels: none -> 53.7 us  [the longest x1 50.4 us: attention(): pl.pallas_call(attention_kernel, out_shape=jax.ShapeDtypeStruct((rows, wi...]
    select_n x65 -> x0, other arithmetic: 42.3 us -> none  [the longest x15 15.4 us: local(): jnp.where(active, join_pair(pieces[slot][0], arrived[slot], own_bit), buf...]
    dot_general x16 -> x2, matrix products: 38.3 us -> 1.56 us  [the longest x1 1.27 us: local(): jnp.dot(x_local, adapter_down, preferred_element_type=F32).astype(BF16)]
  transfers between devices with their start and end apart: 35 -> 5, of which waited for: 19 -> 5; matrix products, arithmetic and copies ran while one was open for 14% -> 1% of each run, Pallas kernels for 0% -> 0%
where the time goes in v1:
time: 294 us; the launch traced here: 293 us
  blocking collectives  127 us (43%)
  waiting for transfers between devices  73.8 us (25%)
  Pallas kernels  53.7 us (18%)
  starting transfers between devices  26.1 us (9%)
  local copies, waits for them, and re-layouts  7.36 us (3%)
    all_to_all x5, blocking collectives, exchange(): return lax.all_to_all(table, axis, split_axis=0, concat_axis=0, tiled=True)  127 us
    all_to_all x2, waiting for transfers between devices, exchange(): return lax.all_to_all(table, axis, split_axis=0, concat_axis=0, tiled=True)  61.8 us
    pallas_call x1, Pallas kernels, attention(): pl.pallas_call(attention_kernel, out_shape=jax.ShapeDtypeStruct((rows, wi...  50.4 us
    all_to_all x2, starting transfers between devices, exchange(): return lax.all_to_all(table, axis, split_axis=0, concat_axis=0, tiled=True)  24.5 us
    ppermute x3, waiting for transfers between devices, local(): lax.ppermute(total, 'dp', [(i, i ^ apart) for i in range(replicas)])  12 us
    unnamed x18, local copies, waits for them, and re-layouts  6.19 us
  transfers between devices with their start and end apart: 5, of which 5 were waited for; matrix products, arithmetic and copies ran while one was open for 1% of the time, Pallas kernels for 0%

profile of v1, /device:TPU:1, one launch (start us, length us, event | category | flops | bytes accessed | tf_op | source)
XLA Modules:
  0.0 293.3 jit_solution(5093107313261253856)
XLA Ops:
  0.6 0.0 copy-start
  0.6 0.0 copy-start.5
  0.7 0.0 copy-start.4
  0.7 0.0 copy-start.3
  0.7 1.2 copy-done
  1.9 1.3 convolution_convert_fusion
  3.1 0.1 copy.19
  3.3 0.1 reshape.107
  3.4 20.3 %all_to_all.59 = bf16[8,2,128]{2,1,0:T(2,128)(2,1)S(1)} all-to-all(bf16[8,2,128]{2,1,0:T(2,128)(2,1)S(1)} %reshape.107), channel_id=1, replica_groups=mesh['half'=2,'sub'=16,'dp'=8] {'dp'}, dimensions={0} | all-to-all | bytes 8192 | tf_op jit(solution)/shard_map/all_to_all | solution.py:236
  23.7 3.6 %all-to-all-start = ((bf16[8,16,6144]{2,1,0:T(8,128)(2,1)}), bf16[8,16,6144]{2,1,0:T(8,128)(2,1)S(1)}, u32[]{:S(2)}, u32[]{:S(2)}) async-start(bf16[8,16,6144]{2,1,0:T(8,128)(2,1)} %bitcast.58), calls=%async_computation | async-start | bytes 3145728 | tf_op jit(solution)/shard_map/all_to_all | solution.py:236
  27.3 0.0 copy-done.5
  27.3 0.2 reduce-window.4
  27.5 0.0 copy-done.4
  27.5 0.6 select_reduce_fusion.2
  28.8 0.7 fusion.3.valid_ref
  29.5 0.3 fusion.4
  29.8 0.1 pad_maximum_fusion
  29.9 0.1 reshape.108
  30.0 21.7 %all-to-all-done = bf16[8,16,6144]{2,1,0:T(8,128)(2,1)S(1)} async-done(((bf16[8,16,6144]{2,1,0:T(8,128)(2,1)}), bf16[8,16,6144]{2,1,0:T(8,128)(2,1)S(1)}, u32[]{:S(2)}, u32[]{:S(2)}) %all-to-all-start) | async-done | bytes 1572896 | tf_op jit(solution)/shard_map/all_to_all | solution.py:236
  51.7 0.0 copy-done.3
  51.7 0.0 copy-start.2
  51.7 1.2 copy-done.2
  52.9 1.0 shard_map.102
  53.9 0.0 copy-start.1
  53.9 1.7 copy-done.1
  55.6 20.9 %all-to-all-start.2 = ((bf16[16,128,768]{2,1,0:T(8,128)(2,1)}), bf16[16,128,768]{2,1,0:T(8,128)(2,1)}, u32[]{:S(2)}, u32[]{:S(2)}) async-start(bf16[16,128,768]{2,1,0:T(8,128)(2,1)} %copy-done.1), calls=%async_computation.2 | async-start | bytes 6291456 | tf_op jit(solution)/shard_map/all_to_all | solution.py:236
  76.6 0.2 select_reduce_fusion
  76.8 40.1 %all-to-all-done.2 = bf16[16,128,768]{2,1,0:T(8,128)(2,1)} async-done(((bf16[16,128,768]{2,1,0:T(8,128)(2,1)}), bf16[16,128,768]{2,1,0:T(8,128)(2,1)}, u32[]{:S(2)}, u32[]{:S(2)}) %all-to-all-start.2) | async-done | bytes 3145760 | tf_op jit(solution)/shard_map/all_to_all | solution.py:236
  116.9 50.4 %shard_map.103 = bf16[2048,768]{1,0:T(8,128)(2,1)S(1)} custom-call(s32[8]{0:T(128)S(1)} %get-tuple-element.23.start_ref, s32[8]{0:T(128)S(1)} %get-tuple-element.22.end_ref, bf16[2048,768]{1,0:T(8,128)(2,1)} %bitcast.11.x_ref), custom_call_target="tpu_custom_call" | custom-call | flops 7247757312 | bytes 6291456 | tf_op jit(solution)/shard_map/pallas_call | solution.py:176
  167.3 47.9 %all_to_all.60.came_ref = bf16[16,128,768]{2,1,0:T(8,128)(2,1)S(1)} all-to-all(bf16[16,128,768]{2,1,0:T(8,128)(2,1)S(1)} %bitcast.53), channel_id=1, replica_groups=mesh['half'=2,'sub'=16,'dp'=8] {'sub'}, dimensions={0} | all-to-all | bytes 6291456 | tf_op jit(solution)/shard_map/all_to_all | solution.py:236
  215.1 2.4 shard_map.104
  217.5 0.1 reshape.109
  217.6 13.0 %all_to_all.61 = bf16[8,2,128]{2,1,0:T(2,128)(2,1)S(1)} all-to-all(bf16[8,2,128]{2,1,0:T(2,128)(2,1)S(1)} %reshape.109), channel_id=1, replica_groups=mesh['half'=2,'sub'=16,'dp'=8] {'dp'}, dimensions={0} | all-to-all | bytes 8192 | tf_op jit(solution)/shard_map/all_to_all | solution.py:236
  230.7 0.1 reshape.110
  230.7 0.3 fusion
  231.1 0.5 copy.18
  231.6 22.1 %all_to_all.62 = f32[32,1,4096]{2,1,0:T(1,128)S(1)} all-to-all(f32[32,1,4096]{2,1,0:T(1,128)S(1)} %copy.18), channel_id=1, replica_groups=mesh['half'=2,'sub'=16,'dp'=8] {'half','sub'}, dimensions={0} | all-to-all | bytes 1048576 | tf_op jit(solution)/shard_map/all_to_all | solution.py:236
  253.7 0.4 reduce_sum.49
  254.0 0.4 collective-permute-start
  254.4 2.6 collective-permute-done
  257.0 0.9 collective-permute-start.1
  257.9 3.2 %collective-permute-done.1 = f32[32,128]{1,0:T(8,128)S(1)} collective-permute-done((f32[32,128]{1,0:T(8,128)S(1)}, f32[32,128]{1,0:T(8,128)S(1)}, u32[]{:S(2)}, u32[]{:S(2)}) %collective-permute-start.1) | collective-permute-done | bytes 16416 | tf_op jit(solution)/shard_map/ppermute | solution.py:309
  261.1 0.3 collective-permute-start.2
  261.4 6.2 %collective-permute-done.2 = f32[32,128]{1,0:T(8,128)S(1)} collective-permute-done((f32[32,128]{1,0:T(8,128)S(1)}, f32[32,128]{1,0:T(8,128)S(1)}, u32[]{:S(2)}, u32[]{:S(2)}) %collective-permute-start.2) | collective-permute-done | bytes 16416 | tf_op jit(solution)/shard_map/ppermute | solution.py:309
  267.6 0.5 broadcast_in_dim.54
  268.1 23.5 %all_to_all.63 = f32[32,1,4096]{2,1,0:T(1,128)S(1)} all-to-all(f32[32,1,4096]{2,1,0:T(1,128)S(1)} %broadcast_in_dim.54), channel_id=1, replica_groups=mesh['half'=2,'sub'=16,'dp'=8] {'half','sub'}, dimensions={0} | all-to-all | bytes 1048576 | tf_op jit(solution)/shard_map/all_to_all | solution.py:236
  291.6 0.9 copy.24
  292.5 0.9 copy.25
  (9 shorter events, 0.1 us)
Async XLA Ops:
  0.6 1.2 copy-start
  0.6 26.7 %copy-start.5 = (s32[1,5]{1,0:T(1,128)S(1)}, s32[1,5]{1,0:T(1,128)}, u32[]{:S(2)}) copy-start(s32[1,5]{1,0:T(1,128)} %param.12) | copy-start | bytes 64
  0.7 26.9 %copy-start.4 = (s32[1,5]{1,0:T(1,128)S(1)}, s32[1,5]{1,0:T(1,128)}, u32[]{:S(2)}) copy-start(s32[1,5]{1,0:T(1,128)} %param.11) | copy-start | bytes 64
  0.7 51.0 %copy-start.3 = (bf16[16,4096]{1,0:T(8,128)(2,1)S(1)}, bf16[16,4096]{1,0:T(8,128)(2,1)}, u32[]{:S(2)}) copy-start(bf16[16,4096]{1,0:T(8,128)(2,1)} %up_ref.3) | copy-start | bytes 393220
  23.7 28.0 %all-to-all-start = ((bf16[8,16,6144]{2,1,0:T(8,128)(2,1)}), bf16[8,16,6144]{2,1,0:T(8,128)(2,1)S(1)}, u32[]{:S(2)}, u32[]{:S(2)}) async-start(bf16[8,16,6144]{2,1,0:T(8,128)(2,1)} %bitcast.58), calls=%async_computation | async-start | bytes 3145728 | tf_op jit(solution)/shard_map/all_to_all | solution.py:236
  51.7 1.2 copy-start.2
  53.9 1.7 copy-start.1
  55.6 61.3 %all-to-all-start.2 = ((bf16[16,128,768]{2,1,0:T(8,128)(2,1)}), bf16[16,128,768]{2,1,0:T(8,128)(2,1)}, u32[]{:S(2)}, u32[]{:S(2)}) async-start(bf16[16,128,768]{2,1,0:T(8,128)(2,1)} %copy-done.1), calls=%async_computation.2 | async-start | bytes 6291456 | tf_op jit(solution)/shard_map/all_to_all | solution.py:236
  254.0 3.0 %collective-permute-start = (f32[32,128]{1,0:T(8,128)S(1)}, f32[32,128]{1,0:T(8,128)S(1)}, u32[]{:S(2)}, u32[]{:S(2)}) collective-permute-start(f32[32,128]{1,0:T(8,128)S(1)} %bitcast.61), channel_id=1, source_target_pairs={{0,1},{1,0},{2,3},{3,2},{4,5},{5,4},{6,7},{7,6},{8,9},{9,8},{10,11... | collective-permute-start | bytes 49160 | tf_op jit(solution)/shard_map/ppermute | solution.py:309
  257.0 4.1 %collective-permute-start.1 = (f32[32,128]{1,0:T(8,128)S(1)}, f32[32,128]{1,0:T(8,128)S(1)}, u32[]{:S(2)}, u32[]{:S(2)}) collective-permute-start(f32[32,128]{1,0:T(8,128)S(1)} %bitcast_add_fusion), channel_id=1, source_target_pairs={{0,2},{1,3},{2,0},{3,1},{4,6},{5,7},{6,4},{7,5},{8,10},{9,11},{10,... | collective-permute-start | bytes 49160 | tf_op jit(solution)/shard_map/ppermute | solution.py:309
  261.1 6.5 %collective-permute-start.2 = (f32[32,128]{1,0:T(8,128)S(1)}, f32[32,128]{1,0:T(8,128)S(1)}, u32[]{:S(2)}, u32[]{:S(2)}) collective-permute-start(f32[32,128]{1,0:T(8,128)S(1)} %fusion.10), channel_id=1, source_target_pairs={{0,4},{1,5},{2,6},{3,7},{4,0},{5,1},{6,2},{7,3},{8,12},{9,13},{10,... | collective-permute-start | bytes 49160 | tf_op jit(solution)/shard_map/ppermute | solution.py:309

commit v2 on v1

v2 whole, which is shorter than its diff:
```python
import math

import jax
import jax.numpy as jnp
from jax import lax
from jax.experimental import pallas as pl
from jax.experimental.pallas import tpu as pltpu
from jax.sharding import Mesh
from jax.sharding import PartitionSpec as P

HEAD_DIM = 128
HALF_DIM = HEAD_DIM // 2
PART = 256
BLOCK = 512
PAIR = 2 * HEAD_DIM
PIECE = 2 * PAIR + 2 * HEAD_DIM
rope_base = 500000.0
VMEM_BYTES = 48 * 1024 * 1024
HIDDEN = -1e30
F32 = jnp.float32
BF16 = jnp.bfloat16


def rope_tables(offsets):
    index_float = jnp.arange(HALF_DIM, dtype=F32)
    inverse = jnp.power(F32(rope_base), -index_float / HALF_DIM)
    angles = offsets.astype(F32)[:, None] * inverse[None, :]
    cosine, sine = jnp.cos(angles), jnp.sin(angles)
    return jnp.concatenate([cosine, cosine], axis=1), jnp.concatenate([-sine, sine], axis=1)


def rotated(table, cosine, sine):
    return table * cosine + pltpu.roll(table, HALF_DIM, 1) * sine


def prepare_kernel(qkv_ref, up_ref, cos_ref, sin_ref, grad_ref, valid_ref, out_ref):
    cosine = cos_ref[...]
    sine = sin_ref[...]
    kept = valid_ref[...] > 0
    rank, queries = up_ref.shape
    kv_width = (qkv_ref.shape[1] - HEAD_DIM - queries) // 2
    low_at = queries + 2 * kv_width
    low = qkv_ref[:, low_at : low_at + rank]
    pieces = out_ref.shape[0]
    for piece in range(pieces):
        columns = slice(piece * PAIR, (piece + 1) * PAIR)
        full = qkv_ref[:, columns].astype(F32) + jnp.dot(
            low, up_ref[:, columns], preferred_element_type=F32
        )
        for head in range(2):
            at = slice(head * HEAD_DIM, (head + 1) * HEAD_DIM)
            out_ref[piece, :, at] = rotated(full[:, at], cosine, sine).astype(BF16)
        grad = grad_ref[:, columns]
        out_ref[piece, :, PAIR : 2 * PAIR] = jnp.where(kept, grad, jnp.zeros_like(grad))
    for key_head in range(kv_width // HEAD_DIM):
        at = queries + key_head * HEAD_DIM
        keys = rotated(qkv_ref[:, at : at + HEAD_DIM].astype(F32), cosine, sine).astype(BF16)
        values = qkv_ref[:, at + kv_width : at + kv_width + HEAD_DIM]
        for piece in (2 * key_head, 2 * key_head + 1):
            out_ref[piece, :, 2 * PAIR : 2 * PAIR + HEAD_DIM] = keys
            out_ref[piece, :, 2 * PAIR + HEAD_DIM :] = values


def attention_kernel(start_ref, end_ref, x_ref, out_ref, kt, vt, dkt, dvt, store0, store1):
    store = (store0, store1)
    step = pl.program_id(0)
    blocks = pl.num_programs(0)
    factor = 1.0 / math.sqrt(HEAD_DIM)
    exponent = factor * math.log2(math.e)
    key_at = 2 * PAIR
    value_at = 2 * PAIR + HEAD_DIM
    tiles = x_ref.shape[0] // BLOCK
    per = BLOCK // PART

    @pl.when(step == 0)
    def _():
        for tile in range(tiles):
            rows = slice(tile * BLOCK, (tile + 1) * BLOCK)
            kt[tile] = x_ref[rows, key_at:value_at].T
            vt[tile] = x_ref[rows, value_at:].T
        dkt[...] = jnp.zeros_like(dkt)
        dvt[...] = jnp.zeros_like(dvt)

    own = pl.ds(pl.multiple_of(step * BLOCK, BLOCK), BLOCK)
    first = start_ref[step * per] // BLOCK
    last = step
    end_row = end_ref[step * per]
    column = lax.broadcasted_iota(jnp.int32, (1, BLOCK), 1)
    row = lax.broadcasted_iota(jnp.int32, (BLOCK, 1), 0)
    low_row = jnp.full((BLOCK, 1), start_ref[step * per] - last * BLOCK, jnp.int32)
    high_row = jnp.full((BLOCK, 1), end_row - last * BLOCK, jnp.int32)
    for part in range(1, per):
        inside = row >= part * PART
        low_row = jnp.where(inside, start_ref[step * per + part] - last * BLOCK, low_row)
        high_row = jnp.where(inside, end_ref[step * per + part] - last * BLOCK, high_row)
    queries = [x_ref[own, h * HEAD_DIM : (h + 1) * HEAD_DIM] for h in range(2)]
    grads = [x_ref[own, PAIR + h * HEAD_DIM : PAIR + (h + 1) * HEAD_DIM] for h in range(2)]

    def folded(op, table):
        parts = [table[:, c : c + HEAD_DIM] for c in range(0, BLOCK, HEAD_DIM)]
        while len(parts) > 1:
            parts = [op(a, b) for a, b in zip(parts[::2], parts[1::2])]
        return parts[0]

    def spread(table):
        return jnp.concatenate([table] * (BLOCK // HEAD_DIM), axis=1)

    def key_rows(tile):
        return pl.ds(pl.multiple_of(tile * BLOCK, BLOCK), BLOCK)

    diagonal = (column == row) | ((column < row) & (column >= low_row) & (column < high_row))
    carry = []
    for h in range(2):
        scores = jnp.dot(queries[h], kt[last], preferred_element_type=F32) * exponent
        scores = jnp.where(diagonal, scores, HIDDEN)
        store[h][last] = scores
        top = folded(jnp.maximum, scores)
        carry += [top, folded(jnp.add, jnp.exp2(scores - spread(top)))]

    def score_pass(tile, carry):
        bias = jnp.where(tile * BLOCK + column < end_row, F32(0.0), F32(HIDDEN))
        result = []
        for h in range(2):
            top, total = carry[2 * h], carry[2 * h + 1]
            scores = jnp.dot(queries[h], kt[tile], preferred_element_type=F32) * exponent + bias
            store[h][tile] = scores
            higher = jnp.maximum(top, folded(jnp.maximum, scores))
            total = total * jnp.exp2(top - higher) + folded(
                jnp.add, jnp.exp2(scores - spread(higher))
            )
            result += [higher, total]
        return tuple(result)

    carry = lax.fori_loop(first, last, score_pass, tuple(carry))
    tops, inverse = [], []
    for h in range(2):
        lane_top, lane_total = carry[2 * h], carry[2 * h + 1]
        top = jnp.max(lane_top, axis=1, keepdims=True)
        total = jnp.sum(lane_total * jnp.exp2(lane_top - top), axis=1, keepdims=True)
        tops.append(top)
        inverse.append(1.0 / total)

    empty = jnp.zeros((BLOCK, HEAD_DIM), F32)

    def probs_of(h, tile):
        return jnp.exp2(store[h][tile] - tops[h]) * inverse[h]

    def out_part(h, tile, total):
        values = x_ref[key_rows(tile), value_at:]
        return total + jnp.dot(
            probs_of(h, tile).astype(BF16), values, preferred_element_type=F32
        )

    outs = [None, None]
    deltas = [None, None]
    queries_t = [table.T for table in queries]
    grads_t = [table.T for table in grads]

    def settle(h, total):
        outs[h] = total.astype(BF16)
        deltas[h] = jnp.sum(
            grads[h].astype(F32) * outs[h].astype(F32), axis=1, keepdims=True
        )

    def grad_part(h, tile, total):
        keys = x_ref[key_rows(tile), key_at:value_at]
        grad_probs = jnp.dot(grads[h], vt[tile], preferred_element_type=F32)
        probs = probs_of(h, tile)
        grad_scores = (probs * (grad_probs - deltas[h])).astype(BF16)
        total = total + jnp.dot(grad_scores, keys, preferred_element_type=F32)
        dkt[tile] += jnp.dot(queries_t[h], grad_scores, preferred_element_type=F32)
        dvt[tile] += jnp.dot(grads_t[h], probs.astype(BF16), preferred_element_type=F32)
        return total

    def out_pass(tile, carry):
        return tuple(out_part(h, tile, carry[h]) for h in range(2))

    def gradient_pass(tile, carry):
        return tuple(grad_part(h, tile, carry[h]) for h in range(2))

    sums = lax.fori_loop(first, last + 1, out_pass, (empty, empty))
    for h in range(2):
        settle(h, sums[h])
    query_sums = lax.fori_loop(first, last + 1, gradient_pass, (empty, empty))
    for h in range(2):
        at = h * HEAD_DIM
        out_ref[own, at : at + HEAD_DIM] = outs[h]
        out_ref[own, PAIR + at : PAIR + at + HEAD_DIM] = (query_sums[h] * factor).astype(BF16)

    @pl.when(step == blocks - 1)
    def _():
        for tile in range(tiles):
            rows = slice(tile * BLOCK, (tile + 1) * BLOCK)
            out_ref[rows, key_at:value_at] = (dkt[tile] * factor).T.astype(BF16)
            out_ref[rows, value_at:] = dvt[tile].T.astype(BF16)


def attention(table, starts, ends):
    rows, width = table.shape
    blocks = rows // BLOCK
    tiles = blocks * (blocks + 1) // 2
    return pl.pallas_call(
        attention_kernel,
        out_shape=jax.ShapeDtypeStruct((rows, width), BF16),
        grid_spec=pltpu.PrefetchScalarGridSpec(
            num_scalar_prefetch=2,
            grid=(blocks,),
            in_specs=[pl.BlockSpec((rows, width), lambda i, *_: (0, 0))],
            out_specs=pl.BlockSpec((rows, width), lambda i, *_: (0, 0)),
            scratch_shapes=[
                pltpu.VMEM((blocks, HEAD_DIM, BLOCK), BF16),
                pltpu.VMEM((blocks, HEAD_DIM, BLOCK), BF16),
                pltpu.VMEM((blocks, HEAD_DIM, BLOCK), F32),
                pltpu.VMEM((blocks, HEAD_DIM, BLOCK), F32),
                pltpu.VMEM((blocks, BLOCK, BLOCK), F32),
                pltpu.VMEM((blocks, BLOCK, BLOCK), F32),
            ],
        ),
        compiler_params=pltpu.CompilerParams(vmem_limit_bytes=VMEM_BYTES),
        cost_estimate=pl.CostEstimate(
            flops=tiles * 2 * 6 * 2 * BLOCK * BLOCK * HEAD_DIM,
            bytes_accessed=4 * rows * width,
            transcendentals=tiles * 2 * BLOCK * BLOCK,
        ),
    )(starts, ends, table)


def finish_kernel(
    came_ref, low_ref, up_ref, inputs_ref, cos_ref, sin_ref, out_ref, grad_ref, term_ref
):
    cosine = cos_ref[...]
    sine = -sin_ref[...]
    rank, queries = up_ref.shape
    low_t = low_ref[...].astype(F32).T.astype(BF16)
    kv_width = (grad_ref.shape[1] - queries) // 2
    dlow = jnp.zeros(low_ref.shape, F32)
    for piece in range(came_ref.shape[0]):
        columns = slice(piece * PAIR, (piece + 1) * PAIR)
        out_ref[:, columns] = came_ref[piece, :, :PAIR]
        for head in range(2):
            at = PAIR + head * HEAD_DIM
            to = piece * PAIR + head * HEAD_DIM
            grad_ref[:, to : to + HEAD_DIM] = rotated(
                came_ref[piece, :, at : at + HEAD_DIM].astype(F32), cosine, sine
            ).astype(BF16)
        part = grad_ref[:, columns]
        dlow += lax.dot_general(
            part, up_ref[:, columns], (((1,), (1,)), ((), ())), preferred_element_type=F32
        )
        term_ref[piece, rank:] = jnp.dot(low_t, part, preferred_element_type=F32)
    dlow_t = dlow.astype(BF16).astype(F32).T.astype(BF16)
    for piece in range(came_ref.shape[0]):
        columns = slice(piece * PAIR, (piece + 1) * PAIR)
        term_ref[piece, :rank] = jnp.dot(
            dlow_t, inputs_ref[:, columns], preferred_element_type=F32
        )
    for key_head in range(kv_width // HEAD_DIM):
        pair = (2 * key_head, 2 * key_head + 1)
        keys, values = (
            sum(came_ref[piece, :, at : at + HEAD_DIM].astype(F32) for piece in pair)
            for at in (2 * PAIR, 2 * PAIR + HEAD_DIM)
        )
        at = queries + key_head * HEAD_DIM
        grad_ref[:, at : at + HEAD_DIM] = rotated(keys, cosine, sine).astype(BF16)
        grad_ref[:, at + kv_width : at + kv_width + HEAD_DIM] = values.astype(BF16)


def exchange(table, axis):
    return lax.all_to_all(table, axis, split_axis=0, concat_axis=0, tiled=True)


def local(
    projection_rows, normed_input_rows, adapter_down, adapter_up, lengths, groups, output_gradient
):
    qkv_local = projection_rows[0]
    x_local = normed_input_rows[0]
    grad_raw = output_gradient[0]
    length_row = lengths[0]
    width_row = groups[0]
    token_count, model_width = x_local.shape
    qkv_width = qkv_local.shape[1]
    rank, query_columns = adapter_up.shape
    members = lax.axis_size("sub")
    half_index = lax.axis_index("half")
    group_index = half_index * members + lax.axis_index("sub")
    low_local = jnp.dot(x_local, adapter_down, preferred_element_type=F32).astype(BF16)
    low_wide = jnp.pad(low_local, ((0, 0), (0, HEAD_DIM - rank)))
    packed_qkv = exchange(jnp.concatenate([qkv_local, low_wide], axis=1), "dp")
    packed_low = packed_qkv[:, qkv_width : qkv_width + rank]

    ends_dev = jnp.cumsum(width_row)
    starts_dev = ends_dev - width_row

    def owner_of(device):
        picked = (device[:, None] >= starts_dev[None, :]) & (device[:, None] < ends_dev[None, :])
        start = jnp.sum(jnp.where(picked, starts_dev[None, :], 0), axis=1)
        length = jnp.sum(jnp.where(picked, length_row[None, :], 0), axis=1)
        return start, length

    start_me, length_me = owner_of(group_index[None])
    row_at = jnp.arange(token_count, dtype=jnp.int32)
    local_offsets = (group_index - start_me) * token_count + row_at
    row_valid = (local_offsets < length_me).astype(jnp.int32)[:, None]
    cosine, sine = rope_tables(local_offsets)
    per_block = PART // token_count
    block_device = half_index * members + per_block * jnp.arange(
        members // per_block, dtype=jnp.int32
    )
    block_start, block_length = owner_of(block_device)
    first_rows = (block_start - half_index * members) * token_count
    starts = first_rows
    ends = first_rows + block_length

    params = pltpu.CompilerParams(vmem_limit_bytes=VMEM_BYTES)
    pieces = pl.pallas_call(
        prepare_kernel,
        out_shape=jax.ShapeDtypeStruct((members, token_count, PIECE), BF16),
        compiler_params=params,
    )(packed_qkv, adapter_up, cosine, sine, grad_raw, row_valid)
    table = exchange(pieces, "sub").reshape(members * token_count, PIECE)
    table, x_held = lax.optimization_barrier((table, x_local))
    packed_inputs = exchange(x_held, "dp")
    results = attention(table, starts, ends)
    came = exchange(results.reshape(members, token_count, PIECE), "sub")
    attn_rows, grad_rows, terms = pl.pallas_call(
        finish_kernel,
        out_shape=(
            jax.ShapeDtypeStruct((token_count, query_columns), BF16),
            jax.ShapeDtypeStruct((token_count, qkv_width), BF16),
            jax.ShapeDtypeStruct((members, 2 * rank, PAIR), F32),
        ),
        compiler_params=params,
    )(came, packed_low, adapter_up, packed_inputs, cosine, sine)
    total = jnp.sum(exchange(terms, "sub"), axis=0)
    for axis, apart in (("half", 1), ("dp", 1), ("dp", 2), ("dp", 4)):
        size = lax.axis_size(axis)
        total = total + lax.ppermute(total, axis, [(i, i ^ apart) for i in range(size)])
    whole = exchange(jnp.broadcast_to(total.astype(BF16)[None], terms.shape), "sub").astype(F32)
    grad_a = whole[:, :rank].transpose(0, 2, 1).reshape(model_width, rank)
    grad_b = whole[:, rank:].transpose(1, 0, 2).reshape(rank, query_columns)
    return (attn_rows[None], grad_rows[None], grad_a, grad_b)


def solution(mesh):
    members, replicas = mesh.devices.shape
    split = Mesh(mesh.devices.reshape(2, members // 2, replicas), ("half", "sub", "dp"))
    rows = P("dp", ("half", "sub"), None)
    placed = (rows, rows, P(), P(), P("dp", None), P("dp", None), rows)
    return jax.shard_map(
        local,
        mesh=split,
        in_specs=placed,
        out_specs=(rows, rows, P(), P()),
        check_vma=False,
    )
```

time: 294 us -> 245 us (0.83)
  blocking collectives: 127 us -> 93.4 us
  Pallas kernels: 53.7 us -> 22.2 us
  starting transfers between devices: 26.1 us -> 44.4 us
  waiting for transfers between devices: 73.8 us -> 67.8 us
    all_to_all x5 -> x3, blocking collectives: 127 us -> 93.4 us  [exchange(): return lax.all_to_all(table, axis, split_axis=0, concat_axis=0, tiled=True)]
    pallas_call x1, Pallas kernels: 50.4 us -> 18.4 us  [attention(): pl.pallas_call(attention_kernel, out_shape=jax.ShapeDtypeStruct((rows, wi...]
    ppermute x3 -> x4, starting transfers between devices: 1.54 us -> 15.2 us  [local(): lax.ppermute(total, axis, [(i, i ^ apart) for i in range(size)])]
    ppermute x3 -> x4, waiting for transfers between devices: 12 us -> 5.78 us  [local(): lax.ppermute(total, axis, [(i, i ^ apart) for i in range(size)])]
    all_to_all x2 -> x3, starting transfers between devices: 24.5 us -> 29.3 us  [exchange(): return lax.all_to_all(table, axis, split_axis=0, concat_axis=0, tiled=True)]
    unnamed x18 -> x22, local copies, waits for them, and re-layouts: 6.19 us -> 5.82 us
    all_to_all x2 -> x3, waiting for transfers between devices: 61.8 us -> 62 us  [exchange(): return lax.all_to_all(table, axis, split_axis=0, concat_axis=0, tiled=True)]
  transfers between devices with their start and end apart: 5 -> 7, of which waited for: 5 -> 6; matrix products, arithmetic and copies ran while one was open for 1% -> 1% of each run, Pallas kernels for 0% -> 8%
where the time goes in v2:
time: 245 us; the launch traced here: 244 us
  blocking collectives  93.4 us (38%)
  waiting for transfers between devices  67.8 us (28%)
  starting transfers between devices  44.4 us (18%)
  Pallas kernels  22.2 us (9%)
  local copies, waits for them, and re-layouts  8.67 us (4%)
  other arithmetic  4.88 us (2%)
    all_to_all x3, blocking collectives, exchange(): return lax.all_to_all(table, axis, split_axis=0, concat_axis=0, tiled=True)  93.4 us
    all_to_all x3, waiting for transfers between devices, exchange(): return lax.all_to_all(table, axis, split_axis=0, concat_axis=0, tiled=True)  62 us
    all_to_all x3, starting transfers between devices, exchange(): return lax.all_to_all(table, axis, split_axis=0, concat_axis=0, tiled=True)  29.3 us
    pallas_call x1, Pallas kernels, attention(): pl.pallas_call(attention_kernel, out_shape=jax.ShapeDtypeStruct((rows, wi...  18.4 us
    ppermute x4, starting transfers between devices, local(): lax.ppermute(total, axis, [(i, i ^ apart) for i in range(size)])  15.2 us
    unnamed x22, local copies, waits for them, and re-layouts  5.82 us
    ppermute x4, waiting for transfers between devices, local(): lax.ppermute(total, axis, [(i, i ^ apart) for i in range(size)])  5.78 us
  transfers between devices with their start and end apart: 7, of which 6 were waited for; matrix products, arithmetic and copies ran while one was open for 1% of the time, Pallas kernels for 8%

profile of v2, /device:TPU:1, one launch (start us, length us, event | category | flops | bytes accessed | tf_op | source)
XLA Modules:
  0.0 244.4 jit_solution(18019330011827061618)
XLA Ops:
  0.6 0.0 copy-start
  0.6 0.9 copy-done
  1.5 1.6 convolution_convert_fusion
  3.1 0.1 copy.24
  3.3 2.7 %pad_maximum_fusion = bf16[8,16,6272]{2,1,0:T(8,128)(2,1)} fusion(bf16[8,16,128]{2,1,0:T(8,128)(2,1)S(1)} %bitcast.50, bf16[8,16,6144]{2,1,0:T(8,128)(2,1)} %bitcast.47), kind=kLoop, calls=%fused_computation | loop fusion | flops 3211264 | bytes 3211264 | tf_op jit(solution)/shard_map/concatenate | solution.py:288
  6.0 0.0 copy-start.9
  6.0 0.0 copy-start.8
  6.0 0.0 copy-start.5
  6.0 0.0 copy-start.6
  6.0 11.8 %all-to-all-start = ((bf16[8,16,6272]{2,1,0:T(8,128)(2,1)}), bf16[8,16,6272]{2,1,0:T(8,128)(2,1)S(1)}, u32[]{:S(2)}, u32[]{:S(2)}) async-start(bf16[8,16,6272]{2,1,0:T(8,128)(2,1)} %pad_maximum_fusion), calls=%async_computation | async-start | bytes 3211264 | tf_op jit(solution)/shard_map/all_to_all | solution.py:269
  17.8 0.0 copy-done.9
  17.8 0.2 reduce-window.4
  18.0 0.0 copy-done.8
  18.0 0.6 select_reduce_fusion.2
  19.3 0.7 fusion.valid_ref
  20.0 0.3 fusion.1
  20.3 0.1 pad_maximum_fusion.1
  20.4 23.0 %all-to-all-done = bf16[8,16,6272]{2,1,0:T(8,128)(2,1)S(1)} async-done(((bf16[8,16,6272]{2,1,0:T(8,128)(2,1)}), bf16[8,16,6272]{2,1,0:T(8,128)(2,1)S(1)}, u32[]{:S(2)}, u32[]{:S(2)}) %all-to-all-start) | async-done | bytes 1605664 | tf_op jit(solution)/shard_map/all_to_all | solution.py:269
  43.4 0.0 copy-done.5
  43.4 0.0 copy-done.6
  43.4 1.0 shard_map.102
  44.4 0.2 copy-done.1
  44.6 58.3 %all_to_all.39 = bf16[16,128,768]{2,1,0:T(8,128)(2,1)} all-to-all(bf16[16,128,768]{2,1,0:T(8,128)(2,1)S(1)} %shard_map.102), channel_id=1, replica_groups=mesh['half'=2,'sub'=16,'dp'=8] {'sub'}, dimensions={0} | all-to-all | bytes 6291456 | tf_op jit(solution)/shard_map/all_to_all | solution.py:269
  102.9 4.3 %all-to-all-start.3 = ((bf16[8,16,4096]{2,1,0:T(8,128)(2,1)}), bf16[8,16,4096]{2,1,0:T(8,128)(2,1)S(1)}, u32[]{:S(2)}, u32[]{:S(2)}) async-start(bf16[8,16,4096]{2,1,0:T(8,128)(2,1)} %bitcast.45), calls=%async_computation.3 | async-start | bytes 2097152 | tf_op jit(solution)/shard_map/all_to_all | solution.py:269
  107.2 0.2 select_reduce_fusion
  107.4 18.4 %shard_map.103 = bf16[2048,768]{1,0:T(8,128)(2,1)S(1)} custom-call(s32[8]{0:T(128)S(1)} %get-tuple-element.19.start_ref, s32[8]{0:T(128)S(1)} %get-tuple-element.18.end_ref, bf16[2048,768]{1,0:T(8,128)(2,1)} %bitcast.46), custom_call_target="tpu_custom_call" | custom-call | flops 8053063680 | bytes 6291456 | tf_op jit(solution)/shard_map/pallas_call | solution.py:202
  125.8 0.0 copy-start.4
  125.8 1.6 copy-done.4
  127.4 0.0 all-to-all-done.3
  127.4 1.0 copy-done.2
  128.4 13.2 %all-to-all-start.2 = ((bf16[16,128,768]{2,1,0:T(8,128)(2,1)}), bf16[16,128,768]{2,1,0:T(8,128)(2,1)S(1)}, u32[]{:S(2)}, u32[]{:S(2)}) async-start(bf16[16,128,768]{2,1,0:T(8,128)(2,1)} %bitcast.43), calls=%async_computation.2 | async-start | bytes 6291456 | tf_op jit(solution)/shard_map/all_to_all | solution.py:269
  141.6 1.4 slice.12.low_ref
  143.0 39.0 %all-to-all-done.2.came_ref = bf16[16,128,768]{2,1,0:T(8,128)(2,1)S(1)} async-done(((bf16[16,128,768]{2,1,0:T(8,128)(2,1)}), bf16[16,128,768]{2,1,0:T(8,128)(2,1)S(1)}, u32[]{:S(2)}, u32[]{:S(2)}) %all-to-all-start.2) | async-done | bytes 3145760 | tf_op jit(solution)/shard_map/all_to_all | solution.py:269
  181.9 1.2 copy-done.3
  183.2 0.8 copy-done.7
  183.9 2.8 %shard_map.104 = (bf16[128,4096]{1,0:T(8,128)(2,1)}, bf16[128,6144]{1,0:T(8,128)(2,1)}, f32[16,32,256]{2,1,0:T(8,128)S(1)}) custom-call(bf16[16,128,768]{2,1,0:T(8,128)(2,1)S(1)} %all-to-all-done.2.came_ref, bf16[128,16]{1,0:T(8,128)(2,1)S(1)} %copy-done.7, bf16[16,4096]{1,0:T(8,128)(2,1)S(1)} %copy-done.6, bf16[128,4096]{1,0:T(8,128)(2,1)S(1)} %bitcast.42, ...), custom_call_target="tpu_custom_call" | custom-call | tf_op jit(solution)/shard_map/pallas_call | solution.py:325
  186.7 19.7 %all_to_all.40 = f32[16,32,256]{2,1,0:T(8,128)S(1)} all-to-all(f32[16,32,256]{2,1,0:T(8,128)S(1)} %get-tuple-element.13), channel_id=1, replica_groups=mesh['half'=2,'sub'=16,'dp'=8] {'sub'}, dimensions={0} | all-to-all | bytes 1048576 | tf_op jit(solution)/shard_map/all_to_all | solution.py:269
  206.4 4.1 %collective-permute-start = (f32[32,256]{1,0:T(8,128)S(1)}, f32[32,256]{1,0:T(8,128)S(1)}, u32[]{:S(2)}, u32[]{:S(2)}) collective-permute-start(f32[32,256]{1,0:T(8,128)S(1)} %reduce_sum.49), channel_id=1, source_target_pairs={{0,128},{128,0},{1,129},{129,1},{2,130},{130,2},{3,131},{131,3},{4... | collective-permute-start | bytes 98312 | tf_op jit(solution)/shard_map/ppermute | solution.py:337
  210.5 1.3 collective-permute-done
  211.8 3.2 %collective-permute-start.1 = (f32[32,256]{1,0:T(8,128)S(1)}, f32[32,256]{1,0:T(8,128)S(1)}, u32[]{:S(2)}, u32[]{:S(2)}) collective-permute-start(f32[32,256]{1,0:T(8,128)S(1)} %add.60), channel_id=1, source_target_pairs={{0,1},{1,0},{2,3},{3,2},{4,5},{5,4},{6,7},{7,6},{8,9},{9,8},{10,11... | collective-permute-start | bytes 98312 | tf_op jit(solution)/shard_map/ppermute | solution.py:337
  215.0 1.3 collective-permute-done.1
  216.3 2.4 collective-permute-start.2
  218.7 1.9 collective-permute-done.2
  220.6 5.5 %collective-permute-start.3 = (f32[32,256]{1,0:T(8,128)S(1)}, f32[32,256]{1,0:T(8,128)S(1)}, u32[]{:S(2)}, u32[]{:S(2)}) collective-permute-start(f32[32,256]{1,0:T(8,128)S(1)} %add.62), channel_id=1, source_target_pairs={{0,4},{1,5},{2,6},{3,7},{4,0},{5,1},{6,2},{7,3},{8,12},{9,13},{10,... | collective-permute-start | bytes 98312 | tf_op jit(solution)/shard_map/ppermute | solution.py:337
  226.1 1.3 collective-permute-done.3
  227.4 15.4 %all_to_all.41 = bf16[16,32,256]{2,1,0:T(8,128)(2,1)S(1)} all-to-all(bf16[16,32,256]{2,1,0:T(8,128)(2,1)S(1)} %broadcast_in_dim.52), channel_id=1, replica_groups=mesh['half'=2,'sub'=16,'dp'=8] {'sub'}, dimensions={0} | all-to-all | bytes 524288 | tf_op jit(solution)/shard_map/all_to_all | solution.py:269
  242.9 0.7 copy.26
  243.7 0.7 copy.25
  (17 shorter events, 0.2 us)
Async XLA Ops:
  0.6 0.9 copy-start
  6.0 11.8 %copy-start.9 = (s32[1,5]{1,0:T(1,128)S(1)}, s32[1,5]{1,0:T(1,128)}, u32[]{:S(2)}) copy-start(s32[1,5]{1,0:T(1,128)} %param.12) | copy-start | bytes 64
  6.0 12.0 %copy-start.8 = (s32[1,5]{1,0:T(1,128)S(1)}, s32[1,5]{1,0:T(1,128)}, u32[]{:S(2)}) copy-start(s32[1,5]{1,0:T(1,128)} %param.11) | copy-start | bytes 64
  6.0 37.4 %copy-start.5 = (bf16[1,128,4096]{2,1,0:T(8,128)(2,1)S(1)}, bf16[1,128,4096]{2,1,0:T(8,128)(2,1)}, u32[]{:S(2)}) copy-start(bf16[1,128,4096]{2,1,0:T(8,128)(2,1)} %param.13) | copy-start | bytes 3145732
  6.0 37.4 %copy-start.6 = (bf16[16,4096]{1,0:T(8,128)(2,1)S(1)}, bf16[16,4096]{1,0:T(8,128)(2,1)}, u32[]{:S(2)}) copy-start(bf16[16,4096]{1,0:T(8,128)(2,1)} %up_ref.3) | copy-start | bytes 393220
  6.0 37.4 %all-to-all-start = ((bf16[8,16,6272]{2,1,0:T(8,128)(2,1)}), bf16[8,16,6272]{2,1,0:T(8,128)(2,1)S(1)}, u32[]{:S(2)}, u32[]{:S(2)}) async-start(bf16[8,16,6272]{2,1,0:T(8,128)(2,1)} %pad_maximum_fusion), calls=%async_computation | async-start | bytes 3211264 | tf_op jit(solution)/shard_map/all_to_all | solution.py:269
  43.4 1.2 copy-start.1
  102.9 24.5 %all-to-all-start.3 = ((bf16[8,16,4096]{2,1,0:T(8,128)(2,1)}), bf16[8,16,4096]{2,1,0:T(8,128)(2,1)S(1)}, u32[]{:S(2)}, u32[]{:S(2)}) async-start(bf16[8,16,4096]{2,1,0:T(8,128)(2,1)} %bitcast.45), calls=%async_computation.3 | async-start | bytes 2097152 | tf_op jit(solution)/shard_map/all_to_all | solution.py:269
  125.8 1.6 copy-start.4
  127.4 1.0 copy-start.2
  128.4 53.6 %all-to-all-start.2 = ((bf16[16,128,768]{2,1,0:T(8,128)(2,1)}), bf16[16,128,768]{2,1,0:T(8,128)(2,1)S(1)}, u32[]{:S(2)}, u32[]{:S(2)}) async-start(bf16[16,128,768]{2,1,0:T(8,128)(2,1)} %bitcast.43), calls=%async_computation.2 | async-start | bytes 6291456 | tf_op jit(solution)/shard_map/all_to_all | solution.py:269
  181.9 1.2 copy-start.3
  183.2 0.8 copy-start.7
  206.4 5.4 %collective-permute-start = (f32[32,256]{1,0:T(8,128)S(1)}, f32[32,256]{1,0:T(8,128)S(1)}, u32[]{:S(2)}, u32[]{:S(2)}) collective-permute-start(f32[32,256]{1,0:T(8,128)S(1)} %reduce_sum.49), channel_id=1, source_target_pairs={{0,128},{128,0},{1,129},{129,1},{2,130},{130,2},{3,131},{131,3},{4... | collective-permute-start | bytes 98312 | tf_op jit(solution)/shard_map/ppermute | solution.py:337
  211.8 4.5 %collective-permute-start.1 = (f32[32,256]{1,0:T(8,128)S(1)}, f32[32,256]{1,0:T(8,128)S(1)}, u32[]{:S(2)}, u32[]{:S(2)}) collective-permute-start(f32[32,256]{1,0:T(8,128)S(1)} %add.60), channel_id=1, source_target_pairs={{0,1},{1,0},{2,3},{3,2},{4,5},{5,4},{6,7},{7,6},{8,9},{9,8},{10,11... | collective-permute-start | bytes 98312 | tf_op jit(solution)/shard_map/ppermute | solution.py:337
  216.3 4.3 %collective-permute-start.2 = (f32[32,256]{1,0:T(8,128)S(1)}, f32[32,256]{1,0:T(8,128)S(1)}, u32[]{:S(2)}, u32[]{:S(2)}) collective-permute-start(f32[32,256]{1,0:T(8,128)S(1)} %add.61), channel_id=1, source_target_pairs={{0,2},{1,3},{2,0},{3,1},{4,6},{5,7},{6,4},{7,5},{8,10},{9,11},{10,... | collective-permute-start | bytes 98312 | tf_op jit(solution)/shard_map/ppermute | solution.py:337
  220.6 6.8 %collective-permute-start.3 = (f32[32,256]{1,0:T(8,128)S(1)}, f32[32,256]{1,0:T(8,128)S(1)}, u32[]{:S(2)}, u32[]{:S(2)}) collective-permute-start(f32[32,256]{1,0:T(8,128)S(1)} %add.62), channel_id=1, source_target_pairs={{0,4},{1,5},{2,6},{3,7},{4,0},{5,1},{6,2},{7,3},{8,12},{9,13},{10,... | collective-permute-start | bytes 98312 | tf_op jit(solution)/shard_map/ppermute | solution.py:337

commit v3 on v2

--- a/solution.py
+++ b/solution.py
@@ -16,6 +16,7 @@
 PIECE = 2 * PAIR + 2 * HEAD_DIM
 rope_base = 500000.0
 VMEM_BYTES = 48 * 1024 * 1024
+ATTENTION_VMEM_BYTES = 60 * 1024 * 1024
 HIDDEN = -1e30
 F32 = jnp.float32
 BF16 = jnp.bfloat16
@@ -31,6 +32,21 @@
 
 def rotated(table, cosine, sine):
     return table * cosine + pltpu.roll(table, HALF_DIM, 1) * sine
+
+
+def widen_kernel(inputs_ref, down_ref, qkv_ref, out_ref, slab, sems):
+    width = qkv_ref.shape[1]
+    move = pltpu.make_async_copy(qkv_ref, out_ref.at[:, :width], sems.at[0])
+    move.start()
+    low = lax.dot_general(
+        inputs_ref[...], down_ref[...], (((1,), (1,)), ((), ())), preferred_element_type=F32
+    )
+    slab[...] = jnp.zeros_like(slab)
+    slab[:, : low.shape[1]] = low.astype(BF16)
+    add = pltpu.make_async_copy(slab, out_ref.at[:, width:], sems.at[1])
+    add.start()
+    move.wait()
+    add.wait()
 
 
 def prepare_kernel(qkv_ref, up_ref, cos_ref, sin_ref, grad_ref, valid_ref, out_ref):
@@ -216,7 +232,7 @@
                 pltpu.VMEM((blocks, BLOCK, BLOCK), F32),
             ],
         ),
-        compiler_params=pltpu.CompilerParams(vmem_limit_bytes=VMEM_BYTES),
+        compiler_params=pltpu.CompilerParams(vmem_limit_bytes=ATTENTION_VMEM_BYTES),
         cost_estimate=pl.CostEstimate(
             flops=tiles * 2 * 6 * 2 * BLOCK * BLOCK * HEAD_DIM,
             bytes_accessed=4 * rows * width,
@@ -247,13 +263,13 @@
         dlow += lax.dot_general(
             part, up_ref[:, columns], (((1,), (1,)), ((), ())), preferred_element_type=F32
         )
-        term_ref[piece, rank:] = jnp.dot(low_t, part, preferred_element_type=F32)
+        term_ref[piece, rank:] = jnp.dot(low_t, part, preferred_element_type=F32).astype(BF16)
     dlow_t = dlow.astype(BF16).astype(F32).T.astype(BF16)
     for piece in range(came_ref.shape[0]):
         columns = slice(piece * PAIR, (piece + 1) * PAIR)
         term_ref[piece, :rank] = jnp.dot(
             dlow_t, inputs_ref[:, columns], preferred_element_type=F32
-        )
+        ).astype(BF16)
     for key_head in range(kv_width // HEAD_DIM):
         pair = (2 * key_head, 2 * key_head + 1)
         keys, values = (
@@ -263,6 +279,14 @@
         at = queries + key_head * HEAD_DIM
         grad_ref[:, at : at + HEAD_DIM] = rotated(keys, cosine, sine).astype(BF16)
         grad_ref[:, at + kv_width : at + kv_width + HEAD_DIM] = values.astype(BF16)
+
+
+def unfold_kernel(whole_ref, first_ref, second_ref):
+    rank = first_ref.shape[0]
+    for piece in range(whole_ref.shape[0]):
+        columns = slice(piece * PAIR, (piece + 1) * PAIR)
+        first_ref[:, columns] = whole_ref[piece, :rank].astype(F32)
+        second_ref[:, columns] = whole_ref[piece, rank:].astype(F32)
 
 
 def exchange(table, axis):
@@ -283,9 +307,20 @@
     members = lax.axis_size("sub")
     half_index = lax.axis_index("half")
     group_index = half_index * members + lax.axis_index("sub")
-    low_local = jnp.dot(x_local, adapter_down, preferred_element_type=F32).astype(BF16)
-    low_wide = jnp.pad(low_local, ((0, 0), (0, HEAD_DIM - rank)))
-    packed_qkv = exchange(jnp.concatenate([qkv_local, low_wide], axis=1), "dp")
+    in_vmem = pl.BlockSpec(memory_space=pltpu.VMEM)
+    in_place = pl.BlockSpec(memory_space=pl.ANY)
+    wide = pl.pallas_call(
+        widen_kernel,
+        out_shape=jax.ShapeDtypeStruct((token_count, qkv_width + HEAD_DIM), BF16),
+        in_specs=[in_vmem, in_vmem, in_place],
+        out_specs=in_place,
+        scratch_shapes=[
+            pltpu.VMEM((token_count, HEAD_DIM), BF16),
+            pltpu.SemaphoreType.DMA((2,)),
+        ],
+        compiler_params=pltpu.CompilerParams(vmem_limit_bytes=VMEM_BYTES),
+    )(x_local, adapter_down.T, qkv_local)
+    packed_qkv = exchange(wide, "dp")
     packed_low = packed_qkv[:, qkv_width : qkv_width + rank]
 
     ends_dev = jnp.cumsum(width_row)
@@ -327,18 +362,24 @@
         out_shape=(
             jax.ShapeDtypeStruct((token_count, query_columns), BF16),
             jax.ShapeDtypeStruct((token_count, qkv_width), BF16),
-            jax.ShapeDtypeStruct((members, 2 * rank, PAIR), F32),
+            jax.ShapeDtypeStruct((members, 2 * rank, PAIR), BF16),
         ),
         compiler_params=params,
     )(came, packed_low, adapter_up, packed_inputs, cosine, sine)
-    total = jnp.sum(exchange(terms, "sub"), axis=0)
+    total = jnp.sum(exchange(terms, "sub").astype(F32), axis=0)
     for axis, apart in (("half", 1), ("dp", 1), ("dp", 2), ("dp", 4)):
         size = lax.axis_size(axis)
         total = total + lax.ppermute(total, axis, [(i, i ^ apart) for i in range(size)])
-    whole = exchange(jnp.broadcast_to(total.astype(BF16)[None], terms.shape), "sub").astype(F32)
-    grad_a = whole[:, :rank].transpose(0, 2, 1).reshape(model_width, rank)
-    grad_b = whole[:, rank:].transpose(1, 0, 2).reshape(rank, query_columns)
-    return (attn_rows[None], grad_rows[None], grad_a, grad_b)
+    whole = exchange(jnp.broadcast_to(total.astype(BF16)[None], terms.shape), "sub")
+    grad_a, grad_b = pl.pallas_call(
+        unfold_kernel,
+        out_shape=(
+            jax.ShapeDtypeStruct((rank, model_width), F32),
+            jax.ShapeDtypeStruct((rank, query_columns), F32),
+        ),
+        compiler_params=params,
+    )(whole)
+    return (attn_rows[None], grad_rows[None], grad_a.T, grad_b)
 
 
 def solution(mesh):

time: 245 us -> 241 us (0.984)
  Pallas kernels: 22.2 us -> 39 us
  starting transfers between devices: 44.4 us -> 29.9 us
  local copies, waits for them, and re-layouts: 8.67 us -> 5.3 us
  waiting for transfers between devices: 67.8 us -> 70.4 us
    pallas_call x1, Pallas kernels: 18.4 us -> 31.9 us  [attention(): pl.pallas_call(attention_kernel, out_shape=jax.ShapeDtypeStruct((rows, wi...]
    all_to_all x3, starting transfers between devices: 29.3 us -> 20.9 us  [exchange(): return lax.all_to_all(table, axis, split_axis=0, concat_axis=0, tiled=True)]
    ppermute x4, starting transfers between devices: 15.2 us -> 9.01 us  [local(): lax.ppermute(total, axis, [(i, i ^ apart) for i in range(size)])]
    pallas_call x0 -> x2, Pallas kernels: none -> 3.34 us  [the longest x1 2.52 us: local(): pl.pallas_call(widen_kernel, out_shape=jax.ShapeDtypeStruct((token_count,...]
    ppermute x4, waiting for transfers between devices: 5.78 us -> 8.72 us  [local(): lax.ppermute(total, axis, [(i, i ^ apart) for i in range(size)])]
    concatenate x1 -> x0, other arithmetic: 2.69 us -> none  [local(): packed_qkv = exchange(jnp.concatenate([qkv_local, low_wide], axis=1), 'dp')]
    unnamed x22 -> x18, local copies, waits for them, and re-layouts: 5.82 us -> 4.52 us
  transfers between devices with their start and end apart: 7 -> 7, of which waited for: 6 -> 6; matrix products, arithmetic and copies ran while one was open for 1% -> 1% of each run, Pallas kernels for 8% -> 13%
where the time goes in v3:
time: 241 us; the launch traced here: 240 us
  blocking collectives  91.2 us (38%)
  waiting for transfers between devices  70.4 us (29%)
  Pallas kernels  39 us (16%)
  starting transfers between devices  29.9 us (12%)
  local copies, waits for them, and re-layouts  5.3 us (2%)
  other arithmetic  2.68 us (1%)
    all_to_all x3, blocking collectives, exchange(): return lax.all_to_all(table, axis, split_axis=0, concat_axis=0, tiled=True)  91.2 us
    all_to_all x3, waiting for transfers between devices, exchange(): return lax.all_to_all(table, axis, split_axis=0, concat_axis=0, tiled=True)  61.7 us
    pallas_call x1, Pallas kernels, attention(): pl.pallas_call(attention_kernel, out_shape=jax.ShapeDtypeStruct((rows, wi...  31.9 us
    all_to_all x3, starting transfers between devices, exchange(): return lax.all_to_all(table, axis, split_axis=0, concat_axis=0, tiled=True)  20.9 us
    ppermute x4, starting transfers between devices, local(): lax.ppermute(total, axis, [(i, i ^ apart) for i in range(size)])  9.01 us
    ppermute x4, waiting for transfers between devices, local(): lax.ppermute(total, axis, [(i, i ^ apart) for i in range(size)])  8.72 us
  transfers between devices with their start and end apart: 7, of which 6 were waited for; matrix products, arithmetic and copies ran while one was open for 1% of the time, Pallas kernels for 13%

profile of v3, /device:TPU:1, one launch (start us, length us, event | category | flops | bytes accessed | tf_op | source)
XLA Modules:
  0.0 239.9 jit_solution(9312811538645094521)
XLA Ops:
  0.6 0.0 copy-start.3
  0.6 1.4 copy-done.3
  2.0 0.0 copy-start.6
  2.0 0.9 copy-done.6
  2.9 0.0 copy-start.8
  2.9 0.0 copy-start.7
  3.0 0.0 copy-start.4
  3.0 0.0 copy-start.5
  3.0 2.5 %shard_map.102 = bf16[128,6272]{1,0:T(8,128)(2,1)} custom-call(bf16[128,4096]{1,0:T(8,128)(2,1)} %bitcast.5.inputs_ref, bf16[16,4096]{1,0:T(8,128)(2,1)S(1)} %bitcast.36, bf16[128,6144]{1,0:T(8,128)(2,1)S(1)} %bitcast.34), custom_call_target="tpu_custom_call" | custom-call | tf_op jit(solution)/shard_map/pallas_call | solution.py:312
  5.5 11.7 %all-to-all-start = ((bf16[8,16,6272]{2,1,0:T(8,128)(2,1)}), bf16[8,16,6272]{2,1,0:T(8,128)(2,1)S(1)}, u32[]{:S(2)}, u32[]{:S(2)}) async-start(bf16[8,16,6272]{2,1,0:T(8,128)(2,1)} %bitcast.8), calls=%async_computation | async-start | bytes 3211264 | tf_op jit(solution)/shard_map/all_to_all | solution.py:293
  17.1 0.0 copy-done.8
  17.1 0.2 reduce-window.4
  17.3 0.0 copy-done.7
  17.3 0.6 select_reduce_fusion.2
  18.6 0.7 fusion.valid_ref
  19.3 0.3 fusion.1
  19.6 0.1 pad_maximum_fusion
  19.7 23.0 %all-to-all-done = bf16[8,16,6272]{2,1,0:T(8,128)(2,1)S(1)} async-done(((bf16[8,16,6272]{2,1,0:T(8,128)(2,1)}), bf16[8,16,6272]{2,1,0:T(8,128)(2,1)S(1)}, u32[]{:S(2)}, u32[]{:S(2)}) %all-to-all-start) | async-done | bytes 1605664 | tf_op jit(solution)/shard_map/all_to_all | solution.py:293
  42.8 0.0 copy-start
  42.8 0.0 copy-done.4
  42.8 0.0 copy-done.5
  42.8 1.0 shard_map.103
  43.8 58.4 %all_to_all.42 = bf16[16,128,768]{2,1,0:T(8,128)(2,1)} all-to-all(bf16[16,128,768]{2,1,0:T(8,128)(2,1)S(1)} %shard_map.103), channel_id=1, replica_groups=mesh['half'=2,'sub'=16,'dp'=8] {'sub'}, dimensions={0} | all-to-all | bytes 6291456 | tf_op jit(solution)/shard_map/all_to_all | solution.py:293
  102.1 0.0 copy-done
  102.1 4.3 %all-to-all-start.3 = ((bf16[8,16,4096]{2,1,0:T(8,128)(2,1)}), bf16[8,16,4096]{2,1,0:T(8,128)(2,1)S(1)}, u32[]{:S(2)}, u32[]{:S(2)}) async-start(bf16[8,16,4096]{2,1,0:T(8,128)(2,1)} %bitcast.13), calls=%async_computation.3 | async-start | bytes 2097152 | tf_op jit(solution)/shard_map/all_to_all | solution.py:293
  106.4 0.2 select_reduce_fusion
  106.6 0.5 fusion.3
  107.1 31.9 %shard_map.104 = bf16[2048,768]{1,0:T(8,128)(2,1)} custom-call(s32[8]{0:T(128)} %get-tuple-element.23.start_ref, s32[8]{0:T(128)} %get-tuple-element.22.end_ref, bf16[2048,768]{1,0:T(8,128)(2,1)} %bitcast.37), custom_call_target="tpu_custom_call" | custom-call | flops 8053063680 | bytes 6291456 | tf_op jit(solution)/shard_map/pallas_call | solution.py:218
  139.0 0.0 all-to-all-done.3
  139.0 0.0 copy-start.1
  139.0 1.0 copy-done.1
  140.0 5.0 %all-to-all-start.2 = ((bf16[16,128,768]{2,1,0:T(8,128)(2,1)}), bf16[16,128,768]{2,1,0:T(8,128)(2,1)S(1)}, u32[]{:S(2)}, u32[]{:S(2)}) async-start(bf16[16,128,768]{2,1,0:T(8,128)(2,1)} %bitcast.38), calls=%async_computation.2 | async-start | bytes 6291456 | tf_op jit(solution)/shard_map/all_to_all | solution.py:293
  145.0 0.8 slice.4.low_ref
  145.7 38.7 %all-to-all-done.2.came_ref = bf16[16,128,768]{2,1,0:T(8,128)(2,1)S(1)} async-done(((bf16[16,128,768]{2,1,0:T(8,128)(2,1)}), bf16[16,128,768]{2,1,0:T(8,128)(2,1)S(1)}, u32[]{:S(2)}, u32[]{:S(2)}) %all-to-all-start.2) | async-done | bytes 3145760 | tf_op jit(solution)/shard_map/all_to_all | solution.py:293
  184.4 0.0 copy-start.2
  184.4 1.2 copy-done.2
  185.6 2.8 %shard_map.105 = (bf16[128,4096]{1,0:T(8,128)(2,1)}, bf16[128,6144]{1,0:T(8,128)(2,1)}, bf16[16,32,256]{2,1,0:T(8,128)(2,1)S(1)}) custom-call(bf16[16,128,768]{2,1,0:T(8,128)(2,1)S(1)} %all-to-all-done.2.came_ref, bf16[128,16]{1,0:T(8,128)(2,1)S(1)} %slice.4.low_ref, bf16[16,4096]{1,0:T(8,128)(2,1)S(1)} %copy-done.5, bf16[128,4096]{1,0:T(8,128)(2,1)S(1)} %bitcast.33, ...), custom_call_target="tpu_custom_call" | custom-call | tf_op jit(solution)/shard_map/pallas_call | solution.py:360
  188.4 17.5 %all_to_all.43 = bf16[16,32,256]{2,1,0:T(8,128)(2,1)S(1)} all-to-all(bf16[16,32,256]{2,1,0:T(8,128)(2,1)S(1)} %get-tuple-element.15), channel_id=1, replica_groups=mesh['half'=2,'sub'=16,'dp'=8] {'sub'}, dimensions={0} | all-to-all | bytes 524288 | tf_op jit(solution)/shard_map/all_to_all | solution.py:293
  206.0 0.1 collective-permute-start
  206.1 3.7 %collective-permute-done = f32[32,256]{1,0:T(8,128)S(1)} collective-permute-done((f32[32,256]{1,0:T(8,128)S(1)}, f32[32,256]{1,0:T(8,128)S(1)}, u32[]{:S(2)}, u32[]{:S(2)}) %collective-permute-start) | collective-permute-done | bytes 32800 | tf_op jit(solution)/shard_map/ppermute | solution.py:372
  209.7 0.3 collective-permute-start.1
  210.0 2.5 %collective-permute-done.1 = f32[32,256]{1,0:T(8,128)S(1)} collective-permute-done((f32[32,256]{1,0:T(8,128)S(1)}, f32[32,256]{1,0:T(8,128)S(1)}, u32[]{:S(2)}, u32[]{:S(2)}) %collective-permute-start.1) | collective-permute-done | bytes 32800 | tf_op jit(solution)/shard_map/ppermute | solution.py:372
  212.5 3.2 %collective-permute-start.2 = (f32[32,256]{1,0:T(8,128)S(1)}, f32[32,256]{1,0:T(8,128)S(1)}, u32[]{:S(2)}, u32[]{:S(2)}) collective-permute-start(f32[32,256]{1,0:T(8,128)S(1)} %add.59), channel_id=1, source_target_pairs={{0,2},{1,3},{2,0},{3,1},{4,6},{5,7},{6,4},{7,5},{8,10},{9,11},{10,... | collective-permute-start | bytes 98312 | tf_op jit(solution)/shard_map/ppermute | solution.py:372
  215.7 1.3 collective-permute-done.2
  217.0 5.4 %collective-permute-start.3 = (f32[32,256]{1,0:T(8,128)S(1)}, f32[32,256]{1,0:T(8,128)S(1)}, u32[]{:S(2)}, u32[]{:S(2)}) collective-permute-start(f32[32,256]{1,0:T(8,128)S(1)} %add.60), channel_id=1, source_target_pairs={{0,4},{1,5},{2,6},{3,7},{4,0},{5,1},{6,2},{7,3},{8,12},{9,13},{10,... | collective-permute-start | bytes 98312 | tf_op jit(solution)/shard_map/ppermute | solution.py:372
  222.4 1.3 collective-permute-done.3
  223.8 15.3 %all_to_all.44.whole_ref = bf16[16,32,256]{2,1,0:T(8,128)(2,1)S(1)} all-to-all(bf16[16,32,256]{2,1,0:T(8,128)(2,1)S(1)} %broadcast_in_dim.52), channel_id=1, replica_groups=mesh['half'=2,'sub'=16,'dp'=8] {'sub'}, dimensions={0} | all-to-all | bytes 524288 | tf_op jit(solution)/shard_map/all_to_all | solution.py:293
  239.1 0.8 shard_map.106
  (9 shorter events, 0.1 us)
Async XLA Ops:
  0.6 1.4 copy-start.3
  2.0 0.9 copy-start.6
  2.9 14.2 %copy-start.8 = (s32[1,5]{1,0:T(1,128)S(1)}, s32[1,5]{1,0:T(1,128)}, u32[]{:S(2)}) copy-start(s32[1,5]{1,0:T(1,128)} %param.12) | copy-start | bytes 64
  2.9 14.4 %copy-start.7 = (s32[1,5]{1,0:T(1,128)S(1)}, s32[1,5]{1,0:T(1,128)}, u32[]{:S(2)}) copy-start(s32[1,5]{1,0:T(1,128)} %param.11) | copy-start | bytes 64
  3.0 39.8 %copy-start.4 = (bf16[1,128,4096]{2,1,0:T(8,128)(2,1)S(1)}, bf16[1,128,4096]{2,1,0:T(8,128)(2,1)}, u32[]{:S(2)}) copy-start(bf16[1,128,4096]{2,1,0:T(8,128)(2,1)} %param.13) | copy-start | bytes 3145732
  3.0 39.8 %copy-start.5 = (bf16[16,4096]{1,0:T(8,128)(2,1)S(1)}, bf16[16,4096]{1,0:T(8,128)(2,1)}, u32[]{:S(2)}) copy-start(bf16[16,4096]{1,0:T(8,128)(2,1)} %up_ref.3) | copy-start | bytes 393220
  5.5 37.3 %all-to-all-start = ((bf16[8,16,6272]{2,1,0:T(8,128)(2,1)}), bf16[8,16,6272]{2,1,0:T(8,128)(2,1)S(1)}, u32[]{:S(2)}, u32[]{:S(2)}) async-start(bf16[8,16,6272]{2,1,0:T(8,128)(2,1)} %bitcast.8), calls=%async_computation | async-start | bytes 3211264 | tf_op jit(solution)/shard_map/all_to_all | solution.py:293
  42.8 59.4 %copy-start = (bf16[8,16,6272]{2,1,0:T(8,128)(2,1)}, bf16[8,16,6272]{2,1,0:T(8,128)(2,1)S(1)}, u32[]{:S(2)}) copy-start(bf16[8,16,6272]{2,1,0:T(8,128)(2,1)S(1)} %all-to-all-done) | copy-start | bytes 4816900
  102.1 36.9 %all-to-all-start.3 = ((bf16[8,16,4096]{2,1,0:T(8,128)(2,1)}), bf16[8,16,4096]{2,1,0:T(8,128)(2,1)S(1)}, u32[]{:S(2)}, u32[]{:S(2)}) async-start(bf16[8,16,4096]{2,1,0:T(8,128)(2,1)} %bitcast.13), calls=%async_computation.3 | async-start | bytes 2097152 | tf_op jit(solution)/shard_map/all_to_all | solution.py:293
  139.0 1.0 copy-start.1
  140.0 44.4 %all-to-all-start.2 = ((bf16[16,128,768]{2,1,0:T(8,128)(2,1)}), bf16[16,128,768]{2,1,0:T(8,128)(2,1)S(1)}, u32[]{:S(2)}, u32[]{:S(2)}) async-start(bf16[16,128,768]{2,1,0:T(8,128)(2,1)} %bitcast.38), calls=%async_computation.2 | async-start | bytes 6291456 | tf_op jit(solution)/shard_map/all_to_all | solution.py:293
  184.4 1.2 copy-start.2
  206.0 3.8 %collective-permute-start = (f32[32,256]{1,0:T(8,128)S(1)}, f32[32,256]{1,0:T(8,128)S(1)}, u32[]{:S(2)}, u32[]{:S(2)}) collective-permute-start(f32[32,256]{1,0:T(8,128)S(1)} %convert_reduce_fusion), channel_id=1, source_target_pairs={{0,128},{128,0},{1,129},{129,1},{2,130},{130,2},{3,131},{131,3},{4... | collective-permute-start | bytes 98312 | tf_op jit(solution)/shard_map/ppermute | solution.py:372
  209.7 2.8 %collective-permute-start.1 = (f32[32,256]{1,0:T(8,128)S(1)}, f32[32,256]{1,0:T(8,128)S(1)}, u32[]{:S(2)}, u32[]{:S(2)}) collective-permute-start(f32[32,256]{1,0:T(8,128)S(1)} %add.58), channel_id=1, source_target_pairs={{0,1},{1,0},{2,3},{3,2},{4,5},{5,4},{6,7},{7,6},{8,9},{9,8},{10,11... | collective-permute-start | bytes 98312 | tf_op jit(solution)/shard_map/ppermute | solution.py:372
  212.5 4.5 %collective-permute-start.2 = (f32[32,256]{1,0:T(8,128)S(1)}, f32[32,256]{1,0:T(8,128)S(1)}, u32[]{:S(2)}, u32[]{:S(2)}) collective-permute-start(f32[32,256]{1,0:T(8,128)S(1)} %add.59), channel_id=1, source_target_pairs={{0,2},{1,3},{2,0},{3,1},{4,6},{5,7},{6,4},{7,5},{8,10},{9,11},{10,... | collective-permute-start | bytes 98312 | tf_op jit(solution)/shard_map/ppermute | solution.py:372
  217.0 6.7 %collective-permute-start.3 = (f32[32,256]{1,0:T(8,128)S(1)}, f32[32,256]{1,0:T(8,128)S(1)}, u32[]{:S(2)}, u32[]{:S(2)}) collective-permute-start(f32[32,256]{1,0:T(8,128)S(1)} %add.60), channel_id=1, source_target_pairs={{0,4},{1,5},{2,6},{3,7},{4,0},{5,1},{6,2},{7,3},{8,12},{9,13},{10,... | collective-permute-start | bytes 98312 | tf_op jit(solution)/shard_map/ppermute | solution.py:372

commit v4 on v3

--- a/solution.py
+++ b/solution.py
@@ -18,6 +18,7 @@
 VMEM_BYTES = 48 * 1024 * 1024
 ATTENTION_VMEM_BYTES = 60 * 1024 * 1024
 HIDDEN = -1e30
+CHUNKS = 4
 F32 = jnp.float32
 BF16 = jnp.bfloat16
 
@@ -34,16 +35,30 @@
     return table * cosine + pltpu.roll(table, HALF_DIM, 1) * sine
 
 
-def widen_kernel(inputs_ref, down_ref, qkv_ref, out_ref, slab, sems):
+def widen_kernel(inputs_ref, down_ref, qkv_ref, out_ref, inputs, down, slab, sems):
     width = qkv_ref.shape[1]
-    move = pltpu.make_async_copy(qkv_ref, out_ref.at[:, :width], sems.at[0])
+    chunk = inputs.shape[1] // CHUNKS
+    parts = [slice(part * chunk, (part + 1) * chunk) for part in range(CHUNKS)]
+    loads = [
+        pltpu.make_async_copy(inputs_ref.at[:, part], inputs.at[:, part], sems.at[index])
+        for index, part in enumerate(parts)
+    ]
+    load_down = pltpu.make_async_copy(down_ref, down, sems.at[CHUNKS])
+    move = pltpu.make_async_copy(qkv_ref, out_ref.at[:, :width], sems.at[CHUNKS + 1])
+    load_down.start()
+    for load in loads:
+        load.start()
     move.start()
-    low = lax.dot_general(
-        inputs_ref[...], down_ref[...], (((1,), (1,)), ((), ())), preferred_element_type=F32
-    )
+    low = jnp.zeros((inputs.shape[0], down.shape[0]), F32)
     slab[...] = jnp.zeros_like(slab)
+    load_down.wait()
+    for load, part in zip(loads, parts):
+        load.wait()
+        low += lax.dot_general(
+            inputs[:, part], down[:, part], (((1,), (1,)), ((), ())), preferred_element_type=F32
+        )
     slab[:, : low.shape[1]] = low.astype(BF16)
-    add = pltpu.make_async_copy(slab, out_ref.at[:, width:], sems.at[1])
+    add = pltpu.make_async_copy(slab, out_ref.at[:, width:], sems.at[CHUNKS + 2])
     add.start()
     move.wait()
     add.wait()
@@ -77,61 +92,63 @@
             out_ref[piece, :, 2 * PAIR + HEAD_DIM :] = values
 
 
-def attention_kernel(start_ref, end_ref, x_ref, out_ref, kt, vt, dkt, dvt, store0, store1):
+def attention_kernel(
+    start_ref, end_ref, q_ref, g_ref, kv_ref, out_ref, kt, vt, dkt, dvt, store0, store1, held, tail, sems
+):
     store = (store0, store1)
     step = pl.program_id(0)
-    blocks = pl.num_programs(0)
+    blocks = held.shape[0]
     factor = 1.0 / math.sqrt(HEAD_DIM)
     exponent = factor * math.log2(math.e)
-    key_at = 2 * PAIR
-    value_at = 2 * PAIR + HEAD_DIM
-    tiles = x_ref.shape[0] // BLOCK
-    per = BLOCK // PART
+    parts = BLOCK // PART
 
     @pl.when(step == 0)
     def _():
-        for tile in range(tiles):
+        for tile in range(blocks):
             rows = slice(tile * BLOCK, (tile + 1) * BLOCK)
-            kt[tile] = x_ref[rows, key_at:value_at].T
-            vt[tile] = x_ref[rows, value_at:].T
+            kt[tile] = kv_ref[rows, :HEAD_DIM].T
+            vt[tile] = kv_ref[rows, HEAD_DIM:].T
         dkt[...] = jnp.zeros_like(dkt)
         dvt[...] = jnp.zeros_like(dvt)
 
-    own = pl.ds(pl.multiple_of(step * BLOCK, BLOCK), BLOCK)
-    first = start_ref[step * per] // BLOCK
-    last = step
-    end_row = end_ref[step * per]
+    first = start_ref[step * parts] // BLOCK
+    end_row = end_ref[step * parts]
+    own = pl.multiple_of(step * BLOCK, BLOCK)
     column = lax.broadcasted_iota(jnp.int32, (1, BLOCK), 1)
-    row = lax.broadcasted_iota(jnp.int32, (BLOCK, 1), 0)
-    low_row = jnp.full((BLOCK, 1), start_ref[step * per] - last * BLOCK, jnp.int32)
-    high_row = jnp.full((BLOCK, 1), end_row - last * BLOCK, jnp.int32)
-    for part in range(1, per):
-        inside = row >= part * PART
-        low_row = jnp.where(inside, start_ref[step * per + part] - last * BLOCK, low_row)
-        high_row = jnp.where(inside, end_ref[step * per + part] - last * BLOCK, high_row)
-    queries = [x_ref[own, h * HEAD_DIM : (h + 1) * HEAD_DIM] for h in range(2)]
-    grads = [x_ref[own, PAIR + h * HEAD_DIM : PAIR + (h + 1) * HEAD_DIM] for h in range(2)]
+    queries = [q_ref[:, h * HEAD_DIM : (h + 1) * HEAD_DIM] for h in range(2)]
+    grads = [g_ref[:, h * HEAD_DIM : (h + 1) * HEAD_DIM] for h in range(2)]
+    corners = [(slice(p * PART, (p + 1) * PART), (p + 1) * PART) for p in range(parts)]
 
     def folded(op, table):
-        parts = [table[:, c : c + HEAD_DIM] for c in range(0, BLOCK, HEAD_DIM)]
-        while len(parts) > 1:
-            parts = [op(a, b) for a, b in zip(parts[::2], parts[1::2])]
-        return parts[0]
-
-    def spread(table):
-        return jnp.concatenate([table] * (BLOCK // HEAD_DIM), axis=1)
+        pieces = [table[:, c : c + HEAD_DIM] for c in range(0, table.shape[1], HEAD_DIM)]
+        while len(pieces) > 1:
+            pieces = [op(a, b) for a, b in zip(pieces[::2], pieces[1::2])]
+        return pieces[0]
+
+    def spread(table, width):
+        return jnp.concatenate([table] * (width // HEAD_DIM), axis=1)
 
     def key_rows(tile):
         return pl.ds(pl.multiple_of(tile * BLOCK, BLOCK), BLOCK)
 
-    diagonal = (column == row) | ((column < row) & (column >= low_row) & (column < high_row))
+    def corner_allowed(p, width):
+        low = start_ref[step * parts + p] - own
+        high = end_ref[step * parts + p] - own
+        row = lax.broadcasted_iota(jnp.int32, (PART, 1), 0) + p * PART
+        at = column[:, :width]
+        return (at == row) | ((at < row) & (at >= low) & (at < high))
+
+    allowed = [corner_allowed(p, width) for p, (_, width) in enumerate(corners)]
     carry = []
     for h in range(2):
-        scores = jnp.dot(queries[h], kt[last], preferred_element_type=F32) * exponent
-        scores = jnp.where(diagonal, scores, HIDDEN)
-        store[h][last] = scores
-        top = folded(jnp.maximum, scores)
-        carry += [top, folded(jnp.add, jnp.exp2(scores - spread(top)))]
+        highs, sums = [], []
+        for p, (rows, width) in enumerate(corners):
+            scores = jnp.dot(queries[h][rows], kt[step, :, :width], preferred_element_type=F32)
+            scores = jnp.where(allowed[p], scores * exponent, HIDDEN)
+            store[h][step, rows, :width] = scores
+            highs.append(folded(jnp.maximum, scores))
+            sums.append(folded(jnp.add, jnp.exp2(scores - spread(highs[-1], width))))
+        carry += [jnp.concatenate(highs, axis=0), jnp.concatenate(sums, axis=0)]
 
     def score_pass(tile, carry):
         bias = jnp.where(tile * BLOCK + column < end_row, F32(0.0), F32(HIDDEN))
@@ -142,12 +159,12 @@
             store[h][tile] = scores
             higher = jnp.maximum(top, folded(jnp.maximum, scores))
             total = total * jnp.exp2(top - higher) + folded(
-                jnp.add, jnp.exp2(scores - spread(higher))
+                jnp.add, jnp.exp2(scores - spread(higher, BLOCK))
             )
             result += [higher, total]
         return tuple(result)
 
-    carry = lax.fori_loop(first, last, score_pass, tuple(carry))
+    carry = lax.fori_loop(first, step, score_pass, tuple(carry))
     tops, inverse = [], []
     for h in range(2):
         lane_top, lane_total = carry[2 * h], carry[2 * h + 1]
@@ -156,59 +173,97 @@
         tops.append(top)
         inverse.append(1.0 / total)
 
-    empty = jnp.zeros((BLOCK, HEAD_DIM), F32)
+    def corner_probs(h, rows, width):
+        return jnp.exp2(store[h][step, rows, :width] - tops[h][rows]) * inverse[h][rows]
 
     def probs_of(h, tile):
         return jnp.exp2(store[h][tile] - tops[h]) * inverse[h]
 
-    def out_part(h, tile, total):
-        values = x_ref[key_rows(tile), value_at:]
-        return total + jnp.dot(
-            probs_of(h, tile).astype(BF16), values, preferred_element_type=F32
-        )
-
-    outs = [None, None]
-    deltas = [None, None]
+    own_rows = key_rows(step)
+    keys, values = kv_ref[own_rows, :HEAD_DIM], kv_ref[own_rows, HEAD_DIM:]
+    sums = []
+    for h in range(2):
+        sums.append(
+            jnp.concatenate(
+                [
+                    jnp.dot(
+                        corner_probs(h, rows, width).astype(BF16),
+                        values[:width],
+                        preferred_element_type=F32,
+                    )
+                    for rows, width in corners
+                ],
+                axis=0,
+            )
+        )
+
+    def out_pass(tile, carry):
+        values = kv_ref[key_rows(tile), HEAD_DIM:]
+        return tuple(
+            carry[h]
+            + jnp.dot(probs_of(h, tile).astype(BF16), values, preferred_element_type=F32)
+            for h in range(2)
+        )
+
+    sums = lax.fori_loop(first, step, out_pass, tuple(sums))
+    outs = [total.astype(BF16) for total in sums]
+    deltas = [
+        jnp.sum(grads[h].astype(F32) * outs[h].astype(F32), axis=1, keepdims=True) for h in range(2)
+    ]
     queries_t = [table.T for table in queries]
     grads_t = [table.T for table in grads]
 
-    def settle(h, total):
-        outs[h] = total.astype(BF16)
-        deltas[h] = jnp.sum(
-            grads[h].astype(F32) * outs[h].astype(F32), axis=1, keepdims=True
-        )
-
-    def grad_part(h, tile, total):
-        keys = x_ref[key_rows(tile), key_at:value_at]
-        grad_probs = jnp.dot(grads[h], vt[tile], preferred_element_type=F32)
-        probs = probs_of(h, tile)
-        grad_scores = (probs * (grad_probs - deltas[h])).astype(BF16)
-        total = total + jnp.dot(grad_scores, keys, preferred_element_type=F32)
-        dkt[tile] += jnp.dot(queries_t[h], grad_scores, preferred_element_type=F32)
-        dvt[tile] += jnp.dot(grads_t[h], probs.astype(BF16), preferred_element_type=F32)
-        return total
-
-    def out_pass(tile, carry):
-        return tuple(out_part(h, tile, carry[h]) for h in range(2))
+    query_sums = []
+    for h in range(2):
+        found = []
+        for rows, width in corners:
+            grad_probs = jnp.dot(grads[h][rows], vt[step, :, :width], preferred_element_type=F32)
+            probs = corner_probs(h, rows, width)
+            grad_scores = (probs * (grad_probs - deltas[h][rows])).astype(BF16)
+            found.append(jnp.dot(grad_scores, keys[:width], preferred_element_type=F32))
+            dkt[step, :, :width] += jnp.dot(
+                queries_t[h][:, rows], grad_scores, preferred_element_type=F32
+            )
+            dvt[step, :, :width] += jnp.dot(
+                grads_t[h][:, rows], probs.astype(BF16), preferred_element_type=F32
+            )
+        query_sums.append(jnp.concatenate(found, axis=0))
 
     def gradient_pass(tile, carry):
-        return tuple(grad_part(h, tile, carry[h]) for h in range(2))
-
-    sums = lax.fori_loop(first, last + 1, out_pass, (empty, empty))
-    for h in range(2):
-        settle(h, sums[h])
-    query_sums = lax.fori_loop(first, last + 1, gradient_pass, (empty, empty))
+        keys = kv_ref[key_rows(tile), :HEAD_DIM]
+        result = []
+        for h in range(2):
+            grad_probs = jnp.dot(grads[h], vt[tile], preferred_element_type=F32)
+            probs = probs_of(h, tile)
+            grad_scores = (probs * (grad_probs - deltas[h])).astype(BF16)
+            result.append(carry[h] + jnp.dot(grad_scores, keys, preferred_element_type=F32))
+            dkt[tile] += jnp.dot(queries_t[h], grad_scores, preferred_element_type=F32)
+            dvt[tile] += jnp.dot(grads_t[h], probs.astype(BF16), preferred_element_type=F32)
+        return tuple(result)
+
+    query_sums = lax.fori_loop(first, step, gradient_pass, tuple(query_sums))
     for h in range(2):
         at = h * HEAD_DIM
-        out_ref[own, at : at + HEAD_DIM] = outs[h]
-        out_ref[own, PAIR + at : PAIR + at + HEAD_DIM] = (query_sums[h] * factor).astype(BF16)
+        held[step, :, at : at + HEAD_DIM] = outs[h]
+        held[step, :, PAIR + at : PAIR + at + HEAD_DIM] = (query_sums[h] * factor).astype(BF16)
+
+    def block_copy(block):
+        rows = pl.ds(pl.multiple_of(block * BLOCK, BLOCK), BLOCK)
+        return pltpu.make_async_copy(held.at[block], out_ref.at[rows, : 2 * PAIR], sems.at[block])
+
+    block_copy(step).start()
 
     @pl.when(step == blocks - 1)
     def _():
-        for tile in range(tiles):
+        for tile in range(blocks):
             rows = slice(tile * BLOCK, (tile + 1) * BLOCK)
-            out_ref[rows, key_at:value_at] = (dkt[tile] * factor).T.astype(BF16)
-            out_ref[rows, value_at:] = dvt[tile].T.astype(BF16)
+            tail[rows, :HEAD_DIM] = (dkt[tile] * factor).T.astype(BF16)
+            tail[rows, HEAD_DIM:] = dvt[tile].T.astype(BF16)
+        last = pltpu.make_async_copy(tail, out_ref.at[:, 2 * PAIR :], sems.at[blocks])
+        last.start()
+        for block in range(blocks):
+            block_copy(block).wait()
+        last.wait()
 
 
 def attention(table, starts, ends):
@@ -221,8 +276,12 @@
         grid_spec=pltpu.PrefetchScalarGridSpec(
             num_scalar_prefetch=2,
             grid=(blocks,),
-            in_specs=[pl.BlockSpec((rows, width), lambda i, *_: (0, 0))],
-            out_specs=pl.BlockSpec((rows, width), lambda i, *_: (0, 0)),
+            in_specs=[
+                pl.BlockSpec((BLOCK, PAIR), lambda i, *_: (i, 0)),
+                pl.BlockSpec((BLOCK, PAIR), lambda i, *_: (i, 1)),
+                pl.BlockSpec((rows, PAIR), lambda i, *_: (0, 2)),
+            ],
+            out_specs=pl.BlockSpec(memory_space=pl.ANY),
             scratch_shapes=[
                 pltpu.VMEM((blocks, HEAD_DIM, BLOCK), BF16),
                 pltpu.VMEM((blocks, HEAD_DIM, BLOCK), BF16),
@@ -230,6 +289,9 @@
                 pltpu.VMEM((blocks, HEAD_DIM, BLOCK), F32),
                 pltpu.VMEM((blocks, BLOCK, BLOCK), F32),
                 pltpu.VMEM((blocks, BLOCK, BLOCK), F32),
+                pltpu.VMEM((blocks, BLOCK, 2 * PAIR), BF16),
+                pltpu.VMEM((rows, PAIR), BF16),
+                pltpu.SemaphoreType.DMA((blocks + 1,)),
             ],
         ),
         compiler_params=pltpu.CompilerParams(vmem_limit_bytes=ATTENTION_VMEM_BYTES),
@@ -238,21 +300,21 @@
             bytes_accessed=4 * rows * width,
             transcendentals=tiles * 2 * BLOCK * BLOCK,
         ),
-    )(starts, ends, table)
-
-
-def finish_kernel(
-    came_ref, low_ref, up_ref, inputs_ref, cos_ref, sin_ref, out_ref, grad_ref, term_ref
+    )(starts, ends, table, table, table)
+
+
+def query_kernel(
+    came_ref, low_ref, up_ref, inputs_ref, cos_ref, sin_ref, grad_ref, term_ref, inputs, sem
 ):
+    load = pltpu.make_async_copy(inputs_ref, inputs, sem)
+    load.start()
     cosine = cos_ref[...]
     sine = -sin_ref[...]
-    rank, queries = up_ref.shape
+    rank = up_ref.shape[0]
     low_t = low_ref[...].astype(F32).T.astype(BF16)
-    kv_width = (grad_ref.shape[1] - queries) // 2
     dlow = jnp.zeros(low_ref.shape, F32)
     for piece in range(came_ref.shape[0]):
         columns = slice(piece * PAIR, (piece + 1) * PAIR)
-        out_ref[:, columns] = came_ref[piece, :, :PAIR]
         for head in range(2):
             at = PAIR + head * HEAD_DIM
             to = piece * PAIR + head * HEAD_DIM
@@ -265,11 +327,22 @@
         )
         term_ref[piece, rank:] = jnp.dot(low_t, part, preferred_element_type=F32).astype(BF16)
     dlow_t = dlow.astype(BF16).astype(F32).T.astype(BF16)
+    load.wait()
     for piece in range(came_ref.shape[0]):
         columns = slice(piece * PAIR, (piece + 1) * PAIR)
         term_ref[piece, :rank] = jnp.dot(
-            dlow_t, inputs_ref[:, columns], preferred_element_type=F32
+            dlow_t, inputs[:, columns], preferred_element_type=F32
         ).astype(BF16)
+
+
+def finish_kernel(came_ref, query_ref, cos_ref, sin_ref, out_ref, grad_ref):
+    cosine = cos_ref[...]
+    sine = -sin_ref[...]
+    queries = query_ref.shape[1]
+    kv_width = (grad_ref.shape[1] - queries) // 2
+    grad_ref[:, :queries] = query_ref[...]
+    for piece in range(came_ref.shape[0]):
+        out_ref[:, piece * PAIR : (piece + 1) * PAIR] = came_ref[piece, :, :PAIR]
     for key_head in range(kv_width // HEAD_DIM):
         pair = (2 * key_head, 2 * key_head + 1)
         keys, values = (
@@ -312,11 +385,13 @@
     wide = pl.pallas_call(
         widen_kernel,
         out_shape=jax.ShapeDtypeStruct((token_count, qkv_width + HEAD_DIM), BF16),
-        in_specs=[in_vmem, in_vmem, in_place],
+        in_specs=[in_place, in_place, in_place],
         out_specs=in_place,
         scratch_shapes=[
+            pltpu.VMEM((token_count, model_width), BF16),
+            pltpu.VMEM((rank, model_width), BF16),
             pltpu.VMEM((token_count, HEAD_DIM), BF16),
-            pltpu.SemaphoreType.DMA((2,)),
+            pltpu.SemaphoreType.DMA((CHUNKS + 3,)),
         ],
         compiler_params=pltpu.CompilerParams(vmem_limit_bytes=VMEM_BYTES),
     )(x_local, adapter_down.T, qkv_local)
@@ -357,15 +432,32 @@
     packed_inputs = exchange(x_held, "dp")
     results = attention(table, starts, ends)
     came = exchange(results.reshape(members, token_count, PIECE), "sub")
-    attn_rows, grad_rows, terms = pl.pallas_call(
+    query_gradient, terms = pl.pallas_call(
+        query_kernel,
+        out_shape=(
+            jax.ShapeDtypeStruct((token_count, query_columns), BF16),
+            jax.ShapeDtypeStruct((members, 2 * rank, PAIR), BF16),
+        ),
+        in_specs=[in_vmem, in_vmem, in_vmem, in_place, in_vmem, in_vmem],
+        scratch_shapes=[
+            pltpu.VMEM((token_count, model_width), BF16),
+            pltpu.SemaphoreType.DMA(()),
+        ],
+        compiler_params=params,
+    )(came, packed_low, adapter_up, packed_inputs, cosine, sine)
+    attn_rows, grad_rows = pl.pallas_call(
         finish_kernel,
         out_shape=(
             jax.ShapeDtypeStruct((token_count, query_columns), BF16),
             jax.ShapeDtypeStruct((token_count, qkv_width), BF16),
-            jax.ShapeDtypeStruct((members, 2 * rank, PAIR), BF16),
         ),
         compiler_params=params,
-    )(came, packed_low, adapter_up, packed_inputs, cosine, sine)
+        cost_estimate=pl.CostEstimate(
+            flops=token_count * qkv_width,
+            bytes_accessed=8 * token_count * qkv_width,
+            transcendentals=0,
+        ),
+    )(came, query_gradient, cosine, sine)
     total = jnp.sum(exchange(terms, "sub").astype(F32), axis=0)
     for axis, apart in (("half", 1), ("dp", 1), ("dp", 2), ("dp", 4)):
         size = lax.axis_size(axis)

time: 241 us -> 240 us (level)
  blocking collectives: 91.2 us -> 75.8 us
  starting transfers between devices: 29.9 us -> 37.2 us
  waiting for transfers between devices: 70.4 us -> 76.4 us
  local copies, waits for them, and re-layouts: 5.3 us -> 8.19 us
    all_to_all x3 -> x2, blocking collectives: 91.2 us -> 75.8 us  [exchange(): return lax.all_to_all(table, axis, split_axis=0, concat_axis=0, tiled=True)]
    all_to_all x3 -> x4, starting transfers between devices: 20.9 us -> 30.1 us  [exchange(): return lax.all_to_all(table, axis, split_axis=0, concat_axis=0, tiled=True)]
    all_to_all x3 -> x4, waiting for transfers between devices: 61.7 us -> 66 us  [exchange(): return lax.all_to_all(table, axis, split_axis=0, concat_axis=0, tiled=True)]
    pallas_call x1, Pallas kernels: 31.9 us -> 29.4 us  [attention(): pl.pallas_call(attention_kernel, out_shape=jax.ShapeDtypeStruct((rows, wi...]
    unnamed x18 -> x22, local copies, waits for them, and re-layouts: 4.52 us -> 6.7 us
  transfers between devices with their start and end apart: 7 -> 8, of which waited for: 6 -> 7; matrix products, arithmetic and copies ran while one was open for 1% -> 1% of each run, Pallas kernels for 13% -> 13%
where the time goes in v4:
time: 240 us; the launch traced here: 239 us
  waiting for transfers between devices  76.4 us (32%)
  blocking collectives  75.8 us (32%)
  Pallas kernels  37.7 us (16%)
  starting transfers between devices  37.2 us (16%)
  local copies, waits for them, and re-layouts  8.19 us (3%)
  other arithmetic  2.68 us (1%)
    all_to_all x2, blocking collectives, exchange(): return lax.all_to_all(table, axis, split_axis=0, concat_axis=0, tiled=True)  75.8 us
    all_to_all x4, waiting for transfers between devices, exchange(): return lax.all_to_all(table, axis, split_axis=0, concat_axis=0, tiled=True)  66 us
    all_to_all x4, starting transfers between devices, exchange(): return lax.all_to_all(table, axis, split_axis=0, concat_axis=0, tiled=True)  30.1 us
    pallas_call x1, Pallas kernels, attention(): pl.pallas_call(attention_kernel, out_shape=jax.ShapeDtypeStruct((rows, wi...  29.4 us
    ppermute x4, waiting for transfers between devices, local(): lax.ppermute(total, axis, [(i, i ^ apart) for i in range(size)])  10.4 us
    ppermute x4, starting transfers between devices, local(): lax.ppermute(total, axis, [(i, i ^ apart) for i in range(size)])  7.1 us
    unnamed x22, local copies, waits for them, and re-layouts  6.7 us
  transfers between devices with their start and end apart: 8, of which 7 were waited for; matrix products, arithmetic and copies ran while one was open for 1% of the time, Pallas kernels for 13%

profile of v4, /device:TPU:1, one launch (start us, length us, event | category | flops | bytes accessed | tf_op | source)
XLA Modules:
  0.0 239.3 jit_solution(3975039505521071027)
XLA Ops:
  0.6 0.0 copy-start.3
  0.6 1.4 copy-done.3
  2.0 0.0 copy-start.8
  2.0 0.9 copy-done.8
  3.0 3.3 %shard_map.102 = bf16[128,6272]{1,0:T(8,128)(2,1)} custom-call(bf16[128,4096]{1,0:T(8,128)(2,1)} %bitcast.5.inputs_ref, bf16[16,4096]{1,0:T(8,128)(2,1)S(1)} %bitcast.36, bf16[128,6144]{1,0:T(8,128)(2,1)S(1)} %bitcast.34), custom_call_target="tpu_custom_call" | custom-call | tf_op jit(solution)/shard_map/pallas_call | solution.py:385
  6.3 11.7 %all-to-all-start = ((bf16[8,16,6272]{2,1,0:T(8,128)(2,1)}), bf16[8,16,6272]{2,1,0:T(8,128)(2,1)S(1)}, u32[]{:S(2)}, u32[]{:S(2)}) async-start(bf16[8,16,6272]{2,1,0:T(8,128)(2,1)} %bitcast.8), calls=%async_computation | async-start | bytes 3211264 | tf_op jit(solution)/shard_map/all_to_all | solution.py:366
  18.0 0.0 copy-done.10
  18.0 0.2 reduce-window.4
  18.1 0.0 copy-done.9
  18.1 0.6 select_reduce_fusion.2
  19.5 0.7 fusion.valid_ref
  20.1 0.3 fusion.1
  20.4 0.1 pad_maximum_fusion
  20.5 23.0 %all-to-all-done = bf16[8,16,6272]{2,1,0:T(8,128)(2,1)S(1)} async-done(((bf16[8,16,6272]{2,1,0:T(8,128)(2,1)}), bf16[8,16,6272]{2,1,0:T(8,128)(2,1)S(1)}, u32[]{:S(2)}, u32[]{:S(2)}) %all-to-all-start) | async-done | bytes 1605664 | tf_op jit(solution)/shard_map/all_to_all | solution.py:366
  43.6 0.0 copy-done.4
  43.6 0.0 copy-done.7
  43.6 1.0 shard_map.103
  44.6 58.3 %all_to_all.42 = bf16[16,128,768]{2,1,0:T(8,128)(2,1)} all-to-all(bf16[16,128,768]{2,1,0:T(8,128)(2,1)S(1)} %shard_map.103), channel_id=1, replica_groups=mesh['half'=2,'sub'=16,'dp'=8] {'sub'}, dimensions={0} | all-to-all | bytes 6291456 | tf_op jit(solution)/shard_map/all_to_all | solution.py:366
  102.9 0.0 copy-done
  102.9 4.2 %all-to-all-start.3 = ((bf16[8,16,4096]{2,1,0:T(8,128)(2,1)}), bf16[8,16,4096]{2,1,0:T(8,128)(2,1)S(1)}, u32[]{:S(2)}, u32[]{:S(2)}) async-start(bf16[8,16,4096]{2,1,0:T(8,128)(2,1)} %bitcast.13), calls=%async_computation.3 | async-start | bytes 2097152 | tf_op jit(solution)/shard_map/all_to_all | solution.py:366
  107.2 0.2 select_reduce_fusion
  107.3 0.5 fusion.3
  107.9 29.4 %shard_map.104 = bf16[2048,768]{1,0:T(8,128)(2,1)} custom-call(s32[8]{0:T(128)} %get-tuple-element.25.start_ref, s32[8]{0:T(128)} %get-tuple-element.24.end_ref, bf16[2048,768]{1,0:T(8,128)(2,1)} %bitcast.37, bf16[2048,768]{1,0:T(8,128)(2,1)} %bitcast.38, bf16[2048,768]{1,0:T(8,128)(2,1)} %bitcast.39), custom_call_target="tpu_custom_call" | custom-call | flops 8053063680 | bytes 6291456 | tf_op jit(solution)/shard_map/pallas_call | solution.py:273
  137.2 0.0 all-to-all-done.3
  137.2 0.0 copy-start.1
  137.3 1.0 copy-done.1
  138.2 5.0 %all-to-all-start.2 = ((bf16[16,128,768]{2,1,0:T(8,128)(2,1)}), bf16[16,128,768]{2,1,0:T(8,128)(2,1)S(1)}, u32[]{:S(2)}, u32[]{:S(2)}) async-start(bf16[16,128,768]{2,1,0:T(8,128)(2,1)} %bitcast.40), calls=%async_computation.2 | async-start | bytes 6291456 | tf_op jit(solution)/shard_map/all_to_all | solution.py:366
  143.2 0.8 slice.4.low_ref
  143.9 38.7 %all-to-all-done.2.came_ref = bf16[16,128,768]{2,1,0:T(8,128)(2,1)S(1)} async-done(((bf16[16,128,768]{2,1,0:T(8,128)(2,1)}), bf16[16,128,768]{2,1,0:T(8,128)(2,1)S(1)}, u32[]{:S(2)}, u32[]{:S(2)}) %all-to-all-start.2) | async-done | bytes 3145760 | tf_op jit(solution)/shard_map/all_to_all | solution.py:366
  182.6 1.2 copy-done.2
  183.9 1.4 shard_map.105
  185.3 0.0 copy-start.5
  185.3 1.0 copy-done.5
  186.3 17.5 %all_to_all.43 = bf16[16,32,256]{2,1,0:T(8,128)(2,1)S(1)} all-to-all(bf16[16,32,256]{2,1,0:T(8,128)(2,1)S(1)} %get-tuple-element.17), channel_id=1, replica_groups=mesh['half'=2,'sub'=16,'dp'=8] {'sub'}, dimensions={0} | all-to-all | bytes 524288 | tf_op jit(solution)/shard_map/all_to_all | solution.py:366
  203.8 0.1 collective-permute-start
  203.9 3.7 %collective-permute-done = f32[32,256]{1,0:T(8,128)S(1)} collective-permute-done((f32[32,256]{1,0:T(8,128)S(1)}, f32[32,256]{1,0:T(8,128)S(1)}, u32[]{:S(2)}, u32[]{:S(2)}) %collective-permute-start) | collective-permute-done | bytes 32800 | tf_op jit(solution)/shard_map/ppermute | solution.py:464
  207.5 0.4 collective-permute-start.1
  207.9 2.4 %collective-permute-done.1 = f32[32,256]{1,0:T(8,128)S(1)} collective-permute-done((f32[32,256]{1,0:T(8,128)S(1)}, f32[32,256]{1,0:T(8,128)S(1)}, u32[]{:S(2)}, u32[]{:S(2)}) %collective-permute-start.1) | collective-permute-done | bytes 32800 | tf_op jit(solution)/shard_map/ppermute | solution.py:464
  210.3 1.9 collective-permute-start.2
  212.2 2.4 %collective-permute-done.2 = f32[32,256]{1,0:T(8,128)S(1)} collective-permute-done((f32[32,256]{1,0:T(8,128)S(1)}, f32[32,256]{1,0:T(8,128)S(1)}, u32[]{:S(2)}, u32[]{:S(2)}) %collective-permute-start.2) | collective-permute-done | bytes 32800 | tf_op jit(solution)/shard_map/ppermute | solution.py:464
  214.6 4.8 %collective-permute-start.3 = (f32[32,256]{1,0:T(8,128)S(1)}, f32[32,256]{1,0:T(8,128)S(1)}, u32[]{:S(2)}, u32[]{:S(2)}) collective-permute-start(f32[32,256]{1,0:T(8,128)S(1)} %add.60), channel_id=1, source_target_pairs={{0,4},{1,5},{2,6},{3,7},{4,0},{5,1},{6,2},{7,3},{8,12},{9,13},{10,... | collective-permute-start | bytes 98312 | tf_op jit(solution)/shard_map/ppermute | solution.py:464
  219.4 1.9 collective-permute-done.3
  221.3 0.7 broadcast_in_dim.52
  222.0 9.2 %all-to-all-start.5 = ((bf16[16,32,256]{2,1,0:T(8,128)(2,1)}), bf16[16,32,256]{2,1,0:T(8,128)(2,1)S(1)}, u32[]{:S(2)}, u32[]{:S(2)}) async-start(bf16[16,32,256]{2,1,0:T(8,128)(2,1)} %broadcast_in_dim.52), calls=%async_computation.5 | async-start | bytes 524288 | tf_op jit(solution)/shard_map/all_to_all | solution.py:366
  231.3 1.2 copy-done.6
  232.5 1.7 shard_map.106
  234.2 4.3 %all-to-all-done.5.whole_ref = bf16[16,32,256]{2,1,0:T(8,128)(2,1)S(1)} async-done(((bf16[16,32,256]{2,1,0:T(8,128)(2,1)}), bf16[16,32,256]{2,1,0:T(8,128)(2,1)S(1)}, u32[]{:S(2)}, u32[]{:S(2)}) %all-to-all-start.5) | async-done | bytes 262176 | tf_op jit(solution)/shard_map/all_to_all | solution.py:366
  238.5 0.8 shard_map.107
  (15 shorter events, 0.1 us)
Async XLA Ops:
  0.6 1.4 copy-start.3
  2.0 0.9 copy-start.8
  2.9 15.0 %copy-start.10 = (s32[1,5]{1,0:T(1,128)S(1)}, s32[1,5]{1,0:T(1,128)}, u32[]{:S(2)}) copy-start(s32[1,5]{1,0:T(1,128)} %param.12) | copy-start | bytes 64
  2.9 15.2 %copy-start.9 = (s32[1,5]{1,0:T(1,128)S(1)}, s32[1,5]{1,0:T(1,128)}, u32[]{:S(2)}) copy-start(s32[1,5]{1,0:T(1,128)} %param.11) | copy-start | bytes 64
  3.0 40.6 %copy-start.4 = (bf16[1,128,4096]{2,1,0:T(8,128)(2,1)S(1)}, bf16[1,128,4096]{2,1,0:T(8,128)(2,1)}, u32[]{:S(2)}) copy-start(bf16[1,128,4096]{2,1,0:T(8,128)(2,1)} %param.13) | copy-start | bytes 3145732
  3.0 40.6 %copy-start.7 = (bf16[16,4096]{1,0:T(8,128)(2,1)S(1)}, bf16[16,4096]{1,0:T(8,128)(2,1)}, u32[]{:S(2)}) copy-start(bf16[16,4096]{1,0:T(8,128)(2,1)} %up_ref.3) | copy-start | bytes 393220
  6.3 37.3 %all-to-all-start = ((bf16[8,16,6272]{2,1,0:T(8,128)(2,1)}), bf16[8,16,6272]{2,1,0:T(8,128)(2,1)S(1)}, u32[]{:S(2)}, u32[]{:S(2)}) async-start(bf16[8,16,6272]{2,1,0:T(8,128)(2,1)} %bitcast.8), calls=%async_computation | async-start | bytes 3211264 | tf_op jit(solution)/shard_map/all_to_all | solution.py:366
  43.6 59.4 %copy-start = (bf16[8,16,6272]{2,1,0:T(8,128)(2,1)}, bf16[8,16,6272]{2,1,0:T(8,128)(2,1)S(1)}, u32[]{:S(2)}) copy-start(bf16[8,16,6272]{2,1,0:T(8,128)(2,1)S(1)} %all-to-all-done) | copy-start | bytes 4816900
  102.9 34.3 %all-to-all-start.3 = ((bf16[8,16,4096]{2,1,0:T(8,128)(2,1)}), bf16[8,16,4096]{2,1,0:T(8,128)(2,1)S(1)}, u32[]{:S(2)}, u32[]{:S(2)}) async-start(bf16[8,16,4096]{2,1,0:T(8,128)(2,1)} %bitcast.13), calls=%async_computation.3 | async-start | bytes 2097152 | tf_op jit(solution)/shard_map/all_to_all | solution.py:366
  137.2 1.0 copy-start.1
  138.2 44.4 %all-to-all-start.2 = ((bf16[16,128,768]{2,1,0:T(8,128)(2,1)}), bf16[16,128,768]{2,1,0:T(8,128)(2,1)S(1)}, u32[]{:S(2)}, u32[]{:S(2)}) async-start(bf16[16,128,768]{2,1,0:T(8,128)(2,1)} %bitcast.40), calls=%async_computation.2 | async-start | bytes 6291456 | tf_op jit(solution)/shard_map/all_to_all | solution.py:366
  182.6 1.2 copy-start.2
  185.3 1.0 copy-start.5
  203.8 3.8 %collective-permute-start = (f32[32,256]{1,0:T(8,128)S(1)}, f32[32,256]{1,0:T(8,128)S(1)}, u32[]{:S(2)}, u32[]{:S(2)}) collective-permute-start(f32[32,256]{1,0:T(8,128)S(1)} %convert_reduce_fusion), channel_id=1, source_target_pairs={{0,128},{128,0},{1,129},{129,1},{2,130},{130,2},{3,131},{131,3},{4... | collective-permute-start | bytes 98312 | tf_op jit(solution)/shard_map/ppermute | solution.py:464
  207.5 2.8 %collective-permute-start.1 = (f32[32,256]{1,0:T(8,128)S(1)}, f32[32,256]{1,0:T(8,128)S(1)}, u32[]{:S(2)}, u32[]{:S(2)}) collective-permute-start(f32[32,256]{1,0:T(8,128)S(1)} %add.58), channel_id=1, source_target_pairs={{0,1},{1,0},{2,3},{3,2},{4,5},{5,4},{6,7},{7,6},{8,9},{9,8},{10,11... | collective-permute-start | bytes 98312 | tf_op jit(solution)/shard_map/ppermute | solution.py:464
  210.3 4.3 %collective-permute-start.2 = (f32[32,256]{1,0:T(8,128)S(1)}, f32[32,256]{1,0:T(8,128)S(1)}, u32[]{:S(2)}, u32[]{:S(2)}) collective-permute-start(f32[32,256]{1,0:T(8,128)S(1)} %add.59), channel_id=1, source_target_pairs={{0,2},{1,3},{2,0},{3,1},{4,6},{5,7},{6,4},{7,5},{8,10},{9,11},{10,... | collective-permute-start | bytes 98312 | tf_op jit(solution)/shard_map/ppermute | solution.py:464
  214.6 6.7 %collective-permute-start.3 = (f32[32,256]{1,0:T(8,128)S(1)}, f32[32,256]{1,0:T(8,128)S(1)}, u32[]{:S(2)}, u32[]{:S(2)}) collective-permute-start(f32[32,256]{1,0:T(8,128)S(1)} %add.60), channel_id=1, source_target_pairs={{0,4},{1,5},{2,6},{3,7},{4,0},{5,1},{6,2},{7,3},{8,12},{9,13},{10,... | collective-permute-start | bytes 98312 | tf_op jit(solution)/shard_map/ppermute | solution.py:464
  222.0 16.5 %all-to-all-start.5 = ((bf16[16,32,256]{2,1,0:T(8,128)(2,1)}), bf16[16,32,256]{2,1,0:T(8,128)(2,1)S(1)}, u32[]{:S(2)}, u32[]{:S(2)}) async-start(bf16[16,32,256]{2,1,0:T(8,128)(2,1)} %broadcast_in_dim.52), calls=%async_computation.5 | async-start | bytes 524288 | tf_op jit(solution)/shard_map/all_to_all | solution.py:366
  231.3 1.2 copy-start.6

commit v5 on v4

--- a/solution.py
+++ b/solution.py
@@ -35,30 +35,28 @@
     return table * cosine + pltpu.roll(table, HALF_DIM, 1) * sine
 
 
-def widen_kernel(inputs_ref, down_ref, qkv_ref, out_ref, inputs, down, slab, sems):
+def widen_kernel(inputs_ref, down_ref, qkv_ref, out_ref, inputs, slab, sems):
     width = qkv_ref.shape[1]
+    rank = down_ref.shape[0]
     chunk = inputs.shape[1] // CHUNKS
     parts = [slice(part * chunk, (part + 1) * chunk) for part in range(CHUNKS)]
     loads = [
         pltpu.make_async_copy(inputs_ref.at[:, part], inputs.at[:, part], sems.at[index])
         for index, part in enumerate(parts)
     ]
-    load_down = pltpu.make_async_copy(down_ref, down, sems.at[CHUNKS])
-    move = pltpu.make_async_copy(qkv_ref, out_ref.at[:, :width], sems.at[CHUNKS + 1])
-    load_down.start()
+    move = pltpu.make_async_copy(qkv_ref, out_ref.at[:, :width], sems.at[CHUNKS])
     for load in loads:
         load.start()
     move.start()
-    low = jnp.zeros((inputs.shape[0], down.shape[0]), F32)
+    low = jnp.zeros((inputs.shape[0], rank), F32)
     slab[...] = jnp.zeros_like(slab)
-    load_down.wait()
     for load, part in zip(loads, parts):
         load.wait()
         low += lax.dot_general(
-            inputs[:, part], down[:, part], (((1,), (1,)), ((), ())), preferred_element_type=F32
-        )
-    slab[:, : low.shape[1]] = low.astype(BF16)
-    add = pltpu.make_async_copy(slab, out_ref.at[:, width:], sems.at[CHUNKS + 2])
+            inputs[:, part], down_ref[:, part], (((1,), (1,)), ((), ())), preferred_element_type=F32
+        )
+    slab[:, :rank] = low.astype(BF16)
+    add = pltpu.make_async_copy(slab, out_ref.at[:, width:], sems.at[CHUNKS + 1])
     add.start()
     move.wait()
     add.wait()
@@ -272,7 +270,7 @@
     tiles = blocks * (blocks + 1) // 2
     return pl.pallas_call(
         attention_kernel,
-        out_shape=jax.ShapeDtypeStruct((rows, width), BF16),
+        out_shape=pltpu.HBM((rows, width), BF16),
         grid_spec=pltpu.PrefetchScalarGridSpec(
             num_scalar_prefetch=2,
             grid=(blocks,),
@@ -362,6 +360,10 @@
         second_ref[:, columns] = whole_ref[piece, rank:].astype(F32)
 
 
+def in_hbm(table):
+    return pltpu.with_memory_space_constraint(table, pltpu.HBM)
+
+
 def exchange(table, axis):
     return lax.all_to_all(table, axis, split_axis=0, concat_axis=0, tiled=True)
 
@@ -384,17 +386,16 @@
     in_place = pl.BlockSpec(memory_space=pl.ANY)
     wide = pl.pallas_call(
         widen_kernel,
-        out_shape=jax.ShapeDtypeStruct((token_count, qkv_width + HEAD_DIM), BF16),
-        in_specs=[in_place, in_place, in_place],
+        out_shape=pltpu.HBM((token_count, qkv_width + HEAD_DIM), BF16),
+        in_specs=[in_place, in_vmem, in_place],
         out_specs=in_place,
         scratch_shapes=[
             pltpu.VMEM((token_count, model_width), BF16),
-            pltpu.VMEM((rank, model_width), BF16),
             pltpu.VMEM((token_count, HEAD_DIM), BF16),
-            pltpu.SemaphoreType.DMA((CHUNKS + 3,)),
+            pltpu.SemaphoreType.DMA((CHUNKS + 2,)),
         ],
         compiler_params=pltpu.CompilerParams(vmem_limit_bytes=VMEM_BYTES),
-    )(x_local, adapter_down.T, qkv_local)
+    )(in_hbm(x_local), adapter_down.T, in_hbm(qkv_local))
     packed_qkv = exchange(wide, "dp")
     packed_low = packed_qkv[:, qkv_width : qkv_width + rank]
 
@@ -427,9 +428,9 @@
         out_shape=jax.ShapeDtypeStruct((members, token_count, PIECE), BF16),
         compiler_params=params,
     )(packed_qkv, adapter_up, cosine, sine, grad_raw, row_valid)
-    table = exchange(pieces, "sub").reshape(members * token_count, PIECE)
+    table = in_hbm(exchange(pieces, "sub").reshape(members * token_count, PIECE))
     table, x_held = lax.optimization_barrier((table, x_local))
-    packed_inputs = exchange(x_held, "dp")
+    packed_inputs = in_hbm(exchange(x_held, "dp"))
     results = attention(table, starts, ends)
     came = exchange(results.reshape(members, token_count, PIECE), "sub")
     query_gradient, terms = pl.pallas_call(

time: 240 us -> 283 us (1.18)
  Pallas kernels: 37.7 us -> 71.4 us
  starting transfers between devices: 37.2 us -> 52.5 us
    pallas_call x2, Pallas kernels: 32.7 us -> 66.2 us  [the longest x1 48.8 us: local(): pl.pallas_call(widen_kernel, out_shape=pltpu.HBM((token_count, qkv_width...]
    all_to_all x4, starting transfers between devices: 30.1 us -> 39.6 us  [exchange(): return lax.all_to_all(table, axis, split_axis=0, concat_axis=0, tiled=True)]
    ppermute x4, starting transfers between devices: 7.1 us -> 12.9 us  [local(): lax.ppermute(total, axis, [(i, i ^ apart) for i in range(size)])]
    ppermute x4, waiting for transfers between devices: 10.4 us -> 6 us  [local(): lax.ppermute(total, axis, [(i, i ^ apart) for i in range(size)])]
    unnamed x22 -> x18, local copies, waits for them, and re-layouts: 6.7 us -> 4.07 us
  transfers between devices with their start and end apart: 8 -> 8, of which waited for: 7 -> 8; matrix products, arithmetic and copies ran while one was open for 1% -> 1% of each run, Pallas kernels for 13% -> 7%
where the time goes in v5:
time: 283 us; the launch traced here: 282 us
  blocking collectives  75.4 us (27%)
  waiting for transfers between devices  73.6 us (26%)
  Pallas kernels  71.4 us (25%)
  starting transfers between devices  52.5 us (19%)
  local copies, waits for them, and re-layouts  5.56 us (2%)
    all_to_all x2, blocking collectives, exchange(): return lax.all_to_all(table, axis, split_axis=0, concat_axis=0, tiled=True)  75.4 us
    all_to_all x4, waiting for transfers between devices, exchange(): return lax.all_to_all(table, axis, split_axis=0, concat_axis=0, tiled=True)  67.6 us
    pallas_call x1, Pallas kernels, local(): pl.pallas_call(widen_kernel, out_shape=pltpu.HBM((token_count, qkv_width...  48.8 us
    all_to_all x4, starting transfers between devices, exchange(): return lax.all_to_all(table, axis, split_axis=0, concat_axis=0, tiled=True)  39.6 us
    pallas_call x1, Pallas kernels, attention(): pl.pallas_call(attention_kernel, out_shape=pltpu.HBM((rows, width), BF16)...  17.4 us
    ppermute x4, starting transfers between devices, local(): lax.ppermute(total, axis, [(i, i ^ apart) for i in range(size)])  12.9 us
    ppermute x4, waiting for transfers between devices, local(): lax.ppermute(total, axis, [(i, i ^ apart) for i in range(size)])  6 us
  transfers between devices with their start and end apart: 8, of which 8 were waited for; matrix products, arithmetic and copies ran while one was open for 1% of the time, Pallas kernels for 7%

profile of v5, /device:TPU:1, one launch (start us, length us, event | category | flops | bytes accessed | tf_op | source)
XLA Modules:
  0.0 282.5 jit_solution(11780404844153175774)
XLA Ops:
  0.6 0.0 copy-start.5
  0.6 0.9 copy-done.5
  1.5 0.0 copy-start.8
  1.5 0.0 copy-start.7
  1.5 0.0 copy-start.1
  1.5 0.0 copy-start.4
  1.5 48.8 %shard_map.102 = bf16[128,6272]{1,0:T(8,128)(2,1)} custom-call(bf16[128,4096]{1,0:T(8,128)(2,1)} %bitcast.5.inputs_ref, bf16[16,4096]{1,0:T(8,128)(2,1)S(1)} %bitcast.34, bf16[128,6144]{1,0:T(8,128)(2,1)} %bitcast.41), custom_call_target="tpu_custom_call" | custom-call | tf_op jit(solution)/shard_map/pallas_call | solution.py:387
  50.4 11.7 %all-to-all-start = ((bf16[8,16,6272]{2,1,0:T(8,128)(2,1)}), bf16[8,16,6272]{2,1,0:T(8,128)(2,1)S(1)}, u32[]{:S(2)}, u32[]{:S(2)}) async-start(bf16[8,16,6272]{2,1,0:T(8,128)(2,1)} %bitcast.35), calls=%async_computation | async-start | bytes 3211264 | tf_op jit(solution)/shard_map/all_to_all | solution.py:368
  62.0 0.0 copy-done.8
  62.0 0.2 reduce-window.4
  62.2 0.0 copy-done.7
  62.2 0.6 select_reduce_fusion.2
  63.5 0.7 fusion.valid_ref
  64.2 0.3 fusion.1
  64.5 0.1 pad_maximum_fusion
  64.6 23.0 %all-to-all-done = bf16[8,16,6272]{2,1,0:T(8,128)(2,1)S(1)} async-done(((bf16[8,16,6272]{2,1,0:T(8,128)(2,1)}), bf16[8,16,6272]{2,1,0:T(8,128)(2,1)S(1)}, u32[]{:S(2)}, u32[]{:S(2)}) %all-to-all-start) | async-done | bytes 1605664 | tf_op jit(solution)/shard_map/all_to_all | solution.py:368
  87.7 0.0 copy-done.1
  87.7 0.0 copy-done.4
  87.7 1.0 shard_map.103
  88.7 58.3 %all_to_all.42 = bf16[16,128,768]{2,1,0:T(8,128)(2,1)} all-to-all(bf16[16,128,768]{2,1,0:T(8,128)(2,1)S(1)} %shard_map.103), channel_id=1, replica_groups=mesh['half'=2,'sub'=16,'dp'=8] {'sub'}, dimensions={0} | all-to-all | bytes 6291456 | tf_op jit(solution)/shard_map/all_to_all | solution.py:368
  147.0 0.0 copy-done
  147.0 4.3 %all-to-all-start.3 = ((bf16[8,16,4096]{2,1,0:T(8,128)(2,1)}), bf16[8,16,4096]{2,1,0:T(8,128)(2,1)S(1)}, u32[]{:S(2)}, u32[]{:S(2)}) async-start(bf16[8,16,4096]{2,1,0:T(8,128)(2,1)} %bitcast.13), calls=%async_computation.3 | async-start | bytes 2097152 | tf_op jit(solution)/shard_map/all_to_all | solution.py:368
  151.3 0.2 select_reduce_fusion
  151.5 0.5 fusion.3
  152.0 17.4 %shard_map.104 = bf16[2048,768]{1,0:T(8,128)(2,1)} custom-call(s32[8]{0:T(128)} %get-tuple-element.25.start_ref, s32[8]{0:T(128)} %get-tuple-element.24.end_ref, bf16[2048,768]{1,0:T(8,128)(2,1)} %bitcast.37, bf16[2048,768]{1,0:T(8,128)(2,1)} %bitcast.38, bf16[2048,768]{1,0:T(8,128)(2,1)} %bitcast.39), custom_call_target="tpu_custom_call" | custom-call | flops 8053063680 | bytes 6291456 | tf_op jit(solution)/shard_map/pallas_call | solution.py:271
  169.4 0.7 all-to-all-done.3
  170.0 1.0 copy-done.6
  171.0 14.7 %all-to-all-start.2 = ((bf16[16,128,768]{2,1,0:T(8,128)(2,1)}), bf16[16,128,768]{2,1,0:T(8,128)(2,1)S(1)}, u32[]{:S(2)}, u32[]{:S(2)}) async-start(bf16[16,128,768]{2,1,0:T(8,128)(2,1)} %bitcast.40), calls=%async_computation.2 | async-start | bytes 6291456 | tf_op jit(solution)/shard_map/all_to_all | solution.py:368
  185.7 0.8 slice.4.low_ref
  186.5 39.6 %all-to-all-done.2.came_ref = bf16[16,128,768]{2,1,0:T(8,128)(2,1)S(1)} async-done(((bf16[16,128,768]{2,1,0:T(8,128)(2,1)}), bf16[16,128,768]{2,1,0:T(8,128)(2,1)S(1)}, u32[]{:S(2)}, u32[]{:S(2)}) %all-to-all-start.2) | async-done | bytes 3145760 | tf_op jit(solution)/shard_map/all_to_all | solution.py:368
  226.0 1.6 shard_map.105
  227.7 0.0 copy-start.2
  227.7 1.0 copy-done.2
  228.6 17.0 %all_to_all.43 = bf16[16,32,256]{2,1,0:T(8,128)(2,1)S(1)} all-to-all(bf16[16,32,256]{2,1,0:T(8,128)(2,1)S(1)} %get-tuple-element.17), channel_id=1, replica_groups=mesh['half'=2,'sub'=16,'dp'=8] {'sub'}, dimensions={0} | all-to-all | bytes 524288 | tf_op jit(solution)/shard_map/all_to_all | solution.py:368
  245.7 2.2 collective-permute-start
  248.0 1.5 collective-permute-done
  249.5 2.9 %collective-permute-start.1 = (f32[32,256]{1,0:T(8,128)S(1)}, f32[32,256]{1,0:T(8,128)S(1)}, u32[]{:S(2)}, u32[]{:S(2)}) collective-permute-start(f32[32,256]{1,0:T(8,128)S(1)} %add.58), channel_id=1, source_target_pairs={{0,1},{1,0},{2,3},{3,2},{4,5},{5,4},{6,7},{7,6},{8,9},{9,8},{10,11... | collective-permute-start | bytes 98312 | tf_op jit(solution)/shard_map/ppermute | solution.py:465
  252.4 1.3 collective-permute-done.1
  253.7 2.4 collective-permute-start.2
  256.1 1.9 collective-permute-done.2
  258.0 5.4 %collective-permute-start.3 = (f32[32,256]{1,0:T(8,128)S(1)}, f32[32,256]{1,0:T(8,128)S(1)}, u32[]{:S(2)}, u32[]{:S(2)}) collective-permute-start(f32[32,256]{1,0:T(8,128)S(1)} %add.60), channel_id=1, source_target_pairs={{0,4},{1,5},{2,6},{3,7},{4,0},{5,1},{6,2},{7,3},{8,12},{9,13},{10,... | collective-permute-start | bytes 98312 | tf_op jit(solution)/shard_map/ppermute | solution.py:465
  263.4 1.3 collective-permute-done.3
  264.7 0.7 broadcast_in_dim.52
  265.4 9.0 %all-to-all-start.5 = ((bf16[16,32,256]{2,1,0:T(8,128)(2,1)}), bf16[16,32,256]{2,1,0:T(8,128)(2,1)S(1)}, u32[]{:S(2)}, u32[]{:S(2)}) async-start(bf16[16,32,256]{2,1,0:T(8,128)(2,1)} %broadcast_in_dim.52), calls=%async_computation.5 | async-start | bytes 524288 | tf_op jit(solution)/shard_map/all_to_all | solution.py:368
  274.4 1.2 copy-done.3
  275.6 1.7 shard_map.106
  277.4 4.3 %all-to-all-done.5.whole_ref = bf16[16,32,256]{2,1,0:T(8,128)(2,1)S(1)} async-done(((bf16[16,32,256]{2,1,0:T(8,128)(2,1)}), bf16[16,32,256]{2,1,0:T(8,128)(2,1)S(1)}, u32[]{:S(2)}, u32[]{:S(2)}) %all-to-all-start.5) | async-done | bytes 262176 | tf_op jit(solution)/shard_map/all_to_all | solution.py:368
  281.6 0.8 shard_map.107
  (11 shorter events, 0.1 us)
Async XLA Ops:
  0.6 0.9 copy-start.5
  1.5 60.5 %copy-start.8 = (s32[1,5]{1,0:T(1,128)S(1)}, s32[1,5]{1,0:T(1,128)}, u32[]{:S(2)}) copy-start(s32[1,5]{1,0:T(1,128)} %param.12) | copy-start | bytes 64
  1.5 60.7 %copy-start.7 = (s32[1,5]{1,0:T(1,128)S(1)}, s32[1,5]{1,0:T(1,128)}, u32[]{:S(2)}) copy-start(s32[1,5]{1,0:T(1,128)} %param.11) | copy-start | bytes 64
  1.5 86.1 %copy-start.1 = (bf16[1,128,4096]{2,1,0:T(8,128)(2,1)S(1)}, bf16[1,128,4096]{2,1,0:T(8,128)(2,1)}, u32[]{:S(2)}) copy-start(bf16[1,128,4096]{2,1,0:T(8,128)(2,1)} %param.13) | copy-start | bytes 3145732
  1.5 86.1 %copy-start.4 = (bf16[16,4096]{1,0:T(8,128)(2,1)S(1)}, bf16[16,4096]{1,0:T(8,128)(2,1)}, u32[]{:S(2)}) copy-start(bf16[16,4096]{1,0:T(8,128)(2,1)} %up_ref.3) | copy-start | bytes 393220
  50.4 37.3 %all-to-all-start = ((bf16[8,16,6272]{2,1,0:T(8,128)(2,1)}), bf16[8,16,6272]{2,1,0:T(8,128)(2,1)S(1)}, u32[]{:S(2)}, u32[]{:S(2)}) async-start(bf16[8,16,6272]{2,1,0:T(8,128)(2,1)} %bitcast.35), calls=%async_computation | async-start | bytes 3211264 | tf_op jit(solution)/shard_map/all_to_all | solution.py:368
  87.7 59.4 %copy-start = (bf16[8,16,6272]{2,1,0:T(8,128)(2,1)}, bf16[8,16,6272]{2,1,0:T(8,128)(2,1)S(1)}, u32[]{:S(2)}) copy-start(bf16[8,16,6272]{2,1,0:T(8,128)(2,1)S(1)} %all-to-all-done) | copy-start | bytes 4816900
  147.0 23.0 %all-to-all-start.3 = ((bf16[8,16,4096]{2,1,0:T(8,128)(2,1)}), bf16[8,16,4096]{2,1,0:T(8,128)(2,1)S(1)}, u32[]{:S(2)}, u32[]{:S(2)}) async-start(bf16[8,16,4096]{2,1,0:T(8,128)(2,1)} %bitcast.13), calls=%async_computation.3 | async-start | bytes 2097152 | tf_op jit(solution)/shard_map/all_to_all | solution.py:368
  170.0 1.0 copy-start.6
  171.0 55.0 %all-to-all-start.2 = ((bf16[16,128,768]{2,1,0:T(8,128)(2,1)}), bf16[16,128,768]{2,1,0:T(8,128)(2,1)S(1)}, u32[]{:S(2)}, u32[]{:S(2)}) async-start(bf16[16,128,768]{2,1,0:T(8,128)(2,1)} %bitcast.40), calls=%async_computation.2 | async-start | bytes 6291456 | tf_op jit(solution)/shard_map/all_to_all | solution.py:368
  227.7 1.0 copy-start.2
  245.7 3.8 %collective-permute-start = (f32[32,256]{1,0:T(8,128)S(1)}, f32[32,256]{1,0:T(8,128)S(1)}, u32[]{:S(2)}, u32[]{:S(2)}) collective-permute-start(f32[32,256]{1,0:T(8,128)S(1)} %convert_reduce_fusion), channel_id=1, source_target_pairs={{0,128},{128,0},{1,129},{129,1},{2,130},{130,2},{3,131},{131,3},{4... | collective-permute-start | bytes 98312 | tf_op jit(solution)/shard_map/ppermute | solution.py:465
  249.5 4.2 %collective-permute-start.1 = (f32[32,256]{1,0:T(8,128)S(1)}, f32[32,256]{1,0:T(8,128)S(1)}, u32[]{:S(2)}, u32[]{:S(2)}) collective-permute-start(f32[32,256]{1,0:T(8,128)S(1)} %add.58), channel_id=1, source_target_pairs={{0,1},{1,0},{2,3},{3,2},{4,5},{5,4},{6,7},{7,6},{8,9},{9,8},{10,11... | collective-permute-start | bytes 98312 | tf_op jit(solution)/shard_map/ppermute | solution.py:465
  253.7 4.3 %collective-permute-start.2 = (f32[32,256]{1,0:T(8,128)S(1)}, f32[32,256]{1,0:T(8,128)S(1)}, u32[]{:S(2)}, u32[]{:S(2)}) collective-permute-start(f32[32,256]{1,0:T(8,128)S(1)} %add.59), channel_id=1, source_target_pairs={{0,2},{1,3},{2,0},{3,1},{4,6},{5,7},{6,4},{7,5},{8,10},{9,11},{10,... | collective-permute-start | bytes 98312 | tf_op jit(solution)/shard_map/ppermute | solution.py:465
  258.0 6.7 %collective-permute-start.3 = (f32[32,256]{1,0:T(8,128)S(1)}, f32[32,256]{1,0:T(8,128)S(1)}, u32[]{:S(2)}, u32[]{:S(2)}) collective-permute-start(f32[32,256]{1,0:T(8,128)S(1)} %add.60), channel_id=1, source_target_pairs={{0,4},{1,5},{2,6},{3,7},{4,0},{5,1},{6,2},{7,3},{8,12},{9,13},{10,... | collective-permute-start | bytes 98312 | tf_op jit(solution)/shard_map/ppermute | solution.py:465
  265.4 16.2 %all-to-all-start.5 = ((bf16[16,32,256]{2,1,0:T(8,128)(2,1)}), bf16[16,32,256]{2,1,0:T(8,128)(2,1)S(1)}, u32[]{:S(2)}, u32[]{:S(2)}) async-start(bf16[16,32,256]{2,1,0:T(8,128)(2,1)} %broadcast_in_dim.52), calls=%async_computation.5 | async-start | bytes 524288 | tf_op jit(solution)/shard_map/all_to_all | solution.py:368
  274.4 1.2 copy-start.3

commit v6 on v5

--- a/solution.py
+++ b/solution.py
@@ -35,31 +35,46 @@
     return table * cosine + pltpu.roll(table, HALF_DIM, 1) * sine
 
 
-def widen_kernel(inputs_ref, down_ref, qkv_ref, out_ref, inputs, slab, sems):
+def widen_kernel(inputs_ref, down_ref, qkv_ref, out_ref, inputs, down, held, sems, moves):
     width = qkv_ref.shape[1]
     rank = down_ref.shape[0]
+
+    def copies(source, target, span, use, first):
+        size = span // CHUNKS
+        return [
+            pltpu.make_async_copy(
+                source.at[:, part * size : (part + 1) * size],
+                target.at[:, part * size : (part + 1) * size],
+                use.at[first + part],
+            )
+            for part in range(CHUNKS)
+        ]
+
+    load_down = pltpu.make_async_copy(down_ref, down, sems.at[2 * CHUNKS])
+    load_down.start()
+    loads = copies(inputs_ref, inputs, inputs.shape[1], sems, 0)
+    reads = copies(qkv_ref, held, width, sems, CHUNKS)
+    writes = copies(held, out_ref, width, moves, 0)
+    for load in loads + reads:
+        load.start()
+    low = jnp.zeros((inputs.shape[0], rank), F32)
+    held[:, width:] = jnp.zeros((inputs.shape[0], HEAD_DIM), BF16)
     chunk = inputs.shape[1] // CHUNKS
-    parts = [slice(part * chunk, (part + 1) * chunk) for part in range(CHUNKS)]
-    loads = [
-        pltpu.make_async_copy(inputs_ref.at[:, part], inputs.at[:, part], sems.at[index])
-        for index, part in enumerate(parts)
-    ]
-    move = pltpu.make_async_copy(qkv_ref, out_ref.at[:, :width], sems.at[CHUNKS])
-    for load in loads:
-        load.start()
-    move.start()
-    low = jnp.zeros((inputs.shape[0], rank), F32)
-    slab[...] = jnp.zeros_like(slab)
-    for load, part in zip(loads, parts):
+    load_down.wait()
+    for index, load in enumerate(loads):
+        part = slice(index * chunk, (index + 1) * chunk)
         load.wait()
         low += lax.dot_general(
-            inputs[:, part], down_ref[:, part], (((1,), (1,)), ((), ())), preferred_element_type=F32
+            inputs[:, part], down[:, part], (((1,), (1,)), ((), ())), preferred_element_type=F32
         )
-    slab[:, :rank] = low.astype(BF16)
-    add = pltpu.make_async_copy(slab, out_ref.at[:, width:], sems.at[CHUNKS + 1])
-    add.start()
-    move.wait()
-    add.wait()
+        reads[index].wait()
+        writes[index].start()
+    held[:, width : width + rank] = low.astype(BF16)
+    last = pltpu.make_async_copy(held.at[:, width:], out_ref.at[:, width:], moves.at[CHUNKS])
+    last.start()
+    for write in writes:
+        write.wait()
+    last.wait()
 
 
 def prepare_kernel(qkv_ref, up_ref, cos_ref, sin_ref, grad_ref, valid_ref, out_ref):
@@ -387,15 +402,17 @@
     wide = pl.pallas_call(
         widen_kernel,
         out_shape=pltpu.HBM((token_count, qkv_width + HEAD_DIM), BF16),
-        in_specs=[in_place, in_vmem, in_place],
+        in_specs=[in_place, in_place, in_place],
         out_specs=in_place,
         scratch_shapes=[
             pltpu.VMEM((token_count, model_width), BF16),
-            pltpu.VMEM((token_count, HEAD_DIM), BF16),
-            pltpu.SemaphoreType.DMA((CHUNKS + 2,)),
+            pltpu.VMEM((rank, model_width), BF16),
+            pltpu.VMEM((token_count, qkv_width + HEAD_DIM), BF16),
+            pltpu.SemaphoreType.DMA((2 * CHUNKS + 1,)),
+            pltpu.SemaphoreType.DMA((CHUNKS + 1,)),
         ],
         compiler_params=pltpu.CompilerParams(vmem_limit_bytes=VMEM_BYTES),
-    )(in_hbm(x_local), adapter_down.T, in_hbm(qkv_local))
+    )(in_hbm(x_local), in_hbm(adapter_down.T), in_hbm(qkv_local))
     packed_qkv = exchange(wide, "dp")
     packed_low = packed_qkv[:, qkv_width : qkv_width + rank]
 
@@ -437,7 +454,7 @@
         query_kernel,
         out_shape=(
             jax.ShapeDtypeStruct((token_count, query_columns), BF16),
-            jax.ShapeDtypeStruct((members, 2 * rank, PAIR), BF16),
+            pltpu.HBM((members, 2 * rank, PAIR), BF16),
         ),
         in_specs=[in_vmem, in_vmem, in_vmem, in_place, in_vmem, in_vmem],
         scratch_shapes=[

time: 283 us -> 238 us (0.84)
  Pallas kernels: 71.4 us -> 24.5 us
  waiting for transfers between devices: 73.6 us -> 78.3 us
    pallas_call x1, Pallas kernels: 48.8 us -> 3.18 us  [local(): pl.pallas_call(widen_kernel, out_shape=pltpu.HBM((token_count, qkv_width...]
where the time goes in v6:
time: 238 us; the launch traced here: 237 us
  waiting for transfers between devices  78.3 us (33%)
  blocking collectives  75.6 us (32%)
  starting transfers between devices  50.3 us (21%)
  Pallas kernels  24.5 us (10%)
  local copies, waits for them, and re-layouts  4.67 us (2%)
  other arithmetic  2.68 us (1%)
    all_to_all x2, blocking collectives, exchange(): return lax.all_to_all(table, axis, split_axis=0, concat_axis=0, tiled=True)  75.6 us
    all_to_all x4, waiting for transfers between devices, exchange(): return lax.all_to_all(table, axis, split_axis=0, concat_axis=0, tiled=True)  70.1 us
    all_to_all x4, starting transfers between devices, exchange(): return lax.all_to_all(table, axis, split_axis=0, concat_axis=0, tiled=True)  39.6 us
    pallas_call x1, Pallas kernels, attention(): pl.pallas_call(attention_kernel, out_shape=pltpu.HBM((rows, width), BF16)...  14.8 us
    ppermute x4, starting transfers between devices, local(): lax.ppermute(total, axis, [(i, i ^ apart) for i in range(size)])  10.7 us
    ppermute x4, waiting for transfers between devices, local(): lax.ppermute(total, axis, [(i, i ^ apart) for i in range(size)])  8.23 us
  transfers between devices with their start and end apart: 8, of which 8 were waited for; matrix products, arithmetic and copies ran while one was open for 1% of the time, Pallas kernels for 7%

profile of v6, /device:TPU:1, one launch (start us, length us, event | category | flops | bytes accessed | tf_op | source)
XLA Modules:
  0.0 237.5 jit_solution(12158537204715152006)
XLA Ops:
  0.6 0.0 copy-start.7
  0.6 0.0 copy-start.6
  0.7 0.0 copy-start.1
  0.7 0.0 copy-start.4
  0.7 3.2 %shard_map.102 = bf16[128,6272]{1,0:T(8,128)(2,1)} custom-call(bf16[128,4096]{1,0:T(8,128)(2,1)} %bitcast.5.inputs_ref, bf16[16,4096]{1,0:T(8,128)(2,1)} %bitcast.41, bf16[128,6144]{1,0:T(8,128)(2,1)} %bitcast.40), custom_call_target="tpu_custom_call" | custom-call | tf_op jit(solution)/shard_map/pallas_call | solution.py:402
  3.9 11.7 %all-to-all-start = ((bf16[8,16,6272]{2,1,0:T(8,128)(2,1)}), bf16[8,16,6272]{2,1,0:T(8,128)(2,1)S(1)}, u32[]{:S(2)}, u32[]{:S(2)}) async-start(bf16[8,16,6272]{2,1,0:T(8,128)(2,1)} %bitcast.34), calls=%async_computation | async-start | bytes 3211264 | tf_op jit(solution)/shard_map/all_to_all | solution.py:383
  15.5 0.0 copy-done.7
  15.5 0.2 reduce-window.4
  15.7 0.0 copy-done.6
  15.7 0.6 select_reduce_fusion.2
  17.0 0.7 fusion.valid_ref
  17.7 0.3 fusion.1
  18.0 0.1 pad_maximum_fusion
  18.1 23.0 %all-to-all-done = bf16[8,16,6272]{2,1,0:T(8,128)(2,1)S(1)} async-done(((bf16[8,16,6272]{2,1,0:T(8,128)(2,1)}), bf16[8,16,6272]{2,1,0:T(8,128)(2,1)S(1)}, u32[]{:S(2)}, u32[]{:S(2)}) %all-to-all-start) | async-done | bytes 1605664 | tf_op jit(solution)/shard_map/all_to_all | solution.py:383
  41.2 0.0 copy-start
  41.2 0.0 copy-done.1
  41.2 0.0 copy-done.4
  41.2 1.0 shard_map.103
  42.2 58.4 %all_to_all.42 = bf16[16,128,768]{2,1,0:T(8,128)(2,1)} all-to-all(bf16[16,128,768]{2,1,0:T(8,128)(2,1)S(1)} %shard_map.103), channel_id=1, replica_groups=mesh['half'=2,'sub'=16,'dp'=8] {'sub'}, dimensions={0} | all-to-all | bytes 6291456 | tf_op jit(solution)/shard_map/all_to_all | solution.py:383
  100.5 0.0 copy-done
  100.5 4.2 %all-to-all-start.3 = ((bf16[8,16,4096]{2,1,0:T(8,128)(2,1)}), bf16[8,16,4096]{2,1,0:T(8,128)(2,1)S(1)}, u32[]{:S(2)}, u32[]{:S(2)}) async-start(bf16[8,16,4096]{2,1,0:T(8,128)(2,1)} %bitcast.13), calls=%async_computation.3 | async-start | bytes 2097152 | tf_op jit(solution)/shard_map/all_to_all | solution.py:383
  104.7 0.2 select_reduce_fusion
  104.9 0.5 fusion.3
  105.4 14.8 %shard_map.104 = bf16[2048,768]{1,0:T(8,128)(2,1)} custom-call(s32[8]{0:T(128)} %get-tuple-element.25.start_ref, s32[8]{0:T(128)} %get-tuple-element.24.end_ref, bf16[2048,768]{1,0:T(8,128)(2,1)} %bitcast.36, bf16[2048,768]{1,0:T(8,128)(2,1)} %bitcast.37, bf16[2048,768]{1,0:T(8,128)(2,1)} %bitcast.38), custom_call_target="tpu_custom_call" | custom-call | flops 8053063680 | bytes 6291456 | tf_op jit(solution)/shard_map/pallas_call | solution.py:286
  120.2 3.2 %all-to-all-done.3 = bf16[8,16,4096]{2,1,0:T(8,128)(2,1)S(1)} async-done(((bf16[8,16,4096]{2,1,0:T(8,128)(2,1)}), bf16[8,16,4096]{2,1,0:T(8,128)(2,1)S(1)}, u32[]{:S(2)}, u32[]{:S(2)}) %all-to-all-start.3) | async-done | bytes 1048608 | tf_op jit(solution)/shard_map/all_to_all | solution.py:383
  123.4 0.0 copy-start.5
  123.4 1.0 copy-done.5
  124.4 14.8 %all-to-all-start.2 = ((bf16[16,128,768]{2,1,0:T(8,128)(2,1)}), bf16[16,128,768]{2,1,0:T(8,128)(2,1)S(1)}, u32[]{:S(2)}, u32[]{:S(2)}) async-start(bf16[16,128,768]{2,1,0:T(8,128)(2,1)} %bitcast.39), calls=%async_computation.2 | async-start | bytes 6291456 | tf_op jit(solution)/shard_map/all_to_all | solution.py:383
  139.2 0.8 slice.4.low_ref
  139.9 39.6 %all-to-all-done.2.came_ref = bf16[16,128,768]{2,1,0:T(8,128)(2,1)S(1)} async-done(((bf16[16,128,768]{2,1,0:T(8,128)(2,1)}), bf16[16,128,768]{2,1,0:T(8,128)(2,1)S(1)}, u32[]{:S(2)}, u32[]{:S(2)}) %all-to-all-start.2) | async-done | bytes 3145760 | tf_op jit(solution)/shard_map/all_to_all | solution.py:383
  179.5 3.0 %shard_map.105 = (bf16[128,4096]{1,0:T(8,128)(2,1)S(1)}, bf16[16,32,256]{2,1,0:T(8,128)(2,1)}) custom-call(bf16[16,128,768]{2,1,0:T(8,128)(2,1)S(1)} %all-to-all-done.2.came_ref, bf16[128,16]{1,0:T(8,128)(2,1)S(1)} %slice.4.low_ref, bf16[16,4096]{1,0:T(8,128)(2,1)S(1)} %copy-done.4, bf16[128,4096]{1,0:T(8,128)(2,1)} %bitcast.35, ...), custom_call_target="tpu_custom_call" | custom-call | tf_op jit(solution)/shard_map/pallas_call | solution.py:453
  182.5 0.0 copy-start.2
  182.5 1.0 copy-done.2
  183.5 17.3 %all_to_all.43 = bf16[16,32,256]{2,1,0:T(8,128)(2,1)S(1)} all-to-all(bf16[16,32,256]{2,1,0:T(8,128)(2,1)} %get-tuple-element.17), channel_id=1, replica_groups=mesh['half'=2,'sub'=16,'dp'=8] {'sub'}, dimensions={0} | all-to-all | bytes 524288 | tf_op jit(solution)/shard_map/all_to_all | solution.py:383
  200.8 2.2 collective-permute-start
  203.0 1.5 collective-permute-done
  204.5 2.9 %collective-permute-start.1 = (f32[32,256]{1,0:T(8,128)S(1)}, f32[32,256]{1,0:T(8,128)S(1)}, u32[]{:S(2)}, u32[]{:S(2)}) collective-permute-start(f32[32,256]{1,0:T(8,128)S(1)} %add.58), channel_id=1, source_target_pairs={{0,1},{1,0},{2,3},{3,2},{4,5},{5,4},{6,7},{7,6},{8,9},{9,8},{10,11... | collective-permute-start | bytes 98312 | tf_op jit(solution)/shard_map/ppermute | solution.py:482
  207.4 1.3 collective-permute-done.1
  208.7 1.6 collective-permute-start.2
  210.3 2.7 %collective-permute-done.2 = f32[32,256]{1,0:T(8,128)S(1)} collective-permute-done((f32[32,256]{1,0:T(8,128)S(1)}, f32[32,256]{1,0:T(8,128)S(1)}, u32[]{:S(2)}, u32[]{:S(2)}) %collective-permute-start.2) | collective-permute-done | bytes 32800 | tf_op jit(solution)/shard_map/ppermute | solution.py:482
  213.0 4.0 %collective-permute-start.3 = (f32[32,256]{1,0:T(8,128)S(1)}, f32[32,256]{1,0:T(8,128)S(1)}, u32[]{:S(2)}, u32[]{:S(2)}) collective-permute-start(f32[32,256]{1,0:T(8,128)S(1)} %add.60), channel_id=1, source_target_pairs={{0,4},{1,5},{2,6},{3,7},{4,0},{5,1},{6,2},{7,3},{8,12},{9,13},{10,... | collective-permute-start | bytes 98312 | tf_op jit(solution)/shard_map/ppermute | solution.py:482
  217.0 2.7 %collective-permute-done.3 = f32[32,256]{1,0:T(8,128)S(1)} collective-permute-done((f32[32,256]{1,0:T(8,128)S(1)}, f32[32,256]{1,0:T(8,128)S(1)}, u32[]{:S(2)}, u32[]{:S(2)}) %collective-permute-start.3) | collective-permute-done | bytes 32800 | tf_op jit(solution)/shard_map/ppermute | solution.py:482
  219.7 0.7 broadcast_in_dim.52
  220.4 9.0 %all-to-all-start.5 = ((bf16[16,32,256]{2,1,0:T(8,128)(2,1)}), bf16[16,32,256]{2,1,0:T(8,128)(2,1)S(1)}, u32[]{:S(2)}, u32[]{:S(2)}) async-start(bf16[16,32,256]{2,1,0:T(8,128)(2,1)} %broadcast_in_dim.52), calls=%async_computation.5 | async-start | bytes 524288 | tf_op jit(solution)/shard_map/all_to_all | solution.py:383
  229.4 1.2 copy-done.3
  230.6 1.7 shard_map.106
  232.4 4.3 %all-to-all-done.5.whole_ref = bf16[16,32,256]{2,1,0:T(8,128)(2,1)S(1)} async-done(((bf16[16,32,256]{2,1,0:T(8,128)(2,1)}), bf16[16,32,256]{2,1,0:T(8,128)(2,1)S(1)}, u32[]{:S(2)}, u32[]{:S(2)}) %all-to-all-start.5) | async-done | bytes 262176 | tf_op jit(solution)/shard_map/all_to_all | solution.py:383
  236.6 0.8 shard_map.107
  (9 shorter events, 0.1 us)
Async XLA Ops:
  0.6 14.9 %copy-start.7 = (s32[1,5]{1,0:T(1,128)S(1)}, s32[1,5]{1,0:T(1,128)}, u32[]{:S(2)}) copy-start(s32[1,5]{1,0:T(1,128)} %param.12) | copy-start | bytes 64
  0.6 15.1 %copy-start.6 = (s32[1,5]{1,0:T(1,128)S(1)}, s32[1,5]{1,0:T(1,128)}, u32[]{:S(2)}) copy-start(s32[1,5]{1,0:T(1,128)} %param.11) | copy-start | bytes 64
  0.7 40.5 %copy-start.1 = (bf16[1,128,4096]{2,1,0:T(8,128)(2,1)S(1)}, bf16[1,128,4096]{2,1,0:T(8,128)(2,1)}, u32[]{:S(2)}) copy-start(bf16[1,128,4096]{2,1,0:T(8,128)(2,1)} %param.13) | copy-start | bytes 3145732
  0.7 40.5 %copy-start.4 = (bf16[16,4096]{1,0:T(8,128)(2,1)S(1)}, bf16[16,4096]{1,0:T(8,128)(2,1)}, u32[]{:S(2)}) copy-start(bf16[16,4096]{1,0:T(8,128)(2,1)} %up_ref.3) | copy-start | bytes 393220
  3.9 37.3 %all-to-all-start = ((bf16[8,16,6272]{2,1,0:T(8,128)(2,1)}), bf16[8,16,6272]{2,1,0:T(8,128)(2,1)S(1)}, u32[]{:S(2)}, u32[]{:S(2)}) async-start(bf16[8,16,6272]{2,1,0:T(8,128)(2,1)} %bitcast.34), calls=%async_computation | async-start | bytes 3211264 | tf_op jit(solution)/shard_map/all_to_all | solution.py:383
  41.2 59.4 %copy-start = (bf16[8,16,6272]{2,1,0:T(8,128)(2,1)}, bf16[8,16,6272]{2,1,0:T(8,128)(2,1)S(1)}, u32[]{:S(2)}) copy-start(bf16[8,16,6272]{2,1,0:T(8,128)(2,1)S(1)} %all-to-all-done) | copy-start | bytes 4816900
  100.5 22.9 %all-to-all-start.3 = ((bf16[8,16,4096]{2,1,0:T(8,128)(2,1)}), bf16[8,16,4096]{2,1,0:T(8,128)(2,1)S(1)}, u32[]{:S(2)}, u32[]{:S(2)}) async-start(bf16[8,16,4096]{2,1,0:T(8,128)(2,1)} %bitcast.13), calls=%async_computation.3 | async-start | bytes 2097152 | tf_op jit(solution)/shard_map/all_to_all | solution.py:383
  123.4 1.0 copy-start.5
  124.4 55.1 %all-to-all-start.2 = ((bf16[16,128,768]{2,1,0:T(8,128)(2,1)}), bf16[16,128,768]{2,1,0:T(8,128)(2,1)S(1)}, u32[]{:S(2)}, u32[]{:S(2)}) async-start(bf16[16,128,768]{2,1,0:T(8,128)(2,1)} %bitcast.39), calls=%async_computation.2 | async-start | bytes 6291456 | tf_op jit(solution)/shard_map/all_to_all | solution.py:383
  182.5 1.0 copy-start.2
  200.8 3.8 %collective-permute-start = (f32[32,256]{1,0:T(8,128)S(1)}, f32[32,256]{1,0:T(8,128)S(1)}, u32[]{:S(2)}, u32[]{:S(2)}) collective-permute-start(f32[32,256]{1,0:T(8,128)S(1)} %convert_reduce_fusion), channel_id=1, source_target_pairs={{0,128},{128,0},{1,129},{129,1},{2,130},{130,2},{3,131},{131,3},{4... | collective-permute-start | bytes 98312 | tf_op jit(solution)/shard_map/ppermute | solution.py:482
  204.5 4.2 %collective-permute-start.1 = (f32[32,256]{1,0:T(8,128)S(1)}, f32[32,256]{1,0:T(8,128)S(1)}, u32[]{:S(2)}, u32[]{:S(2)}) collective-permute-start(f32[32,256]{1,0:T(8,128)S(1)} %add.58), channel_id=1, source_target_pairs={{0,1},{1,0},{2,3},{3,2},{4,5},{5,4},{6,7},{7,6},{8,9},{9,8},{10,11... | collective-permute-start | bytes 98312 | tf_op jit(solution)/shard_map/ppermute | solution.py:482
  208.7 4.3 %collective-permute-start.2 = (f32[32,256]{1,0:T(8,128)S(1)}, f32[32,256]{1,0:T(8,128)S(1)}, u32[]{:S(2)}, u32[]{:S(2)}) collective-permute-start(f32[32,256]{1,0:T(8,128)S(1)} %add.59), channel_id=1, source_target_pairs={{0,2},{1,3},{2,0},{3,1},{4,6},{5,7},{6,4},{7,5},{8,10},{9,11},{10,... | collective-permute-start | bytes 98312 | tf_op jit(solution)/shard_map/ppermute | solution.py:482
  213.0 6.7 %collective-permute-start.3 = (f32[32,256]{1,0:T(8,128)S(1)}, f32[32,256]{1,0:T(8,128)S(1)}, u32[]{:S(2)}, u32[]{:S(2)}) collective-permute-start(f32[32,256]{1,0:T(8,128)S(1)} %add.60), channel_id=1, source_target_pairs={{0,4},{1,5},{2,6},{3,7},{4,0},{5,1},{6,2},{7,3},{8,12},{9,13},{10,... | collective-permute-start | bytes 98312 | tf_op jit(solution)/shard_map/ppermute | solution.py:482
  220.4 16.2 %all-to-all-start.5 = ((bf16[16,32,256]{2,1,0:T(8,128)(2,1)}), bf16[16,32,256]{2,1,0:T(8,128)(2,1)S(1)}, u32[]{:S(2)}, u32[]{:S(2)}) async-start(bf16[16,32,256]{2,1,0:T(8,128)(2,1)} %broadcast_in_dim.52), calls=%async_computation.5 | async-start | bytes 524288 | tf_op jit(solution)/shard_map/all_to_all | solution.py:383
  229.4 1.2 copy-start.3

commit v7 on v6

--- a/solution.py
+++ b/solution.py
@@ -16,7 +16,7 @@
 PIECE = 2 * PAIR + 2 * HEAD_DIM
 rope_base = 500000.0
 VMEM_BYTES = 48 * 1024 * 1024
-ATTENTION_VMEM_BYTES = 60 * 1024 * 1024
+ATTENTION_VMEM_BYTES = 65024 * 1024
 HIDDEN = -1e30
 CHUNKS = 4
 F32 = jnp.float32
@@ -316,8 +316,16 @@
     )(starts, ends, table, table, table)
 
 
+def unrotated_pair(came_ref, piece, cosine, sine):
+    heads = [
+        rotated(came_ref[piece, :, at : at + HEAD_DIM].astype(F32), cosine, sine).astype(BF16)
+        for at in (PAIR, PAIR + HEAD_DIM)
+    ]
+    return jnp.concatenate(heads, axis=1)
+
+
 def query_kernel(
-    came_ref, low_ref, up_ref, inputs_ref, cos_ref, sin_ref, grad_ref, term_ref, inputs, sem
+    came_ref, low_ref, up_ref, inputs_ref, cos_ref, sin_ref, term_ref, inputs, sem
 ):
     load = pltpu.make_async_copy(inputs_ref, inputs, sem)
     load.start()
@@ -328,13 +336,7 @@
     dlow = jnp.zeros(low_ref.shape, F32)
     for piece in range(came_ref.shape[0]):
         columns = slice(piece * PAIR, (piece + 1) * PAIR)
-        for head in range(2):
-            at = PAIR + head * HEAD_DIM
-            to = piece * PAIR + head * HEAD_DIM
-            grad_ref[:, to : to + HEAD_DIM] = rotated(
-                came_ref[piece, :, at : at + HEAD_DIM].astype(F32), cosine, sine
-            ).astype(BF16)
-        part = grad_ref[:, columns]
+        part = unrotated_pair(came_ref, piece, cosine, sine)
         dlow += lax.dot_general(
             part, up_ref[:, columns], (((1,), (1,)), ((), ())), preferred_element_type=F32
         )
@@ -348,14 +350,15 @@
         ).astype(BF16)
 
 
-def finish_kernel(came_ref, query_ref, cos_ref, sin_ref, out_ref, grad_ref):
+def finish_kernel(came_ref, cos_ref, sin_ref, out_ref, grad_ref):
     cosine = cos_ref[...]
     sine = -sin_ref[...]
-    queries = query_ref.shape[1]
+    queries = out_ref.shape[1]
     kv_width = (grad_ref.shape[1] - queries) // 2
-    grad_ref[:, :queries] = query_ref[...]
     for piece in range(came_ref.shape[0]):
-        out_ref[:, piece * PAIR : (piece + 1) * PAIR] = came_ref[piece, :, :PAIR]
+        columns = slice(piece * PAIR, (piece + 1) * PAIR)
+        out_ref[:, columns] = came_ref[piece, :, :PAIR]
+        grad_ref[:, columns] = unrotated_pair(came_ref, piece, cosine, sine)
     for key_head in range(kv_width // HEAD_DIM):
         pair = (2 * key_head, 2 * key_head + 1)
         keys, values = (
@@ -450,12 +453,9 @@
     packed_inputs = in_hbm(exchange(x_held, "dp"))
     results = attention(table, starts, ends)
     came = exchange(results.reshape(members, token_count, PIECE), "sub")
-    query_gradient, terms = pl.pallas_call(
+    terms = pl.pallas_call(
         query_kernel,
-        out_shape=(
-            jax.ShapeDtypeStruct((token_count, query_columns), BF16),
-            pltpu.HBM((members, 2 * rank, PAIR), BF16),
-        ),
+        out_shape=jax.ShapeDtypeStruct((members, 2 * rank, PAIR), BF16),
         in_specs=[in_vmem, in_vmem, in_vmem, in_place, in_vmem, in_vmem],
         scratch_shapes=[
             pltpu.VMEM((token_count, model_width), BF16),
@@ -475,7 +475,7 @@
             bytes_accessed=8 * token_count * qkv_width,
             transcendentals=0,
         ),
-    )(came, query_gradient, cosine, sine)
+    )(came, cosine, sine)
     total = jnp.sum(exchange(terms, "sub").astype(F32), axis=0)
     for axis, apart in (("half", 1), ("dp", 1), ("dp", 2), ("dp", 4)):
         size = lax.axis_size(axis)

time: 238 us -> 235 us (0.987)
  Pallas kernels: 24.5 us -> 38.2 us
  starting transfers between devices: 50.3 us -> 38.6 us
  local copies, waits for them, and re-layouts: 4.67 us -> 1.51 us
  waiting for transfers between devices: 78.3 us -> 75.7 us
    pallas_call x1, Pallas kernels: 14.8 us -> 29.4 us  [attention(): pl.pallas_call(attention_kernel, out_shape=pltpu.HBM((rows, width), BF16)...]
    all_to_all x4, starting transfers between devices: 39.6 us -> 29.8 us  [exchange(): return lax.all_to_all(table, axis, split_axis=0, concat_axis=0, tiled=True)]
    all_to_all x4, waiting for transfers between devices: 70.1 us -> 66.8 us  [exchange(): return lax.all_to_all(table, axis, split_axis=0, concat_axis=0, tiled=True)]
    unnamed x16 -> x10, local copies, waits for them, and re-layouts: 3.17 us -> 0.02 us
  transfers between devices with their start and end apart: 8 -> 8, of which waited for: 8 -> 7; matrix products, arithmetic and copies ran while one was open for 1% -> 1% of each run, Pallas kernels for 7% -> 14%
where the time goes in v7:
time: 235 us; the launch traced here: 234 us
  blocking collectives  75.9 us (32%)
  waiting for transfers between devices  75.7 us (32%)
  starting transfers between devices  38.6 us (16%)
  Pallas kernels  38.2 us (16%)
  other arithmetic  2.68 us (1%)
    all_to_all x2, blocking collectives, exchange(): return lax.all_to_all(table, axis, split_axis=0, concat_axis=0, tiled=True)  75.9 us
    all_to_all x4, waiting for transfers between devices, exchange(): return lax.all_to_all(table, axis, split_axis=0, concat_axis=0, tiled=True)  66.8 us
    all_to_all x4, starting transfers between devices, exchange(): return lax.all_to_all(table, axis, split_axis=0, concat_axis=0, tiled=True)  29.8 us
    pallas_call x1, Pallas kernels, attention(): pl.pallas_call(attention_kernel, out_shape=pltpu.HBM((rows, width), BF16)...  29.4 us
    ppermute x4, waiting for transfers between devices, local(): lax.ppermute(total, axis, [(i, i ^ apart) for i in range(size)])  8.96 us
    ppermute x4, starting transfers between devices, local(): lax.ppermute(total, axis, [(i, i ^ apart) for i in range(size)])  8.78 us
  transfers between devices with their start and end apart: 8, of which 7 were waited for; matrix products, arithmetic and copies ran while one was open for 1% of the time, Pallas kernels for 14%

profile of v7, /device:TPU:1, one launch (start us, length us, event | category | flops | bytes accessed | tf_op | source)
XLA Modules:
  0.0 234.0 jit_solution(17465134542861453981)
XLA Ops:
  0.6 0.0 copy-start.4
  0.6 0.0 copy-start.3
  0.7 0.0 copy-start.1
  0.7 0.0 copy-start.2
  0.7 3.1 %shard_map.102 = bf16[128,6272]{1,0:T(8,128)(2,1)} custom-call(bf16[128,4096]{1,0:T(8,128)(2,1)} %bitcast.5.inputs_ref, bf16[16,4096]{1,0:T(8,128)(2,1)} %bitcast.40, bf16[128,6144]{1,0:T(8,128)(2,1)} %bitcast.39), custom_call_target="tpu_custom_call" | custom-call | tf_op jit(solution)/shard_map/pallas_call | solution.py:405
  3.8 11.7 %all-to-all-start = ((bf16[8,16,6272]{2,1,0:T(8,128)(2,1)}), bf16[8,16,6272]{2,1,0:T(8,128)(2,1)S(1)}, u32[]{:S(2)}, u32[]{:S(2)}) async-start(bf16[8,16,6272]{2,1,0:T(8,128)(2,1)} %bitcast.34), calls=%async_computation | async-start | bytes 3211264 | tf_op jit(solution)/shard_map/all_to_all | solution.py:386
  15.5 0.0 copy-done.4
  15.5 0.2 reduce-window.4
  15.7 0.0 copy-done.3
  15.7 0.6 select_reduce_fusion.2
  17.0 0.7 fusion.valid_ref
  17.7 0.3 fusion.1
  18.0 0.1 pad_maximum_fusion
  18.1 23.0 %all-to-all-done = bf16[8,16,6272]{2,1,0:T(8,128)(2,1)S(1)} async-done(((bf16[8,16,6272]{2,1,0:T(8,128)(2,1)}), bf16[8,16,6272]{2,1,0:T(8,128)(2,1)S(1)}, u32[]{:S(2)}, u32[]{:S(2)}) %all-to-all-start) | async-done | bytes 1605664 | tf_op jit(solution)/shard_map/all_to_all | solution.py:386
  41.1 0.0 copy-start
  41.1 0.0 copy-done.1
  41.1 0.0 copy-done.2
  41.1 1.0 shard_map.103
  42.1 58.4 %all_to_all.42 = bf16[16,128,768]{2,1,0:T(8,128)(2,1)} all-to-all(bf16[16,128,768]{2,1,0:T(8,128)(2,1)S(1)} %shard_map.103), channel_id=1, replica_groups=mesh['half'=2,'sub'=16,'dp'=8] {'sub'}, dimensions={0} | all-to-all | bytes 6291456 | tf_op jit(solution)/shard_map/all_to_all | solution.py:386
  100.5 0.0 copy-done
  100.5 4.3 %all-to-all-start.3 = ((bf16[8,16,4096]{2,1,0:T(8,128)(2,1)}), bf16[8,16,4096]{2,1,0:T(8,128)(2,1)}, u32[]{:S(2)}, u32[]{:S(2)}) async-start(bf16[8,16,4096]{2,1,0:T(8,128)(2,1)} %bitcast.15), calls=%async_computation.3 | async-start | bytes 2097152 | tf_op jit(solution)/shard_map/all_to_all | solution.py:386
  104.8 0.2 select_reduce_fusion
  104.9 0.5 fusion.3
  105.5 29.4 %shard_map.104 = bf16[2048,768]{1,0:T(8,128)(2,1)} custom-call(s32[8]{0:T(128)} %get-tuple-element.21.start_ref, s32[8]{0:T(128)} %get-tuple-element.20.end_ref, bf16[2048,768]{1,0:T(8,128)(2,1)} %bitcast.35, bf16[2048,768]{1,0:T(8,128)(2,1)} %bitcast.36, bf16[2048,768]{1,0:T(8,128)(2,1)} %bitcast.37), custom_call_target="tpu_custom_call" | custom-call | flops 8053063680 | bytes 6291456 | tf_op jit(solution)/shard_map/pallas_call | solution.py:286
  134.9 0.0 all-to-all-done.3
  134.9 4.9 %all-to-all-start.2 = ((bf16[16,128,768]{2,1,0:T(8,128)(2,1)}), bf16[16,128,768]{2,1,0:T(8,128)(2,1)S(1)}, u32[]{:S(2)}, u32[]{:S(2)}) async-start(bf16[16,128,768]{2,1,0:T(8,128)(2,1)} %bitcast.38), calls=%async_computation.2 | async-start | bytes 6291456 | tf_op jit(solution)/shard_map/all_to_all | solution.py:386
  139.8 0.8 slice.4.low_ref
  140.6 38.7 %all-to-all-done.2.came_ref = bf16[16,128,768]{2,1,0:T(8,128)(2,1)S(1)} async-done(((bf16[16,128,768]{2,1,0:T(8,128)(2,1)}), bf16[16,128,768]{2,1,0:T(8,128)(2,1)S(1)}, u32[]{:S(2)}, u32[]{:S(2)}) %all-to-all-start.2) | async-done | bytes 3145760 | tf_op jit(solution)/shard_map/all_to_all | solution.py:386
  179.3 1.6 shard_map.106
  180.9 17.5 %all_to_all.43 = bf16[16,32,256]{2,1,0:T(8,128)(2,1)S(1)} all-to-all(bf16[16,32,256]{2,1,0:T(8,128)(2,1)S(1)} %shard_map.106), channel_id=1, replica_groups=mesh['half'=2,'sub'=16,'dp'=8] {'sub'}, dimensions={0} | all-to-all | bytes 524288 | tf_op jit(solution)/shard_map/all_to_all | solution.py:386
  198.4 0.1 collective-permute-start
  198.5 3.7 %collective-permute-done = f32[32,256]{1,0:T(8,128)S(1)} collective-permute-done((f32[32,256]{1,0:T(8,128)S(1)}, f32[32,256]{1,0:T(8,128)S(1)}, u32[]{:S(2)}, u32[]{:S(2)}) %collective-permute-start) | collective-permute-done | bytes 32800 | tf_op jit(solution)/shard_map/ppermute | solution.py:482
  202.2 1.8 collective-permute-start.1
  203.9 1.3 collective-permute-done.1
  205.2 1.6 collective-permute-start.2
  206.8 2.7 %collective-permute-done.2 = f32[32,256]{1,0:T(8,128)S(1)} collective-permute-done((f32[32,256]{1,0:T(8,128)S(1)}, f32[32,256]{1,0:T(8,128)S(1)}, u32[]{:S(2)}, u32[]{:S(2)}) %collective-permute-start.2) | collective-permute-done | bytes 32800 | tf_op jit(solution)/shard_map/ppermute | solution.py:482
  209.5 5.4 %collective-permute-start.3 = (f32[32,256]{1,0:T(8,128)S(1)}, f32[32,256]{1,0:T(8,128)S(1)}, u32[]{:S(2)}, u32[]{:S(2)}) collective-permute-start(f32[32,256]{1,0:T(8,128)S(1)} %add.60), channel_id=1, source_target_pairs={{0,4},{1,5},{2,6},{3,7},{4,0},{5,1},{6,2},{7,3},{8,12},{9,13},{10,... | collective-permute-start | bytes 98312 | tf_op jit(solution)/shard_map/ppermute | solution.py:482
  214.9 1.3 collective-permute-done.3
  216.2 0.7 broadcast_in_dim.52
  216.9 9.0 %all-to-all-start.5 = ((bf16[16,32,256]{2,1,0:T(8,128)(2,1)}), bf16[16,32,256]{2,1,0:T(8,128)(2,1)S(1)}, u32[]{:S(2)}, u32[]{:S(2)}) async-start(bf16[16,32,256]{2,1,0:T(8,128)(2,1)} %broadcast_in_dim.52), calls=%async_computation.5 | async-start | bytes 524288 | tf_op jit(solution)/shard_map/all_to_all | solution.py:386
  225.9 2.2 shard_map.105
  228.1 5.0 %all-to-all-done.5.whole_ref = bf16[16,32,256]{2,1,0:T(8,128)(2,1)S(1)} async-done(((bf16[16,32,256]{2,1,0:T(8,128)(2,1)}), bf16[16,32,256]{2,1,0:T(8,128)(2,1)S(1)}, u32[]{:S(2)}, u32[]{:S(2)}) %all-to-all-start.5) | async-done | bytes 262176 | tf_op jit(solution)/shard_map/all_to_all | solution.py:386
  233.1 0.8 shard_map.107
  (8 shorter events, 0.1 us)
Async XLA Ops:
  0.6 14.9 %copy-start.4 = (s32[1,5]{1,0:T(1,128)S(1)}, s32[1,5]{1,0:T(1,128)}, u32[]{:S(2)}) copy-start(s32[1,5]{1,0:T(1,128)} %param.12) | copy-start | bytes 64
  0.6 15.0 %copy-start.3 = (s32[1,5]{1,0:T(1,128)S(1)}, s32[1,5]{1,0:T(1,128)}, u32[]{:S(2)}) copy-start(s32[1,5]{1,0:T(1,128)} %param.11) | copy-start | bytes 64
  0.7 40.5 %copy-start.1 = (bf16[1,128,4096]{2,1,0:T(8,128)(2,1)S(1)}, bf16[1,128,4096]{2,1,0:T(8,128)(2,1)}, u32[]{:S(2)}) copy-start(bf16[1,128,4096]{2,1,0:T(8,128)(2,1)} %param.13) | copy-start | bytes 3145732
  0.7 40.5 %copy-start.2 = (bf16[16,4096]{1,0:T(8,128)(2,1)S(1)}, bf16[16,4096]{1,0:T(8,128)(2,1)}, u32[]{:S(2)}) copy-start(bf16[16,4096]{1,0:T(8,128)(2,1)} %up_ref.3) | copy-start | bytes 393220
  3.8 37.3 %all-to-all-start = ((bf16[8,16,6272]{2,1,0:T(8,128)(2,1)}), bf16[8,16,6272]{2,1,0:T(8,128)(2,1)S(1)}, u32[]{:S(2)}, u32[]{:S(2)}) async-start(bf16[8,16,6272]{2,1,0:T(8,128)(2,1)} %bitcast.34), calls=%async_computation | async-start | bytes 3211264 | tf_op jit(solution)/shard_map/all_to_all | solution.py:386
  41.1 59.4 %copy-start = (bf16[8,16,6272]{2,1,0:T(8,128)(2,1)}, bf16[8,16,6272]{2,1,0:T(8,128)(2,1)S(1)}, u32[]{:S(2)}) copy-start(bf16[8,16,6272]{2,1,0:T(8,128)(2,1)S(1)} %all-to-all-done) | copy-start | bytes 4816900
  100.5 34.4 %all-to-all-start.3 = ((bf16[8,16,4096]{2,1,0:T(8,128)(2,1)}), bf16[8,16,4096]{2,1,0:T(8,128)(2,1)}, u32[]{:S(2)}, u32[]{:S(2)}) async-start(bf16[8,16,4096]{2,1,0:T(8,128)(2,1)} %bitcast.15), calls=%async_computation.3 | async-start | bytes 2097152 | tf_op jit(solution)/shard_map/all_to_all | solution.py:386
  134.9 44.4 %all-to-all-start.2 = ((bf16[16,128,768]{2,1,0:T(8,128)(2,1)}), bf16[16,128,768]{2,1,0:T(8,128)(2,1)S(1)}, u32[]{:S(2)}, u32[]{:S(2)}) async-start(bf16[16,128,768]{2,1,0:T(8,128)(2,1)} %bitcast.38), calls=%async_computation.2 | async-start | bytes 6291456 | tf_op jit(solution)/shard_map/all_to_all | solution.py:386
  198.4 3.8 %collective-permute-start = (f32[32,256]{1,0:T(8,128)S(1)}, f32[32,256]{1,0:T(8,128)S(1)}, u32[]{:S(2)}, u32[]{:S(2)}) collective-permute-start(f32[32,256]{1,0:T(8,128)S(1)} %convert_reduce_fusion), channel_id=1, source_target_pairs={{0,128},{128,0},{1,129},{129,1},{2,130},{130,2},{3,131},{131,3},{4... | collective-permute-start | bytes 98312 | tf_op jit(solution)/shard_map/ppermute | solution.py:482
  202.2 3.1 %collective-permute-start.1 = (f32[32,256]{1,0:T(8,128)S(1)}, f32[32,256]{1,0:T(8,128)S(1)}, u32[]{:S(2)}, u32[]{:S(2)}) collective-permute-start(f32[32,256]{1,0:T(8,128)S(1)} %add.58), channel_id=1, source_target_pairs={{0,1},{1,0},{2,3},{3,2},{4,5},{5,4},{6,7},{7,6},{8,9},{9,8},{10,11... | collective-permute-start | bytes 98312 | tf_op jit(solution)/shard_map/ppermute | solution.py:482
  205.2 4.3 %collective-permute-start.2 = (f32[32,256]{1,0:T(8,128)S(1)}, f32[32,256]{1,0:T(8,128)S(1)}, u32[]{:S(2)}, u32[]{:S(2)}) collective-permute-start(f32[32,256]{1,0:T(8,128)S(1)} %add.59), channel_id=1, source_target_pairs={{0,2},{1,3},{2,0},{3,1},{4,6},{5,7},{6,4},{7,5},{8,10},{9,11},{10,... | collective-permute-start | bytes 98312 | tf_op jit(solution)/shard_map/ppermute | solution.py:482
  209.5 6.7 %collective-permute-start.3 = (f32[32,256]{1,0:T(8,128)S(1)}, f32[32,256]{1,0:T(8,128)S(1)}, u32[]{:S(2)}, u32[]{:S(2)}) collective-permute-start(f32[32,256]{1,0:T(8,128)S(1)} %add.60), channel_id=1, source_target_pairs={{0,4},{1,5},{2,6},{3,7},{4,0},{5,1},{6,2},{7,3},{8,12},{9,13},{10,... | collective-permute-start | bytes 98312 | tf_op jit(solution)/shard_map/ppermute | solution.py:482
  216.9 16.2 %all-to-all-start.5 = ((bf16[16,32,256]{2,1,0:T(8,128)(2,1)}), bf16[16,32,256]{2,1,0:T(8,128)(2,1)S(1)}, u32[]{:S(2)}, u32[]{:S(2)}) async-start(bf16[16,32,256]{2,1,0:T(8,128)(2,1)} %broadcast_in_dim.52), calls=%async_computation.5 | async-start | bytes 524288 | tf_op jit(solution)/shard_map/all_to_all | solution.py:386

commit v8 on v7

--- a/solution.py
+++ b/solution.py
@@ -13,6 +13,7 @@
 PART = 256
 BLOCK = 512
 PAIR = 2 * HEAD_DIM
+PIECE_IN = 2 * PAIR + HEAD_DIM
 PIECE = 2 * PAIR + 2 * HEAD_DIM
 rope_base = 500000.0
 VMEM_BYTES = 48 * 1024 * 1024
@@ -100,13 +101,29 @@
         at = queries + key_head * HEAD_DIM
         keys = rotated(qkv_ref[:, at : at + HEAD_DIM].astype(F32), cosine, sine).astype(BF16)
         values = qkv_ref[:, at + kv_width : at + kv_width + HEAD_DIM]
-        for piece in (2 * key_head, 2 * key_head + 1):
-            out_ref[piece, :, 2 * PAIR : 2 * PAIR + HEAD_DIM] = keys
-            out_ref[piece, :, 2 * PAIR + HEAD_DIM :] = values
+        out_ref[2 * key_head, :, 2 * PAIR :] = keys
+        out_ref[2 * key_head + 1, :, 2 * PAIR :] = values
 
 
 def attention_kernel(
-    start_ref, end_ref, q_ref, g_ref, kv_ref, out_ref, kt, vt, dkt, dvt, store0, store1, held, tail, sems
+    start_ref,
+    end_ref,
+    side_ref,
+    q_ref,
+    g_ref,
+    mine_ref,
+    other_ref,
+    out_ref,
+    kv_ref,
+    kt,
+    vt,
+    dkt,
+    dvt,
+    store0,
+    store1,
+    held,
+    tail,
+    sems,
 ):
     store = (store0, store1)
     step = pl.program_id(0)
@@ -115,12 +132,25 @@
     exponent = factor * math.log2(math.e)
     parts = BLOCK // PART
 
+    def place(keys_ref, values_ref):
+        for tile in range(blocks):
+            rows = slice(tile * BLOCK, (tile + 1) * BLOCK)
+            keys, values = keys_ref[rows], values_ref[rows]
+            kv_ref[rows, :HEAD_DIM] = keys
+            kv_ref[rows, HEAD_DIM:] = values
+            kt[tile] = keys.T
+            vt[tile] = values.T
+
+    @pl.when((step == 0) & (side_ref[0] == 0))
+    def _():
+        place(mine_ref, other_ref)
+
+    @pl.when((step == 0) & (side_ref[0] == 1))
+    def _():
+        place(other_ref, mine_ref)
+
     @pl.when(step == 0)
     def _():
-        for tile in range(blocks):
-            rows = slice(tile * BLOCK, (tile + 1) * BLOCK)
-            kt[tile] = kv_ref[rows, :HEAD_DIM].T
-            vt[tile] = kv_ref[rows, HEAD_DIM:].T
         dkt[...] = jnp.zeros_like(dkt)
         dvt[...] = jnp.zeros_like(dvt)
 
@@ -279,23 +309,25 @@
         last.wait()
 
 
-def attention(table, starts, ends):
-    rows, width = table.shape
+def attention(table, other, starts, ends, side):
+    rows, width = table.shape[0], PIECE
     blocks = rows // BLOCK
     tiles = blocks * (blocks + 1) // 2
     return pl.pallas_call(
         attention_kernel,
         out_shape=pltpu.HBM((rows, width), BF16),
         grid_spec=pltpu.PrefetchScalarGridSpec(
-            num_scalar_prefetch=2,
+            num_scalar_prefetch=3,
             grid=(blocks,),
             in_specs=[
                 pl.BlockSpec((BLOCK, PAIR), lambda i, *_: (i, 0)),
                 pl.BlockSpec((BLOCK, PAIR), lambda i, *_: (i, 1)),
-                pl.BlockSpec((rows, PAIR), lambda i, *_: (0, 2)),
+                pl.BlockSpec((rows, HEAD_DIM), lambda i, *_: (0, 2 * PAIR // HEAD_DIM)),
+                pl.BlockSpec((rows, HEAD_DIM), lambda i, *_: (0, 0)),
             ],
             out_specs=pl.BlockSpec(memory_space=pl.ANY),
             scratch_shapes=[
+                pltpu.VMEM((rows, PAIR), BF16),
                 pltpu.VMEM((blocks, HEAD_DIM, BLOCK), BF16),
                 pltpu.VMEM((blocks, HEAD_DIM, BLOCK), BF16),
                 pltpu.VMEM((blocks, HEAD_DIM, BLOCK), F32),
@@ -313,7 +345,7 @@
             bytes_accessed=4 * rows * width,
             transcendentals=tiles * 2 * BLOCK * BLOCK,
         ),
-    )(starts, ends, table, table, table)
+    )(starts, ends, side, table, table, table, other)
 
 
 def unrotated_pair(came_ref, piece, cosine, sine):
@@ -445,13 +477,15 @@
     params = pltpu.CompilerParams(vmem_limit_bytes=VMEM_BYTES)
     pieces = pl.pallas_call(
         prepare_kernel,
-        out_shape=jax.ShapeDtypeStruct((members, token_count, PIECE), BF16),
+        out_shape=jax.ShapeDtypeStruct((members, token_count, PIECE_IN), BF16),
         compiler_params=params,
     )(packed_qkv, adapter_up, cosine, sine, grad_raw, row_valid)
-    table = in_hbm(exchange(pieces, "sub").reshape(members * token_count, PIECE))
+    table = exchange(pieces, "sub").reshape(members * token_count, PIECE_IN)
     table, x_held = lax.optimization_barrier((table, x_local))
     packed_inputs = in_hbm(exchange(x_held, "dp"))
-    results = attention(table, starts, ends)
+    other = lax.ppermute(table[:, 2 * PAIR :], "sub", [(i, i ^ 1) for i in range(members)])
+    side = lax.axis_index("sub").astype(jnp.int32).reshape(1) % 2
+    results = attention(in_hbm(table), other, starts, ends, side)
     came = exchange(results.reshape(members, token_count, PIECE), "sub")
     terms = pl.pallas_call(
         query_kernel,

time: 235 us -> 233 us (level)
  blocking collectives: 75.9 us -> 70.2 us
    all_to_all x2, blocking collectives: 75.9 us -> 70.2 us  [exchange(): return lax.all_to_all(table, axis, split_axis=0, concat_axis=0, tiled=True)]
  transfers between devices with their start and end apart: 8 -> 9, of which waited for: 7 -> 8; matrix products, arithmetic and copies ran while one was open for 1% -> 2% of each run, Pallas kernels for 14% -> 14%
where the time goes in v8:
time: 233 us; the launch traced here: 232 us
  waiting for transfers between devices  77.4 us (33%)
  blocking collectives  70.2 us (30%)
  starting transfers between devices  38.4 us (16%)
  Pallas kernels  38.1 us (16%)
  local copies, waits for them, and re-layouts  3.59 us (2%)
  other arithmetic  2.68 us (1%)
    all_to_all x2, blocking collectives, exchange(): return lax.all_to_all(table, axis, split_axis=0, concat_axis=0, tiled=True)  70.2 us
    all_to_all x4, waiting for transfers between devices, exchange(): return lax.all_to_all(table, axis, split_axis=0, concat_axis=0, tiled=True)  66.8 us
    pallas_call x1, Pallas kernels, attention(): pl.pallas_call(attention_kernel, out_shape=pltpu.HBM((rows, width), BF16)...  29.4 us
    all_to_all x4, starting transfers between devices, exchange(): return lax.all_to_all(table, axis, split_axis=0, concat_axis=0, tiled=True)  28.9 us
    ppermute x4, waiting for transfers between devices, local(): lax.ppermute(total, axis, [(i, i ^ apart) for i in range(size)])  9.83 us
    ppermute x4, starting transfers between devices, local(): lax.ppermute(total, axis, [(i, i ^ apart) for i in range(size)])  7.9 us
  transfers between devices with their start and end apart: 9, of which 8 were waited for; matrix products, arithmetic and copies ran while one was open for 2% of the time, Pallas kernels for 14%

profile of v8, /device:TPU:1, one launch (start us, length us, event | category | flops | bytes accessed | tf_op | source)
XLA Modules:
  0.0 231.8 jit_solution(2354364560174085815)
XLA Ops:
  0.6 3.1 %shard_map.102 = bf16[128,6272]{1,0:T(8,128)(2,1)} custom-call(bf16[128,4096]{1,0:T(8,128)(2,1)} %bitcast.6.inputs_ref, bf16[16,4096]{1,0:T(8,128)(2,1)} %bitcast.42, bf16[128,6144]{1,0:T(8,128)(2,1)} %bitcast.41), custom_call_target="tpu_custom_call" | custom-call | tf_op jit(solution)/shard_map/pallas_call | solution.py:437
  3.7 0.0 copy-start.4
  3.7 0.0 copy-start.3
  3.7 0.0 copy-start.1
  3.8 0.0 copy-start.2
  3.8 11.8 %all-to-all-start = ((bf16[8,16,6272]{2,1,0:T(8,128)(2,1)}), bf16[8,16,6272]{2,1,0:T(8,128)(2,1)S(1)}, u32[]{:S(2)}, u32[]{:S(2)}) async-start(bf16[8,16,6272]{2,1,0:T(8,128)(2,1)} %bitcast.35), calls=%async_computation | async-start | bytes 3211264 | tf_op jit(solution)/shard_map/all_to_all | solution.py:418
  15.6 0.0 copy-done.4
  15.6 0.2 reduce-window.4
  15.7 0.0 copy-done.3
  15.7 0.6 select_reduce_fusion.2
  17.1 0.7 fusion.valid_ref
  17.7 0.3 fusion.1
  18.0 0.1 pad_maximum_fusion
  18.1 23.0 %all-to-all-done = bf16[8,16,6272]{2,1,0:T(8,128)(2,1)S(1)} async-done(((bf16[8,16,6272]{2,1,0:T(8,128)(2,1)}), bf16[8,16,6272]{2,1,0:T(8,128)(2,1)S(1)}, u32[]{:S(2)}, u32[]{:S(2)}) %all-to-all-start) | async-done | bytes 1605664 | tf_op jit(solution)/shard_map/all_to_all | solution.py:418
  41.2 0.0 copy-start
  41.2 0.0 copy-done.1
  41.2 0.0 copy-done.2
  41.2 1.0 shard_map.103
  42.2 0.2 copy-done
  42.4 52.7 %all_to_all.42 = bf16[16,128,640]{2,1,0:T(8,128)(2,1)} all-to-all(bf16[16,128,640]{2,1,0:T(8,128)(2,1)S(1)} %shard_map.103), channel_id=1, replica_groups=mesh['half'=2,'sub'=16,'dp'=8] {'sub'}, dimensions={0} | all-to-all | bytes 5242880 | tf_op jit(solution)/shard_map/all_to_all | solution.py:418
  95.1 4.3 %all-to-all-start.3 = ((bf16[8,16,4096]{2,1,0:T(8,128)(2,1)}), bf16[8,16,4096]{2,1,0:T(8,128)(2,1)}, u32[]{:S(2)}, u32[]{:S(2)}) async-start(bf16[8,16,4096]{2,1,0:T(8,128)(2,1)} %bitcast.16), calls=%async_computation.3 | async-start | bytes 2097152 | tf_op jit(solution)/shard_map/all_to_all | solution.py:418
  99.3 1.1 slice.6
  100.4 1.5 collective-permute-start
  102.0 0.2 select_reduce_fusion
  102.1 0.5 fusion.3
  102.7 0.8 collective-permute-done.other_ref
  103.5 0.0 copy-start.5
  103.5 0.8 copy-done.5
  104.3 29.4 %shard_map.104 = bf16[2048,768]{1,0:T(8,128)(2,1)} custom-call(s32[8]{0:T(128)} %get-tuple-element.21.start_ref, s32[8]{0:T(128)} %get-tuple-element.20.end_ref, s32[1]{0:T(128)S(6)} %select_n.25.side_ref, bf16[2048,640]{1,0:T(8,128)(2,1)} %bitcast.37, bf16[2048,640]{1,0:T(8,128)(2,1)} %bitcast.38, bf16[2048,640]{1,0:T(8,128)(2,1)} %bitcast.39, ...), custom_call_target="tpu_custom_call" | custom-call | flops 8053063680 | bytes 6291456 | tf_op jit(solution)/shard_map/pallas_call | solution.py:316
  133.7 0.0 all-to-all-done.3
  133.8 3.9 %all-to-all-start.2 = ((bf16[16,128,768]{2,1,0:T(8,128)(2,1)}), bf16[16,128,768]{2,1,0:T(8,128)(2,1)S(1)}, u32[]{:S(2)}, u32[]{:S(2)}) async-start(bf16[16,128,768]{2,1,0:T(8,128)(2,1)} %bitcast.40), calls=%async_computation.2 | async-start | bytes 6291456 | tf_op jit(solution)/shard_map/all_to_all | solution.py:418
  137.7 0.8 slice.8.low_ref
  138.4 38.7 %all-to-all-done.2.came_ref = bf16[16,128,768]{2,1,0:T(8,128)(2,1)S(1)} async-done(((bf16[16,128,768]{2,1,0:T(8,128)(2,1)}), bf16[16,128,768]{2,1,0:T(8,128)(2,1)S(1)}, u32[]{:S(2)}, u32[]{:S(2)}) %all-to-all-start.2) | async-done | bytes 3145760 | tf_op jit(solution)/shard_map/all_to_all | solution.py:418
  177.1 1.6 shard_map.106
  178.7 17.5 %all_to_all.43 = bf16[16,32,256]{2,1,0:T(8,128)(2,1)S(1)} all-to-all(bf16[16,32,256]{2,1,0:T(8,128)(2,1)S(1)} %shard_map.106), channel_id=1, replica_groups=mesh['half'=2,'sub'=16,'dp'=8] {'sub'}, dimensions={0} | all-to-all | bytes 524288 | tf_op jit(solution)/shard_map/all_to_all | solution.py:418
  196.3 0.1 collective-permute-start.1
  196.4 3.7 %collective-permute-done.1 = f32[32,256]{1,0:T(8,128)S(1)} collective-permute-done((f32[32,256]{1,0:T(8,128)S(1)}, f32[32,256]{1,0:T(8,128)S(1)}, u32[]{:S(2)}, u32[]{:S(2)}) %collective-permute-start.1) | collective-permute-done | bytes 32800 | tf_op jit(solution)/shard_map/ppermute | solution.py:516
  200.1 0.3 collective-permute-start.2
  200.4 2.4 %collective-permute-done.2 = f32[32,256]{1,0:T(8,128)S(1)} collective-permute-done((f32[32,256]{1,0:T(8,128)S(1)}, f32[32,256]{1,0:T(8,128)S(1)}, u32[]{:S(2)}, u32[]{:S(2)}) %collective-permute-start.2) | collective-permute-done | bytes 32800 | tf_op jit(solution)/shard_map/ppermute | solution.py:516
  202.8 1.8 collective-permute-start.3
  204.7 2.4 %collective-permute-done.3 = f32[32,256]{1,0:T(8,128)S(1)} collective-permute-done((f32[32,256]{1,0:T(8,128)S(1)}, f32[32,256]{1,0:T(8,128)S(1)}, u32[]{:S(2)}, u32[]{:S(2)}) %collective-permute-start.3) | collective-permute-done | bytes 32800 | tf_op jit(solution)/shard_map/ppermute | solution.py:516
  207.1 5.7 %collective-permute-start.4 = (f32[32,256]{1,0:T(8,128)S(1)}, f32[32,256]{1,0:T(8,128)S(1)}, u32[]{:S(2)}, u32[]{:S(2)}) collective-permute-start(f32[32,256]{1,0:T(8,128)S(1)} %add.67), channel_id=1, source_target_pairs={{0,4},{1,5},{2,6},{3,7},{4,0},{5,1},{6,2},{7,3},{8,12},{9,13},{10,... | collective-permute-start | bytes 98312 | tf_op jit(solution)/shard_map/ppermute | solution.py:516
  212.7 1.3 collective-permute-done.4
  214.1 0.7 broadcast_in_dim.52
  214.8 9.0 %all-to-all-start.5 = ((bf16[16,32,256]{2,1,0:T(8,128)(2,1)}), bf16[16,32,256]{2,1,0:T(8,128)(2,1)S(1)}, u32[]{:S(2)}, u32[]{:S(2)}) async-start(bf16[16,32,256]{2,1,0:T(8,128)(2,1)} %broadcast_in_dim.52), calls=%async_computation.5 | async-start | bytes 524288 | tf_op jit(solution)/shard_map/all_to_all | solution.py:418
  223.8 2.2 shard_map.105
  226.0 5.0 %all-to-all-done.5.whole_ref = bf16[16,32,256]{2,1,0:T(8,128)(2,1)S(1)} async-done(((bf16[16,32,256]{2,1,0:T(8,128)(2,1)}), bf16[16,32,256]{2,1,0:T(8,128)(2,1)S(1)}, u32[]{:S(2)}, u32[]{:S(2)}) %all-to-all-start.5) | async-done | bytes 262176 | tf_op jit(solution)/shard_map/all_to_all | solution.py:418
  231.0 0.8 shard_map.107
  (8 shorter events, 0.1 us)
Async XLA Ops:
  3.7 11.8 %copy-start.4 = (s32[1,5]{1,0:T(1,128)S(1)}, s32[1,5]{1,0:T(1,128)}, u32[]{:S(2)}) copy-start(s32[1,5]{1,0:T(1,128)} %param.12) | copy-start | bytes 64
  3.7 12.0 %copy-start.3 = (s32[1,5]{1,0:T(1,128)S(1)}, s32[1,5]{1,0:T(1,128)}, u32[]{:S(2)}) copy-start(s32[1,5]{1,0:T(1,128)} %param.11) | copy-start | bytes 64
  3.7 37.5 %copy-start.1 = (bf16[1,128,4096]{2,1,0:T(8,128)(2,1)S(1)}, bf16[1,128,4096]{2,1,0:T(8,128)(2,1)}, u32[]{:S(2)}) copy-start(bf16[1,128,4096]{2,1,0:T(8,128)(2,1)} %param.13) | copy-start | bytes 3145732
  3.8 37.4 %copy-start.2 = (bf16[16,4096]{1,0:T(8,128)(2,1)S(1)}, bf16[16,4096]{1,0:T(8,128)(2,1)}, u32[]{:S(2)}) copy-start(bf16[16,4096]{1,0:T(8,128)(2,1)} %up_ref.3) | copy-start | bytes 393220
  3.8 37.4 %all-to-all-start = ((bf16[8,16,6272]{2,1,0:T(8,128)(2,1)}), bf16[8,16,6272]{2,1,0:T(8,128)(2,1)S(1)}, u32[]{:S(2)}, u32[]{:S(2)}) async-start(bf16[8,16,6272]{2,1,0:T(8,128)(2,1)} %bitcast.35), calls=%async_computation | async-start | bytes 3211264 | tf_op jit(solution)/shard_map/all_to_all | solution.py:418
  41.2 1.2 copy-start
  95.1 38.7 %all-to-all-start.3 = ((bf16[8,16,4096]{2,1,0:T(8,128)(2,1)}), bf16[8,16,4096]{2,1,0:T(8,128)(2,1)}, u32[]{:S(2)}, u32[]{:S(2)}) async-start(bf16[8,16,4096]{2,1,0:T(8,128)(2,1)} %bitcast.16), calls=%async_computation.3 | async-start | bytes 2097152 | tf_op jit(solution)/shard_map/all_to_all | solution.py:418
  100.4 3.1 %collective-permute-start = (bf16[2048,128]{1,0:T(8,128)(2,1)S(1)}, bf16[2048,128]{1,0:T(8,128)(2,1)S(1)}, u32[]{:S(2)}, u32[]{:S(2)}) collective-permute-start(bf16[2048,128]{1,0:T(8,128)(2,1)S(1)} %slice.6), channel_id=1, source_target_pairs={{0,8},{8,0},{16,24},{24,16},{32,40},{40,32},{48,56},{56,48},{64,72... | collective-permute-start | bytes 1572872 | tf_op jit(solution)/shard_map/ppermute | solution.py:486
  103.5 0.8 copy-start.5
  133.8 43.4 %all-to-all-start.2 = ((bf16[16,128,768]{2,1,0:T(8,128)(2,1)}), bf16[16,128,768]{2,1,0:T(8,128)(2,1)S(1)}, u32[]{:S(2)}, u32[]{:S(2)}) async-start(bf16[16,128,768]{2,1,0:T(8,128)(2,1)} %bitcast.40), calls=%async_computation.2 | async-start | bytes 6291456 | tf_op jit(solution)/shard_map/all_to_all | solution.py:418
  196.3 3.8 %collective-permute-start.1 = (f32[32,256]{1,0:T(8,128)S(1)}, f32[32,256]{1,0:T(8,128)S(1)}, u32[]{:S(2)}, u32[]{:S(2)}) collective-permute-start(f32[32,256]{1,0:T(8,128)S(1)} %convert_reduce_fusion), channel_id=1, source_target_pairs={{0,128},{128,0},{1,129},{129,1},{2,130},{130,2},{3,131},{131,3},{4... | collective-permute-start | bytes 98312 | tf_op jit(solution)/shard_map/ppermute | solution.py:516
  200.1 2.8 %collective-permute-start.2 = (f32[32,256]{1,0:T(8,128)S(1)}, f32[32,256]{1,0:T(8,128)S(1)}, u32[]{:S(2)}, u32[]{:S(2)}) collective-permute-start(f32[32,256]{1,0:T(8,128)S(1)} %add.65), channel_id=1, source_target_pairs={{0,1},{1,0},{2,3},{3,2},{4,5},{5,4},{6,7},{7,6},{8,9},{9,8},{10,11... | collective-permute-start | bytes 98312 | tf_op jit(solution)/shard_map/ppermute | solution.py:516
  202.8 4.3 %collective-permute-start.3 = (f32[32,256]{1,0:T(8,128)S(1)}, f32[32,256]{1,0:T(8,128)S(1)}, u32[]{:S(2)}, u32[]{:S(2)}) collective-permute-start(f32[32,256]{1,0:T(8,128)S(1)} %add.66), channel_id=1, source_target_pairs={{0,2},{1,3},{2,0},{3,1},{4,6},{5,7},{6,4},{7,5},{8,10},{9,11},{10,... | collective-permute-start | bytes 98312 | tf_op jit(solution)/shard_map/ppermute | solution.py:516
  207.1 7.0 %collective-permute-start.4 = (f32[32,256]{1,0:T(8,128)S(1)}, f32[32,256]{1,0:T(8,128)S(1)}, u32[]{:S(2)}, u32[]{:S(2)}) collective-permute-start(f32[32,256]{1,0:T(8,128)S(1)} %add.67), channel_id=1, source_target_pairs={{0,4},{1,5},{2,6},{3,7},{4,0},{5,1},{6,2},{7,3},{8,12},{9,13},{10,... | collective-permute-start | bytes 98312 | tf_op jit(solution)/shard_map/ppermute | solution.py:516
  214.8 16.2 %all-to-all-start.5 = ((bf16[16,32,256]{2,1,0:T(8,128)(2,1)}), bf16[16,32,256]{2,1,0:T(8,128)(2,1)S(1)}, u32[]{:S(2)}, u32[]{:S(2)}) async-start(bf16[16,32,256]{2,1,0:T(8,128)(2,1)} %broadcast_in_dim.52), calls=%async_computation.5 | async-start | bytes 524288 | tf_op jit(solution)/shard_map/all_to_all | solution.py:418

commit v9 on v8

--- a/solution.py
+++ b/solution.py
@@ -17,7 +17,7 @@
 PIECE = 2 * PAIR + 2 * HEAD_DIM
 rope_base = 500000.0
 VMEM_BYTES = 48 * 1024 * 1024
-ATTENTION_VMEM_BYTES = 65024 * 1024
+ATTENTION_VMEM_BYTES = 64768 * 1024
 HIDDEN = -1e30
 CHUNKS = 4
 F32 = jnp.float32
@@ -481,9 +481,9 @@
         compiler_params=params,
     )(packed_qkv, adapter_up, cosine, sine, grad_raw, row_valid)
     table = exchange(pieces, "sub").reshape(members * token_count, PIECE_IN)
-    table, x_held = lax.optimization_barrier((table, x_local))
+    mine, x_held = lax.optimization_barrier((table[:, 2 * PAIR :], x_local))
     packed_inputs = in_hbm(exchange(x_held, "dp"))
-    other = lax.ppermute(table[:, 2 * PAIR :], "sub", [(i, i ^ 1) for i in range(members)])
+    other = lax.ppermute(mine, "sub", [(i, i ^ 1) for i in range(members)])
     side = lax.axis_index("sub").astype(jnp.int32).reshape(1) % 2
     results = attention(in_hbm(table), other, starts, ends, side)
     came = exchange(results.reshape(members, token_count, PIECE), "sub")

time: 233 us -> 233 us (level)
  starting transfers between devices: 38.4 us -> 56.5 us
  Pallas kernels: 38.1 us -> 23.6 us
  waiting for transfers between devices: 77.4 us -> 74.2 us
    pallas_call x1, Pallas kernels: 29.4 us -> 14.9 us  [attention(): pl.pallas_call(attention_kernel, out_shape=pltpu.HBM((rows, width), BF16)...]
    all_to_all x4, starting transfers between devices: 28.9 us -> 39.6 us  [exchange(): return lax.all_to_all(table, axis, split_axis=0, concat_axis=0, tiled=True)]
    ppermute x4, starting transfers between devices: 7.9 us -> 15.4 us  [local(): lax.ppermute(total, axis, [(i, i ^ apart) for i in range(size)])]
    ppermute x4, waiting for transfers between devices: 9.83 us -> 5.73 us  [local(): lax.ppermute(total, axis, [(i, i ^ apart) for i in range(size)])]
  transfers between devices with their start and end apart: 9 -> 9, of which waited for: 8 -> 8; matrix products, arithmetic and copies ran while one was open for 2% -> 1% of each run, Pallas kernels for 14% -> 7%
where the time goes in v9:
time: 233 us; the launch traced here: 232 us
  waiting for transfers between devices  74.2 us (32%)
  blocking collectives  69.7 us (30%)
  starting transfers between devices  56.5 us (24%)
  Pallas kernels  23.6 us (10%)
  local copies, waits for them, and re-layouts  4.07 us (2%)
  other arithmetic  2.68 us (1%)
    all_to_all x2, blocking collectives, exchange(): return lax.all_to_all(table, axis, split_axis=0, concat_axis=0, tiled=True)  69.7 us
    all_to_all x4, waiting for transfers between devices, exchange(): return lax.all_to_all(table, axis, split_axis=0, concat_axis=0, tiled=True)  67.7 us
    all_to_all x4, starting transfers between devices, exchange(): return lax.all_to_all(table, axis, split_axis=0, concat_axis=0, tiled=True)  39.6 us
    ppermute x4, starting transfers between devices, local(): lax.ppermute(total, axis, [(i, i ^ apart) for i in range(size)])  15.4 us
    pallas_call x1, Pallas kernels, attention(): pl.pallas_call(attention_kernel, out_shape=pltpu.HBM((rows, width), BF16)...  14.9 us
    ppermute x4, waiting for transfers between devices, local(): lax.ppermute(total, axis, [(i, i ^ apart) for i in range(size)])  5.73 us
  transfers between devices with their start and end apart: 9, of which 8 were waited for; matrix products, arithmetic and copies ran while one was open for 1% of the time, Pallas kernels for 7%

profile of v9, /device:TPU:1, one launch (start us, length us, event | category | flops | bytes accessed | tf_op | source)
XLA Modules:
  0.0 232.1 jit_solution(13198787494957982394)
XLA Ops:
  0.6 3.1 %shard_map.102 = bf16[128,6272]{1,0:T(8,128)(2,1)} custom-call(bf16[128,4096]{1,0:T(8,128)(2,1)} %bitcast.6.inputs_ref, bf16[16,4096]{1,0:T(8,128)(2,1)} %bitcast.42, bf16[128,6144]{1,0:T(8,128)(2,1)} %bitcast.41), custom_call_target="tpu_custom_call" | custom-call | tf_op jit(solution)/shard_map/pallas_call | solution.py:437
  3.7 0.0 copy-start.5
  3.7 0.0 copy-start.4
  3.7 0.0 copy-start.1
  3.7 0.0 copy-start.2
  3.7 11.8 %all-to-all-start = ((bf16[8,16,6272]{2,1,0:T(8,128)(2,1)}), bf16[8,16,6272]{2,1,0:T(8,128)(2,1)S(1)}, u32[]{:S(2)}, u32[]{:S(2)}) async-start(bf16[8,16,6272]{2,1,0:T(8,128)(2,1)} %bitcast.35), calls=%async_computation | async-start | bytes 3211264 | tf_op jit(solution)/shard_map/all_to_all | solution.py:418
  15.5 0.0 copy-done.5
  15.5 0.2 reduce-window.4
  15.7 0.0 copy-done.4
  15.7 0.6 select_reduce_fusion.2
  17.0 0.7 fusion.valid_ref
  17.7 0.3 fusion.1
  18.0 0.1 pad_maximum_fusion
  18.1 23.0 %all-to-all-done = bf16[8,16,6272]{2,1,0:T(8,128)(2,1)S(1)} async-done(((bf16[8,16,6272]{2,1,0:T(8,128)(2,1)}), bf16[8,16,6272]{2,1,0:T(8,128)(2,1)S(1)}, u32[]{:S(2)}, u32[]{:S(2)}) %all-to-all-start) | async-done | bytes 1605664 | tf_op jit(solution)/shard_map/all_to_all | solution.py:418
  41.2 0.0 copy-start
  41.2 0.0 copy-done.1
  41.2 0.0 copy-done.2
  41.2 1.0 shard_map.103
  42.1 0.2 copy-done
  42.3 52.6 %all_to_all.42 = bf16[16,128,640]{2,1,0:T(8,128)(2,1)S(1)} all-to-all(bf16[16,128,640]{2,1,0:T(8,128)(2,1)S(1)} %shard_map.103), channel_id=1, replica_groups=mesh['half'=2,'sub'=16,'dp'=8] {'sub'}, dimensions={0} | all-to-all | bytes 5242880 | tf_op jit(solution)/shard_map/all_to_all | solution.py:418
  95.0 0.0 copy-start.3
  95.0 1.5 copy-done.3
  96.5 4.3 %all-to-all-start.3 = ((bf16[8,16,4096]{2,1,0:T(8,128)(2,1)}), bf16[8,16,4096]{2,1,0:T(8,128)(2,1)}, u32[]{:S(2)}, u32[]{:S(2)}) async-start(bf16[8,16,4096]{2,1,0:T(8,128)(2,1)} %bitcast.16), calls=%async_computation.3 | async-start | bytes 2097152 | tf_op jit(solution)/shard_map/all_to_all | solution.py:418
  100.8 1.4 collective-permute-start
  102.2 0.2 select_reduce_fusion
  102.4 0.5 fusion.3
  103.0 0.8 collective-permute-done.other_ref
  103.8 0.8 copy-done.6
  104.6 14.9 %shard_map.104 = bf16[2048,768]{1,0:T(8,128)(2,1)} custom-call(s32[8]{0:T(128)} %get-tuple-element.21.start_ref, s32[8]{0:T(128)} %get-tuple-element.20.end_ref, s32[1]{0:T(128)S(6)} %select_n.25.side_ref, bf16[2048,640]{1,0:T(8,128)(2,1)} %bitcast.37, bf16[2048,640]{1,0:T(8,128)(2,1)} %bitcast.38, bf16[2048,640]{1,0:T(8,128)(2,1)} %bitcast.39, ...), custom_call_target="tpu_custom_call" | custom-call | flops 8053063680 | bytes 6291456 | tf_op jit(solution)/shard_map/pallas_call | solution.py:316
  119.5 0.0 all-to-all-done.3
  119.5 14.9 %all-to-all-start.2 = ((bf16[16,128,768]{2,1,0:T(8,128)(2,1)}), bf16[16,128,768]{2,1,0:T(8,128)(2,1)S(1)}, u32[]{:S(2)}, u32[]{:S(2)}) async-start(bf16[16,128,768]{2,1,0:T(8,128)(2,1)} %bitcast.40), calls=%async_computation.2 | async-start | bytes 6291456 | tf_op jit(solution)/shard_map/all_to_all | solution.py:418
  134.3 0.8 slice.9.low_ref
  135.1 39.6 %all-to-all-done.2.came_ref = bf16[16,128,768]{2,1,0:T(8,128)(2,1)S(1)} async-done(((bf16[16,128,768]{2,1,0:T(8,128)(2,1)}), bf16[16,128,768]{2,1,0:T(8,128)(2,1)S(1)}, u32[]{:S(2)}, u32[]{:S(2)}) %all-to-all-start.2) | async-done | bytes 3145760 | tf_op jit(solution)/shard_map/all_to_all | solution.py:418
  174.7 1.6 shard_map.106
  176.3 17.1 %all_to_all.43 = bf16[16,32,256]{2,1,0:T(8,128)(2,1)S(1)} all-to-all(bf16[16,32,256]{2,1,0:T(8,128)(2,1)S(1)} %shard_map.106), channel_id=1, replica_groups=mesh['half'=2,'sub'=16,'dp'=8] {'sub'}, dimensions={0} | all-to-all | bytes 524288 | tf_op jit(solution)/shard_map/all_to_all | solution.py:418
  193.4 4.2 %collective-permute-start.1 = (f32[32,256]{1,0:T(8,128)S(1)}, f32[32,256]{1,0:T(8,128)S(1)}, u32[]{:S(2)}, u32[]{:S(2)}) collective-permute-start(f32[32,256]{1,0:T(8,128)S(1)} %convert_reduce_fusion), channel_id=1, source_target_pairs={{0,128},{128,0},{1,129},{129,1},{2,130},{130,2},{3,131},{131,3},{4... | collective-permute-start | bytes 98312 | tf_op jit(solution)/shard_map/ppermute | solution.py:516
  197.6 1.3 collective-permute-done.1
  198.9 3.1 %collective-permute-start.2 = (f32[32,256]{1,0:T(8,128)S(1)}, f32[32,256]{1,0:T(8,128)S(1)}, u32[]{:S(2)}, u32[]{:S(2)}) collective-permute-start(f32[32,256]{1,0:T(8,128)S(1)} %add.65), channel_id=1, source_target_pairs={{0,1},{1,0},{2,3},{3,2},{4,5},{5,4},{6,7},{7,6},{8,9},{9,8},{10,11... | collective-permute-start | bytes 98312 | tf_op jit(solution)/shard_map/ppermute | solution.py:516
  202.1 1.3 collective-permute-done.2
  203.4 3.0 %collective-permute-start.3 = (f32[32,256]{1,0:T(8,128)S(1)}, f32[32,256]{1,0:T(8,128)S(1)}, u32[]{:S(2)}, u32[]{:S(2)}) collective-permute-start(f32[32,256]{1,0:T(8,128)S(1)} %add.66), channel_id=1, source_target_pairs={{0,2},{1,3},{2,0},{3,1},{4,6},{5,7},{6,4},{7,5},{8,10},{9,11},{10,... | collective-permute-start | bytes 98312 | tf_op jit(solution)/shard_map/ppermute | solution.py:516
  206.3 1.5 collective-permute-done.3
  207.9 5.1 %collective-permute-start.4 = (f32[32,256]{1,0:T(8,128)S(1)}, f32[32,256]{1,0:T(8,128)S(1)}, u32[]{:S(2)}, u32[]{:S(2)}) collective-permute-start(f32[32,256]{1,0:T(8,128)S(1)} %add.67), channel_id=1, source_target_pairs={{0,4},{1,5},{2,6},{3,7},{4,0},{5,1},{6,2},{7,3},{8,12},{9,13},{10,... | collective-permute-start | bytes 98312 | tf_op jit(solution)/shard_map/ppermute | solution.py:516
  213.0 1.6 collective-permute-done.4
  214.6 0.7 broadcast_in_dim.52
  215.3 8.7 %all-to-all-start.5 = ((bf16[16,32,256]{2,1,0:T(8,128)(2,1)}), bf16[16,32,256]{2,1,0:T(8,128)(2,1)S(1)}, u32[]{:S(2)}, u32[]{:S(2)}) async-start(bf16[16,32,256]{2,1,0:T(8,128)(2,1)} %broadcast_in_dim.52), calls=%async_computation.5 | async-start | bytes 524288 | tf_op jit(solution)/shard_map/all_to_all | solution.py:418
  224.0 2.2 shard_map.105
  226.2 5.0 %all-to-all-done.5.whole_ref = bf16[16,32,256]{2,1,0:T(8,128)(2,1)S(1)} async-done(((bf16[16,32,256]{2,1,0:T(8,128)(2,1)}), bf16[16,32,256]{2,1,0:T(8,128)(2,1)S(1)}, u32[]{:S(2)}, u32[]{:S(2)}) %all-to-all-start.5) | async-done | bytes 262176 | tf_op jit(solution)/shard_map/all_to_all | solution.py:418
  231.3 0.8 shard_map.107
  (10 shorter events, 0.1 us)
Async XLA Ops:
  3.7 11.8 %copy-start.5 = (s32[1,5]{1,0:T(1,128)S(1)}, s32[1,5]{1,0:T(1,128)}, u32[]{:S(2)}) copy-start(s32[1,5]{1,0:T(1,128)} %param.12) | copy-start | bytes 64
  3.7 12.0 %copy-start.4 = (s32[1,5]{1,0:T(1,128)S(1)}, s32[1,5]{1,0:T(1,128)}, u32[]{:S(2)}) copy-start(s32[1,5]{1,0:T(1,128)} %param.11) | copy-start | bytes 64
  3.7 37.5 %copy-start.1 = (bf16[1,128,4096]{2,1,0:T(8,128)(2,1)S(1)}, bf16[1,128,4096]{2,1,0:T(8,128)(2,1)}, u32[]{:S(2)}) copy-start(bf16[1,128,4096]{2,1,0:T(8,128)(2,1)} %param.13) | copy-start | bytes 3145732
  3.7 37.4 %copy-start.2 = (bf16[16,4096]{1,0:T(8,128)(2,1)S(1)}, bf16[16,4096]{1,0:T(8,128)(2,1)}, u32[]{:S(2)}) copy-start(bf16[16,4096]{1,0:T(8,128)(2,1)} %up_ref.3) | copy-start | bytes 393220
  3.7 37.4 %all-to-all-start = ((bf16[8,16,6272]{2,1,0:T(8,128)(2,1)}), bf16[8,16,6272]{2,1,0:T(8,128)(2,1)S(1)}, u32[]{:S(2)}, u32[]{:S(2)}) async-start(bf16[8,16,6272]{2,1,0:T(8,128)(2,1)} %bitcast.35), calls=%async_computation | async-start | bytes 3211264 | tf_op jit(solution)/shard_map/all_to_all | solution.py:418
  41.2 1.2 copy-start
  95.0 1.5 copy-start.3
  96.5 22.9 %all-to-all-start.3 = ((bf16[8,16,4096]{2,1,0:T(8,128)(2,1)}), bf16[8,16,4096]{2,1,0:T(8,128)(2,1)}, u32[]{:S(2)}, u32[]{:S(2)}) async-start(bf16[8,16,4096]{2,1,0:T(8,128)(2,1)} %bitcast.16), calls=%async_computation.3 | async-start | bytes 2097152 | tf_op jit(solution)/shard_map/all_to_all | solution.py:418
  100.8 3.0 %collective-permute-start = (bf16[2048,128]{1,0:T(8,128)(2,1)S(1)}, bf16[2048,128]{1,0:T(8,128)(2,1)S(1)}, u32[]{:S(2)}, u32[]{:S(2)}) collective-permute-start(bf16[2048,128]{1,0:T(8,128)(2,1)S(1)} %slice.8), channel_id=1, source_target_pairs={{0,8},{8,0},{16,24},{24,16},{32,40},{40,32},{48,56},{56,48},{64,72... | collective-permute-start | bytes 1572872 | tf_op jit(solution)/shard_map/ppermute | solution.py:486
  103.8 0.8 copy-start.6
  119.5 55.2 %all-to-all-start.2 = ((bf16[16,128,768]{2,1,0:T(8,128)(2,1)}), bf16[16,128,768]{2,1,0:T(8,128)(2,1)S(1)}, u32[]{:S(2)}, u32[]{:S(2)}) async-start(bf16[16,128,768]{2,1,0:T(8,128)(2,1)} %bitcast.40), calls=%async_computation.2 | async-start | bytes 6291456 | tf_op jit(solution)/shard_map/all_to_all | solution.py:418
  193.4 5.5 %collective-permute-start.1 = (f32[32,256]{1,0:T(8,128)S(1)}, f32[32,256]{1,0:T(8,128)S(1)}, u32[]{:S(2)}, u32[]{:S(2)}) collective-permute-start(f32[32,256]{1,0:T(8,128)S(1)} %convert_reduce_fusion), channel_id=1, source_target_pairs={{0,128},{128,0},{1,129},{129,1},{2,130},{130,2},{3,131},{131,3},{4... | collective-permute-start | bytes 98312 | tf_op jit(solution)/shard_map/ppermute | solution.py:516
  198.9 4.4 %collective-permute-start.2 = (f32[32,256]{1,0:T(8,128)S(1)}, f32[32,256]{1,0:T(8,128)S(1)}, u32[]{:S(2)}, u32[]{:S(2)}) collective-permute-start(f32[32,256]{1,0:T(8,128)S(1)} %add.65), channel_id=1, source_target_pairs={{0,1},{1,0},{2,3},{3,2},{4,5},{5,4},{6,7},{7,6},{8,9},{9,8},{10,11... | collective-permute-start | bytes 98312 | tf_op jit(solution)/shard_map/ppermute | solution.py:516
  203.4 4.5 %collective-permute-start.3 = (f32[32,256]{1,0:T(8,128)S(1)}, f32[32,256]{1,0:T(8,128)S(1)}, u32[]{:S(2)}, u32[]{:S(2)}) collective-permute-start(f32[32,256]{1,0:T(8,128)S(1)} %add.66), channel_id=1, source_target_pairs={{0,2},{1,3},{2,0},{3,1},{4,6},{5,7},{6,4},{7,5},{8,10},{9,11},{10,... | collective-permute-start | bytes 98312 | tf_op jit(solution)/shard_map/ppermute | solution.py:516
  207.9 6.7 %collective-permute-start.4 = (f32[32,256]{1,0:T(8,128)S(1)}, f32[32,256]{1,0:T(8,128)S(1)}, u32[]{:S(2)}, u32[]{:S(2)}) collective-permute-start(f32[32,256]{1,0:T(8,128)S(1)} %add.67), channel_id=1, source_target_pairs={{0,4},{1,5},{2,6},{3,7},{4,0},{5,1},{6,2},{7,3},{8,12},{9,13},{10,... | collective-permute-start | bytes 98312 | tf_op jit(solution)/shard_map/ppermute | solution.py:516
  215.3 16.0 %all-to-all-start.5 = ((bf16[16,32,256]{2,1,0:T(8,128)(2,1)}), bf16[16,32,256]{2,1,0:T(8,128)(2,1)S(1)}, u32[]{:S(2)}, u32[]{:S(2)}) async-start(bf16[16,32,256]{2,1,0:T(8,128)(2,1)} %broadcast_in_dim.52), calls=%async_computation.5 | async-start | bytes 524288 | tf_op jit(solution)/shard_map/all_to_all | solution.py:418

commit v10 on v9

--- a/solution.py
+++ b/solution.py
@@ -300,8 +300,8 @@
     def _():
         for tile in range(blocks):
             rows = slice(tile * BLOCK, (tile + 1) * BLOCK)
-            tail[rows, :HEAD_DIM] = (dkt[tile] * factor).T.astype(BF16)
-            tail[rows, HEAD_DIM:] = dvt[tile].T.astype(BF16)
+            tail[rows, :HEAD_DIM] = (dkt[tile] * factor).astype(BF16).T
+            tail[rows, HEAD_DIM:] = dvt[tile].astype(BF16).T
         last = pltpu.make_async_copy(tail, out_ref.at[:, 2 * PAIR :], sems.at[blocks])
         last.start()
         for block in range(blocks):
@@ -402,6 +402,12 @@
         grad_ref[:, at + kv_width : at + kv_width + HEAD_DIM] = values.astype(BF16)
 
 
+def repeat_kernel(total_ref, came_ref, out_ref):
+    total = (total_ref[...] + came_ref[...]).astype(BF16)
+    for piece in range(out_ref.shape[0]):
+        out_ref[piece] = total
+
+
 def unfold_kernel(whole_ref, first_ref, second_ref):
     rank = first_ref.shape[0]
     for piece in range(whole_ref.shape[0]):
@@ -511,10 +517,17 @@
         ),
     )(came, cosine, sine)
     total = jnp.sum(exchange(terms, "sub").astype(F32), axis=0)
+    came_total = jnp.zeros_like(total)
     for axis, apart in (("half", 1), ("dp", 1), ("dp", 2), ("dp", 4)):
+        total = total + came_total
         size = lax.axis_size(axis)
-        total = total + lax.ppermute(total, axis, [(i, i ^ apart) for i in range(size)])
-    whole = exchange(jnp.broadcast_to(total.astype(BF16)[None], terms.shape), "sub")
+        came_total = lax.ppermute(total, axis, [(i, i ^ apart) for i in range(size)])
+    copies = pl.pallas_call(
+        repeat_kernel,
+        out_shape=jax.ShapeDtypeStruct(terms.shape, BF16),
+        compiler_params=params,
+    )(total, came_total)
+    whole = exchange(copies, "sub")
     grad_a, grad_b = pl.pallas_call(
         unfold_kernel,
         out_shape=(

time: 233 us -> 232 us (level)
  no operation moved by 1% of the time
where the time goes in v10:
time: 232 us
  waiting for transfers between devices  74.2 us (32%)
  blocking collectives  69.7 us (30%)
  starting transfers between devices  56.5 us (24%)
  Pallas kernels  24.3 us (10%)
  local copies, waits for them, and re-layouts  3.34 us (1%)
  other arithmetic  2.67 us (1%)
    all_to_all x2, blocking collectives, exchange(): return lax.all_to_all(table, axis, split_axis=0, concat_axis=0, tiled=True)  69.7 us
    all_to_all x4, waiting for transfers between devices, exchange(): return lax.all_to_all(table, axis, split_axis=0, concat_axis=0, tiled=True)  67.7 us
    all_to_all x4, starting transfers between devices, exchange(): return lax.all_to_all(table, axis, split_axis=0, concat_axis=0, tiled=True)  39.7 us
    ppermute x4, starting transfers between devices, local(): lax.ppermute(total, axis, [(i, i ^ apart) for i in range(size)])  15.4 us
    pallas_call x1, Pallas kernels, attention(): pl.pallas_call(attention_kernel, out_shape=pltpu.HBM((rows, width), BF16)...  14.9 us
    ppermute x4, waiting for transfers between devices, local(): lax.ppermute(total, axis, [(i, i ^ apart) for i in range(size)])  5.69 us
  transfers between devices with their start and end apart: 9, of which 8 were waited for; matrix products, arithmetic and copies ran while one was open for 1% of the time, Pallas kernels for 7%

profile of v10, /device:TPU:1, one launch (start us, length us, event | category | flops | bytes accessed | tf_op | source)
XLA Modules:
  0.0 232.1 jit_solution(7142645608497231097)
XLA Ops:
  0.6 3.1 %shard_map.102 = bf16[128,6272]{1,0:T(8,128)(2,1)} custom-call(bf16[128,4096]{1,0:T(8,128)(2,1)} %bitcast.6.inputs_ref, bf16[16,4096]{1,0:T(8,128)(2,1)} %bitcast.42, bf16[128,6144]{1,0:T(8,128)(2,1)} %bitcast.41), custom_call_target="tpu_custom_call" | custom-call | tf_op jit(solution)/shard_map/pallas_call | solution.py:443
  3.7 0.0 copy-start.5
  3.7 0.0 copy-start.4
  3.7 0.0 copy-start.1
  3.7 0.0 copy-start.2
  3.7 11.8 %all-to-all-start = ((bf16[8,16,6272]{2,1,0:T(8,128)(2,1)}), bf16[8,16,6272]{2,1,0:T(8,128)(2,1)S(1)}, u32[]{:S(2)}, u32[]{:S(2)}) async-start(bf16[8,16,6272]{2,1,0:T(8,128)(2,1)} %bitcast.35), calls=%async_computation | async-start | bytes 3211264 | tf_op jit(solution)/shard_map/all_to_all | solution.py:424
  15.5 0.0 copy-done.5
  15.5 0.2 reduce-window.4
  15.7 0.0 copy-done.4
  15.7 0.6 select_reduce_fusion.2
  17.0 0.7 fusion.valid_ref
  17.7 0.3 fusion.1
  18.0 0.1 pad_maximum_fusion
  18.1 23.0 %all-to-all-done = bf16[8,16,6272]{2,1,0:T(8,128)(2,1)S(1)} async-done(((bf16[8,16,6272]{2,1,0:T(8,128)(2,1)}), bf16[8,16,6272]{2,1,0:T(8,128)(2,1)S(1)}, u32[]{:S(2)}, u32[]{:S(2)}) %all-to-all-start) | async-done | bytes 1605664 | tf_op jit(solution)/shard_map/all_to_all | solution.py:424
  41.2 0.0 copy-start
  41.2 0.0 copy-done.1
  41.2 0.0 copy-done.2
  41.2 1.0 shard_map.103
  42.1 0.2 copy-done
  42.3 52.6 %all_to_all.42 = bf16[16,128,640]{2,1,0:T(8,128)(2,1)S(1)} all-to-all(bf16[16,128,640]{2,1,0:T(8,128)(2,1)S(1)} %shard_map.103), channel_id=1, replica_groups=mesh['half'=2,'sub'=16,'dp'=8] {'sub'}, dimensions={0} | all-to-all | bytes 5242880 | tf_op jit(solution)/shard_map/all_to_all | solution.py:424
  95.0 0.0 copy-start.3
  95.0 1.5 copy-done.3
  96.5 4.3 %all-to-all-start.3 = ((bf16[8,16,4096]{2,1,0:T(8,128)(2,1)}), bf16[8,16,4096]{2,1,0:T(8,128)(2,1)}, u32[]{:S(2)}, u32[]{:S(2)}) async-start(bf16[8,16,4096]{2,1,0:T(8,128)(2,1)} %bitcast.16), calls=%async_computation.3 | async-start | bytes 2097152 | tf_op jit(solution)/shard_map/all_to_all | solution.py:424
  100.8 1.4 collective-permute-start
  102.2 0.2 select_reduce_fusion
  102.4 0.5 fusion.3
  103.0 0.8 collective-permute-done.other_ref
  103.8 0.8 copy-done.6
  104.6 14.9 %shard_map.104 = bf16[2048,768]{1,0:T(8,128)(2,1)} custom-call(s32[8]{0:T(128)} %get-tuple-element.21.start_ref, s32[8]{0:T(128)} %get-tuple-element.20.end_ref, s32[1]{0:T(128)S(6)} %select_n.25.side_ref, bf16[2048,640]{1,0:T(8,128)(2,1)} %bitcast.37, bf16[2048,640]{1,0:T(8,128)(2,1)} %bitcast.38, bf16[2048,640]{1,0:T(8,128)(2,1)} %bitcast.39, ...), custom_call_target="tpu_custom_call" | custom-call | flops 8053063680 | bytes 6291456 | tf_op jit(solution)/shard_map/pallas_call | solution.py:316
  119.5 0.0 all-to-all-done.3
  119.5 14.9 %all-to-all-start.2 = ((bf16[16,128,768]{2,1,0:T(8,128)(2,1)}), bf16[16,128,768]{2,1,0:T(8,128)(2,1)S(1)}, u32[]{:S(2)}, u32[]{:S(2)}) async-start(bf16[16,128,768]{2,1,0:T(8,128)(2,1)} %bitcast.40), calls=%async_computation.2 | async-start | bytes 6291456 | tf_op jit(solution)/shard_map/all_to_all | solution.py:424
  134.3 0.8 slice.9.low_ref
  135.1 39.6 %all-to-all-done.2.came_ref = bf16[16,128,768]{2,1,0:T(8,128)(2,1)S(1)} async-done(((bf16[16,128,768]{2,1,0:T(8,128)(2,1)}), bf16[16,128,768]{2,1,0:T(8,128)(2,1)S(1)}, u32[]{:S(2)}, u32[]{:S(2)}) %all-to-all-start.2) | async-done | bytes 3145760 | tf_op jit(solution)/shard_map/all_to_all | solution.py:424
  174.7 1.6 shard_map.106
  176.3 17.1 %all_to_all.43 = bf16[16,32,256]{2,1,0:T(8,128)(2,1)S(1)} all-to-all(bf16[16,32,256]{2,1,0:T(8,128)(2,1)S(1)} %shard_map.106), channel_id=1, replica_groups=mesh['half'=2,'sub'=16,'dp'=8] {'sub'}, dimensions={0} | all-to-all | bytes 524288 | tf_op jit(solution)/shard_map/all_to_all | solution.py:424
  193.4 4.2 %collective-permute-start.1 = (f32[32,256]{1,0:T(8,128)S(1)}, f32[32,256]{1,0:T(8,128)S(1)}, u32[]{:S(2)}, u32[]{:S(2)}) collective-permute-start(f32[32,256]{1,0:T(8,128)S(1)} %convert_reduce_fusion), channel_id=1, source_target_pairs={{0,128},{128,0},{1,129},{129,1},{2,130},{130,2},{3,131},{131,3},{4... | collective-permute-start | bytes 98312 | tf_op jit(solution)/shard_map/ppermute | solution.py:524
  197.6 1.3 collective-permute-done.1
  198.9 1.7 collective-permute-start.2
  200.6 1.3 collective-permute-done.2
  201.9 4.4 %collective-permute-start.3 = (f32[32,256]{1,0:T(8,128)S(1)}, f32[32,256]{1,0:T(8,128)S(1)}, u32[]{:S(2)}, u32[]{:S(2)}) collective-permute-start(f32[32,256]{1,0:T(8,128)S(1)} %add.63), channel_id=1, source_target_pairs={{0,2},{1,3},{2,0},{3,1},{4,6},{5,7},{6,4},{7,5},{8,10},{9,11},{10,... | collective-permute-start | bytes 98312 | tf_op jit(solution)/shard_map/ppermute | solution.py:524
  206.3 1.5 collective-permute-done.3
  207.9 5.1 %collective-permute-start.4 = (f32[32,256]{1,0:T(8,128)S(1)}, f32[32,256]{1,0:T(8,128)S(1)}, u32[]{:S(2)}, u32[]{:S(2)}) collective-permute-start(f32[32,256]{1,0:T(8,128)S(1)} %add.64.total_ref), channel_id=1, source_target_pairs={{0,4},{1,5},{2,6},{3,7},{4,0},{5,1},{6,2},{7,3},{8,12},{9,13},{10,... | collective-permute-start | bytes 98312 | tf_op jit(solution)/shard_map/ppermute | solution.py:524
  213.0 1.5 collective-permute-done.4.came_ref
  214.5 0.7 shard_map.107
  215.3 8.7 %all-to-all-start.5 = ((bf16[16,32,256]{2,1,0:T(8,128)(2,1)}), bf16[16,32,256]{2,1,0:T(8,128)(2,1)S(1)}, u32[]{:S(2)}, u32[]{:S(2)}) async-start(bf16[16,32,256]{2,1,0:T(8,128)(2,1)} %shard_map.107), calls=%async_computation.5 | async-start | bytes 524288 | tf_op jit(solution)/shard_map/all_to_all | solution.py:424
  224.0 2.2 shard_map.105
  226.2 5.0 %all-to-all-done.5.whole_ref = bf16[16,32,256]{2,1,0:T(8,128)(2,1)S(1)} async-done(((bf16[16,32,256]{2,1,0:T(8,128)(2,1)}), bf16[16,32,256]{2,1,0:T(8,128)(2,1)S(1)}, u32[]{:S(2)}, u32[]{:S(2)}) %all-to-all-start.5) | async-done | bytes 262176 | tf_op jit(solution)/shard_map/all_to_all | solution.py:424
  231.2 0.8 shard_map.108
  (9 shorter events, 0.1 us)
Async XLA Ops:
  3.7 11.8 %copy-start.5 = (s32[1,5]{1,0:T(1,128)S(1)}, s32[1,5]{1,0:T(1,128)}, u32[]{:S(2)}) copy-start(s32[1,5]{1,0:T(1,128)} %param.12) | copy-start | bytes 64
  3.7 12.0 %copy-start.4 = (s32[1,5]{1,0:T(1,128)S(1)}, s32[1,5]{1,0:T(1,128)}, u32[]{:S(2)}) copy-start(s32[1,5]{1,0:T(1,128)} %param.11) | copy-start | bytes 64
  3.7 37.5 %copy-start.1 = (bf16[1,128,4096]{2,1,0:T(8,128)(2,1)S(1)}, bf16[1,128,4096]{2,1,0:T(8,128)(2,1)}, u32[]{:S(2)}) copy-start(bf16[1,128,4096]{2,1,0:T(8,128)(2,1)} %param.13) | copy-start | bytes 3145732
  3.7 37.4 %copy-start.2 = (bf16[16,4096]{1,0:T(8,128)(2,1)S(1)}, bf16[16,4096]{1,0:T(8,128)(2,1)}, u32[]{:S(2)}) copy-start(bf16[16,4096]{1,0:T(8,128)(2,1)} %up_ref.3) | copy-start | bytes 393220
  3.7 37.4 %all-to-all-start = ((bf16[8,16,6272]{2,1,0:T(8,128)(2,1)}), bf16[8,16,6272]{2,1,0:T(8,128)(2,1)S(1)}, u32[]{:S(2)}, u32[]{:S(2)}) async-start(bf16[8,16,6272]{2,1,0:T(8,128)(2,1)} %bitcast.35), calls=%async_computation | async-start | bytes 3211264 | tf_op jit(solution)/shard_map/all_to_all | solution.py:424
  41.2 1.2 copy-start
  95.0 1.5 copy-start.3
  96.5 22.9 %all-to-all-start.3 = ((bf16[8,16,4096]{2,1,0:T(8,128)(2,1)}), bf16[8,16,4096]{2,1,0:T(8,128)(2,1)}, u32[]{:S(2)}, u32[]{:S(2)}) async-start(bf16[8,16,4096]{2,1,0:T(8,128)(2,1)} %bitcast.16), calls=%async_computation.3 | async-start | bytes 2097152 | tf_op jit(solution)/shard_map/all_to_all | solution.py:424
  100.8 3.0 %collective-permute-start = (bf16[2048,128]{1,0:T(8,128)(2,1)S(1)}, bf16[2048,128]{1,0:T(8,128)(2,1)S(1)}, u32[]{:S(2)}, u32[]{:S(2)}) collective-permute-start(bf16[2048,128]{1,0:T(8,128)(2,1)S(1)} %slice.8), channel_id=1, source_target_pairs={{0,8},{8,0},{16,24},{24,16},{32,40},{40,32},{48,56},{56,48},{64,72... | collective-permute-start | bytes 1572872 | tf_op jit(solution)/shard_map/ppermute | solution.py:492
  103.8 0.8 copy-start.6
  119.5 55.2 %all-to-all-start.2 = ((bf16[16,128,768]{2,1,0:T(8,128)(2,1)}), bf16[16,128,768]{2,1,0:T(8,128)(2,1)S(1)}, u32[]{:S(2)}, u32[]{:S(2)}) async-start(bf16[16,128,768]{2,1,0:T(8,128)(2,1)} %bitcast.40), calls=%async_computation.2 | async-start | bytes 6291456 | tf_op jit(solution)/shard_map/all_to_all | solution.py:424
  193.4 5.5 %collective-permute-start.1 = (f32[32,256]{1,0:T(8,128)S(1)}, f32[32,256]{1,0:T(8,128)S(1)}, u32[]{:S(2)}, u32[]{:S(2)}) collective-permute-start(f32[32,256]{1,0:T(8,128)S(1)} %convert_reduce_fusion), channel_id=1, source_target_pairs={{0,128},{128,0},{1,129},{129,1},{2,130},{130,2},{3,131},{131,3},{4... | collective-permute-start | bytes 98312 | tf_op jit(solution)/shard_map/ppermute | solution.py:524
  198.9 3.0 %collective-permute-start.2 = (f32[32,256]{1,0:T(8,128)S(1)}, f32[32,256]{1,0:T(8,128)S(1)}, u32[]{:S(2)}, u32[]{:S(2)}) collective-permute-start(f32[32,256]{1,0:T(8,128)S(1)} %add.62), channel_id=1, source_target_pairs={{0,1},{1,0},{2,3},{3,2},{4,5},{5,4},{6,7},{7,6},{8,9},{9,8},{10,11... | collective-permute-start | bytes 98312 | tf_op jit(solution)/shard_map/ppermute | solution.py:524
  201.9 5.9 %collective-permute-start.3 = (f32[32,256]{1,0:T(8,128)S(1)}, f32[32,256]{1,0:T(8,128)S(1)}, u32[]{:S(2)}, u32[]{:S(2)}) collective-permute-start(f32[32,256]{1,0:T(8,128)S(1)} %add.63), channel_id=1, source_target_pairs={{0,2},{1,3},{2,0},{3,1},{4,6},{5,7},{6,4},{7,5},{8,10},{9,11},{10,... | collective-permute-start | bytes 98312 | tf_op jit(solution)/shard_map/ppermute | solution.py:524
  207.9 6.7 %collective-permute-start.4 = (f32[32,256]{1,0:T(8,128)S(1)}, f32[32,256]{1,0:T(8,128)S(1)}, u32[]{:S(2)}, u32[]{:S(2)}) collective-permute-start(f32[32,256]{1,0:T(8,128)S(1)} %add.64.total_ref), channel_id=1, source_target_pairs={{0,4},{1,5},{2,6},{3,7},{4,0},{5,1},{6,2},{7,3},{8,12},{9,13},{10,... | collective-permute-start | bytes 98312 | tf_op jit(solution)/shard_map/ppermute | solution.py:524
  215.3 16.0 %all-to-all-start.5 = ((bf16[16,32,256]{2,1,0:T(8,128)(2,1)}), bf16[16,32,256]{2,1,0:T(8,128)(2,1)S(1)}, u32[]{:S(2)}, u32[]{:S(2)}) async-start(bf16[16,32,256]{2,1,0:T(8,128)(2,1)} %shard_map.107), calls=%async_computation.5 | async-start | bytes 524288 | tf_op jit(solution)/shard_map/all_to_all | solution.py:424
